TPU v7x, 32 devices: a whole 2x2x4 slice. The times are simulated.
32 devices in a mesh: gx: 16 (over z, y, core), gz: 2 (over x).
Axes of the slice: x: 2, y: 2, z: 4, core: 2. Of those that a mesh axis runs over, the one named last changes fastest.
Arguments:
- tokens: bfloat16 [4, 64, 16, 768], P(None, 'gx', 'gz'), may hold values from -60 to 60
- cross_qkv: bfloat16 [768, 2304], P(None, 'gx'), may hold values from -16 to 16
- cross_out: bfloat16 [768, 768], P('gx'), may hold values from -0.21875 to 0.21875
- depth_qkv: bfloat16 [768, 2304], P(None, 'gx'), may hold values from -16 to 16
- depth_out: bfloat16 [768, 768], P('gx'), may hold values from -0.21875 to 0.21875
- up_proj: bfloat16 [768, 3072], P(None, 'gz'), may hold values from -0.21875 to 0.21875
- down_proj: bfloat16 [3072, 768], P('gz'), may hold values from -0.109375 to 0.109375
- gains: float32 [3, 768], replicated, may hold values from 0.5 to 1.5
- head_weight: float32 [768], replicated, may hold values from -0.21875 to 0.21875
- head_bias: float32 [1], replicated, may hold values from -1 to 1
Outputs:
- features: bfloat16 [4, 64, 16, 768], P(None, 'gx', 'gz')
- geotime: float32 [4, 64, 16], P(None, 'gx', 'gz')
All inputs are finite; a program needn't handle non-finite values.
Results may differ from a plain program's by a relative error of at most 0.013.
Values may be sent and summed in bfloat16 or wider, within the bound.
No kernel may reach another device: no remote copies, remote signals or barrier semaphores. Data moves between devices by JAX's collectives and lax.ppermute only.
A program may use at most 64 MiB of HBM per device.

v0:
```python
import math

import jax
import jax.numpy as jnp
from jax import lax
from jax.sharding import PartitionSpec as P

HDIM = 64


log_span = math.log(256.0)


def carried_in(shard, axis, combine, identity):
    peers, position = (lax.axis_size(axis), lax.axis_index(axis))
    everything = lax.all_gather(shard, axis)
    start = jnp.broadcast_to(jnp.asarray(identity, shard.dtype), shard.shape)

    def step(k, before):
        reached = k < position
        new = combine(before, everything[k])
        return jnp.where(reached, new, before)

    return lax.fori_loop(0, peers, step, start)


def encodings(inlines, crosslines, depths, cross_start, depth_start, model_width):
    pairs = model_width // 2
    index = jnp.arange(pairs)
    freq = math.pi * jnp.exp(-log_span * index.astype(jnp.float32) / pairs)
    which = index % 3
    inline_pos = jnp.arange(inlines).astype(jnp.float32)[:, None, None, None]
    cross_pos = (cross_start + jnp.arange(crosslines)).astype(jnp.float32)[None, :, None, None]
    depth_pos = (depth_start + jnp.arange(depths)).astype(jnp.float32)[None, None, :, None]
    zeros = jnp.zeros((inlines, crosslines, depths, pairs), jnp.float32)
    position = jnp.where(
        which == 0, inline_pos + zeros, jnp.where(which == 1, cross_pos + zeros, depth_pos + zeros)
    )
    angle = position * freq
    return jnp.stack([jnp.sin(angle), jnp.cos(angle)], -1).reshape(
        inlines, crosslines, depths, model_width
    )


def normalize(stream, gain):
    scale = lax.rsqrt(jnp.mean(stream * stream, -1, keepdims=True) + 1e-05)
    return (stream * scale * gain).astype(jnp.bfloat16)


def attend(queries, keys, values):
    scale = queries.shape[-1] ** (-0.5)
    scores = (
        jnp.einsum("...qe,...ke->...qk", queries, keys, preferred_element_type=jnp.float32) * scale
    )
    scores = scores - jnp.max(scores, -1, keepdims=True)
    expo = jnp.exp(scores)
    weights = (expo / jnp.sum(expo, -1, keepdims=True)).astype(jnp.bfloat16)
    mixed = jnp.einsum("...qk,...ke->...qe", weights, values, preferred_element_type=jnp.float32)
    return mixed.astype(jnp.bfloat16)


def attend_items(trio):
    return attend(trio[0], trio[1], trio[2])


def body(
    tokens,
    cross_qkv,
    cross_out,
    depth_qkv,
    depth_out,
    up_proj,
    down_proj,
    gains,
    head_weight,
    head_bias,
):
    inlines, cross_dev, depth_dev, model_width = tokens.shape
    tok_rows = inlines * cross_dev * depth_dev
    head_count = model_width // HDIM
    cross_group = lax.axis_size("gx")
    encoding = encodings(
        inlines,
        cross_dev,
        depth_dev,
        lax.axis_index("gx") * cross_dev,
        lax.axis_index("gz") * depth_dev,
        model_width,
    )
    stream = (tokens.astype(jnp.float32) + encoding).reshape(tok_rows, model_width)
    normed = normalize(stream, gains[0])
    packed = jnp.dot(
        normed,
        lax.all_gather(cross_qkv, "gx", axis=1, tiled=True),
        preferred_element_type=jnp.float32,
    ).astype(jnp.bfloat16)
    packed = packed.reshape(inlines, cross_dev, depth_dev, 3, head_count, HDIM)
    lined = jnp.transpose(packed, (3, 0, 2, 4, 1, 5))
    per_item = inlines * depth_dev * head_count // cross_group
    lined = lined.reshape(3, cross_group, per_item, cross_dev, HDIM)
    mixed = attend_items(
        (
            lax.all_to_all(lined[0], "gx", split_axis=0, concat_axis=2, tiled=True),
            lax.all_to_all(lined[1], "gx", split_axis=0, concat_axis=2, tiled=True),
            lax.all_to_all(lined[2], "gx", split_axis=0, concat_axis=2, tiled=True),
        )
    )
    mixed = lax.all_to_all(mixed, "gx", split_axis=2, concat_axis=0, tiled=True)
    mixed = jnp.transpose(
        mixed.reshape(inlines, depth_dev, head_count, cross_dev, HDIM), (0, 3, 1, 2, 4)
    ).reshape(tok_rows, model_width)
    columns = mixed
    stream = stream + jnp.dot(
        columns,
        lax.all_gather(cross_out, "gx", axis=0, tiled=True),
        preferred_element_type=jnp.float32,
    )
    normed = normalize(stream, gains[1])
    packed = jnp.dot(
        normed,
        lax.all_gather(depth_qkv, "gx", axis=1, tiled=True),
        preferred_element_type=jnp.float32,
    ).astype(jnp.bfloat16)
    packed = packed.reshape(inlines, cross_dev, depth_dev, 3, head_count, HDIM)
    lined = jnp.transpose(packed, (3, 0, 1, 4, 2, 5))
    all_keys, all_values = (
        lax.all_gather(lined[1], "gz", axis=3, tiled=True),
        lax.all_gather(lined[2], "gz", axis=3, tiled=True),
    )
    mixed = attend(lined[0], all_keys, all_values)
    mixed = jnp.transpose(mixed, (0, 1, 3, 2, 4)).reshape(tok_rows, model_width)
    columns = mixed
    stream = stream + jnp.dot(
        columns,
        lax.all_gather(depth_out, "gx", axis=0, tiled=True),
        preferred_element_type=jnp.float32,
    )
    normed = normalize(stream, gains[2])
    hidden = jax.nn.gelu(
        jnp.dot(
            lax.all_gather(normed, "gz", axis=0, tiled=True),
            up_proj,
            preferred_element_type=jnp.float32,
        )
    ).astype(jnp.bfloat16)
    stream = stream + lax.psum_scatter(
        jnp.dot(hidden, down_proj, preferred_element_type=jnp.float32).astype(jnp.bfloat16),
        "gz",
        scatter_dimension=0,
        tiled=True,
    ).astype(jnp.float32)
    features = stream.astype(jnp.bfloat16).reshape(inlines, cross_dev, depth_dev, model_width)
    thickness = jax.nn.softplus(
        jnp.dot(stream, head_weight, precision=lax.Precision.HIGHEST) + head_bias[0]
    )
    local_time = jnp.cumsum(thickness.reshape(inlines, cross_dev, depth_dev), axis=2)
    line_total = local_time[:, :, -1]
    carried = carried_in(
        line_total, "gz", lambda earlier, later: earlier + later, jnp.zeros_like(line_total)
    )
    geotime = local_time + carried[:, :, None]
    return (features, geotime)


def solution(mesh):
    return jax.shard_map(
        body,
        mesh=mesh,
        in_specs=(
            P(None, "gx", "gz", None),
            P(None, "gx"),
            P("gx", None),
            P(None, "gx"),
            P("gx", None),
            P(None, "gz"),
            P("gz", None),
            P(),
            P(),
            P(),
        ),
        out_specs=(P(None, "gx", "gz", None), P(None, "gx", "gz")),
        check_vma=False,
    )
```

profile of v0, /device:TPU:0, one launch (start us, length us, event | category | flops | bytes accessed | tf_op | source)
XLA Modules:
  0.0 231.5 jit_solution(11413163250456662044)
XLA Ops:
  7.2 0.7 all-gather.8.cloned.1.call-update
  8.0 0.7 all-gather.10.cloned.1.call-update
  8.7 0.7 all-gather.12.cloned.1.call-update
  9.5 0.8 fusion.32
  10.3 6.3 %copy.49 = f32[4,4,8,384,2]{2,4,3,1,0:T(2,128)} copy(f32[4,4,8,384,2]{3,2,4,1,0:T(8,128)S(1)} %pad_maximum_fusion) | data formatting | bytes 786432 | tf_op jit(solution)/shard_map/stack | solution.py:40
  16.6 4.4 %copy.50 = f32[4,4,8,768]{3,2,1,0:T(8,128)S(1)} copy(f32[4,4,8,768]{2,3,1,0:T(8,128)} %bitcast.82) | data formatting | bytes 786432 | tf_op jit(solution)/shard_map/reshape | solution.py:40
  21.0 0.1 multiply_reduce_fusion.2
  21.5 38.8 %all-gather.8.cloned.1.call-done = bf16[768,2304]{0,1:T(8,128)(2,1)} async-done(((bf16[768,144]{0,1:T(8,128)(2,1)}), bf16[768,2304]{0,1:T(8,128)(2,1)}) %all-gather.8.cloned.1.call-update) | async-done | bytes 3538960 | tf_op jit(solution)/shard_map/all_gather | solution.py:94
  60.2 3.3 %convolution_convert_fusion.1 = bf16[128,2304]{1,0:T(8,128)(2,1)S(1)} fusion(bf16[128,768]{1,0:T(8,128)(2,1)S(1)} %fusion.25, bf16[768,2304]{0,1:T(8,128)(2,1)} %all-gather.8.cloned.1.call-done), kind=kOutput, calls=%fused_computation.4 | convolution fusion | flops 453279744 | bytes 4325376 | tf_op jit(solution)/shard_map/dot_general | solution.py:92
  63.5 1.9 reshape.145
  65.4 2.5 %fusion.44 = (bf16[1,4,8,12,4,64]{5,3,0,2,4,1:T(8,128)(2,1)S(1)}, bf16[1,4,8,12,4,64]{5,3,0,2,4,1:T(8,128)(2,1)S(1)}, bf16[1,4,8,12,4,64]{5,3,0,2,4,1:T(8,128)(2,1)}) fusion(bf16[3,4,8,12,4,64]{5,3,0,2,4,1:T(8,128)(2,1)} %bitcast.83), kind=kLoop, calls=%fused_computation.83 | loop fusion | bytes 1179648 | tf_op jit(solution)/shard_map/slice | solution.py:104
  68.0 1.1 copy.53
  69.0 1.9 reshape.167
  71.0 3.7 %all-to-all-start.1 = ((bf16[16,2,3072]{2,1,0:T(2,128)(2,1)}), bf16[16,2,3072]{2,1,0:T(2,128)(2,1)S(1)}, u32[]{:S(2)}, u32[]{:S(2)}) async-start(bf16[16,2,3072]{2,1,0:T(2,128)(2,1)} %reshape.167), calls=%async_computation.1 | async-start | bytes 393216 | tf_op jit(solution)/shard_map/all_to_all | solution.py:104
  74.7 2.1 copy.51
  76.8 1.9 reshape.165
  78.7 5.3 %all-to-all-done.1 = bf16[16,2,3072]{2,1,0:T(2,128)(2,1)S(1)} async-done(((bf16[16,2,3072]{2,1,0:T(2,128)(2,1)}), bf16[16,2,3072]{2,1,0:T(2,128)(2,1)S(1)}, u32[]{:S(2)}, u32[]{:S(2)}) %all-to-all-start.1) | async-done | bytes 196640 | tf_op jit(solution)/shard_map/all_to_all | solution.py:104
  84.0 4.2 %all-to-all-start = ((bf16[16,2,3072]{2,1,0:T(2,128)(2,1)}), bf16[16,2,3072]{2,1,0:T(2,128)(2,1)}, u32[]{:S(2)}, u32[]{:S(2)}) async-start(bf16[16,2,3072]{2,1,0:T(2,128)(2,1)} %reshape.165), calls=%async_computation | async-start | bytes 393216 | tf_op jit(solution)/shard_map/all_to_all | solution.py:103
  88.2 1.1 copy.55
  89.3 1.9 reshape.163
  91.2 7.8 %all-to-all-done = bf16[16,2,3072]{2,1,0:T(2,128)(2,1)} async-done(((bf16[16,2,3072]{2,1,0:T(2,128)(2,1)}), bf16[16,2,3072]{2,1,0:T(2,128)(2,1)}, u32[]{:S(2)}, u32[]{:S(2)}) %all-to-all-start) | async-done | bytes 196640 | tf_op jit(solution)/shard_map/all_to_all | solution.py:103
  99.0 4.2 %all-to-all-start.2 = ((bf16[16,2,3072]{2,1,0:T(2,128)(2,1)}), bf16[16,2,3072]{2,1,0:T(2,128)(2,1)}, u32[]{:S(2)}, u32[]{:S(2)}) async-start(bf16[16,2,3072]{2,1,0:T(2,128)(2,1)} %reshape.163), calls=%async_computation.2 | async-start | bytes 393216 | tf_op jit(solution)/shard_map/all_to_all | solution.py:105
  103.1 0.3 reshape.168
  103.4 0.2 copy.54
  103.6 1.2 reshape.166
  104.9 1.0 copy.52
  105.8 6.3 %all-to-all-done.2 = bf16[16,2,3072]{2,1,0:T(2,128)(2,1)} async-done(((bf16[16,2,3072]{2,1,0:T(2,128)(2,1)}), bf16[16,2,3072]{2,1,0:T(2,128)(2,1)}, u32[]{:S(2)}, u32[]{:S(2)}) %all-to-all-start.2) | async-done | bytes 196640 | tf_op jit(solution)/shard_map/all_to_all | solution.py:105
  112.2 1.2 reshape.164
  113.4 1.0 copy.56
  114.4 2.1 fusion.46
  116.4 1.2 convolution_multiply_fusion
  117.6 1.9 fusion.14
  119.6 0.3 copy.71
  119.9 0.9 reshape.169
  120.8 3.5 %all-to-all-start.3 = ((bf16[16,2,3072]{2,1,0:T(2,128)(2,1)}), bf16[16,2,3072]{2,1,0:T(2,128)(2,1)S(1)}, u32[]{:S(2)}, u32[]{:S(2)}) async-start(bf16[16,2,3072]{2,1,0:T(2,128)(2,1)} %reshape.169), calls=%async_computation.3 | async-start | bytes 393216 | tf_op jit(solution)/shard_map/all_to_all | solution.py:108
  124.3 0.5 all-gather.14.cloned.1.call-update
  124.9 8.3 %all-to-all-done.3 = bf16[16,2,3072]{2,1,0:T(2,128)(2,1)S(1)} async-done(((bf16[16,2,3072]{2,1,0:T(2,128)(2,1)}), bf16[16,2,3072]{2,1,0:T(2,128)(2,1)S(1)}, u32[]{:S(2)}, u32[]{:S(2)}) %all-to-all-start.3) | async-done | bytes 196640 | tf_op jit(solution)/shard_map/all_to_all | solution.py:108
  133.3 0.3 reshape.170
  133.6 0.2 copy.59
  133.8 0.3 reshape.150
  134.2 1.7 multiply_reduce_fusion.1
  135.9 14.6 %all-gather.12.cloned.1.call-done = bf16[768,2304]{0,1:T(8,128)(2,1)} async-done(((bf16[768,144]{0,1:T(8,128)(2,1)}), bf16[768,2304]{0,1:T(8,128)(2,1)}) %all-gather.12.cloned.1.call-update) | async-done | bytes 3538960 | tf_op jit(solution)/shard_map/all_gather | solution.py:121
  150.5 4.1 %convolution_convert_fusion = bf16[128,2304]{1,0:T(8,128)(2,1)} fusion(bf16[768,2304]{0,1:T(8,128)(2,1)} %all-gather.12.cloned.1.call-done, f32[128,768]{1,0:T(8,128)S(1)} %get-tuple-element.134, f32[768]{0:T(1024)S(1)} %get-tuple-element.115, f32[128]{0:T(128)S(1)} %add_rsqrt_fusion.2), kind=kOutput, calls=%fused_computation.3 | convolution fusion | flops 453574656 | bytes 4525568 | tf_op jit(solution)/shard_map/dot_general | solution.py:119
  154.6 2.8 %reshape.151 = bf16[4,4,8,3,12,64]{5,4,3,2,1,0:T(8,128)(2,1)} reshape(bf16[128,2304]{1,0:T(8,128)(2,1)} %convolution_convert_fusion) | data formatting | bytes 1179648 | tf_op jit(solution)/shard_map/reshape | solution.py:124
  157.4 1.7 copy.70
  159.2 11.9 %all-gather = bf16[1,4,4,12,16,64]{5,4,3,2,1,0:T(8,128)(2,1)S(1)} all-gather(bf16[1,4,4,12,8,64]{5,4,3,2,1,0:T(8,128)(2,1)S(1)} %get-tuple-element.129), channel_id=2, replica_groups=mesh['gx'=16,'gz'=2] {'gz'}, dimensions={4}, use_global_device_ids=true | all-gather | bytes 589824 | tf_op jit(solution)/shard_map/all_gather | solution.py:127
  171.1 11.3 %all-gather.1 = bf16[1,4,4,12,16,64]{5,4,3,2,1,0:T(8,128)(2,1)} all-gather(bf16[1,4,4,12,8,64]{5,4,3,2,1,0:T(8,128)(2,1)S(1)} %get-tuple-element.130), channel_id=3, replica_groups=mesh['gx'=16,'gz'=2] {'gz'}, dimensions={4}, use_global_device_ids=true | all-gather | bytes 589824 | tf_op jit(solution)/shard_map/all_gather | solution.py:128
  182.4 0.5 convolution_multiply_fusion.1
  182.9 0.9 copy-done.1
  183.8 0.5 fusion.47
  184.4 4.4 %fusion.15 = bf16[4,4,8,12,64]{4,2,3,1,0:T(8,128)(2,1)S(1)} fusion(bf16[1,4,4,12,16,64]{5,4,3,2,1,0:T(8,128)(2,1)} %all-gather.1, f32[4,4,12,8]{3,2,1,0:T(8,128)S(1)} %fusion.47, f32[4,4,12,8,16]{4,3,2,1,0:T(8,128)} %copy-done.1), kind=kOutput, calls=%fused_computation.24 | convolution fusion | flops 3319311 | bytes 694272 | tf_op jit(solution)/shard_map/...qk,...ke->...qe/dot_general | solution.py:58
  188.8 0.9 copy.62
  189.7 1.4 reshape.152
  191.1 1.7 multiply_reduce_fusion
  192.8 0.1 multiply_convert_fusion
  192.9 6.8 %all_gather.30 = bf16[256,768]{1,0:T(8,128)(2,1)S(1)} all-gather(bf16[128,768]{1,0:T(8,128)(2,1)S(1)} %multiply_convert_fusion), channel_id=1, replica_groups=mesh['gx'=16,'gz'=2] {'gz'}, dimensions={0}, use_global_device_ids=true | all-gather | bytes 589824 | tf_op jit(solution)/shard_map/all_gather | solution.py:141
  199.7 4.0 %convolution_convert_fusion.2 = bf16[256,768]{1,0:T(8,128)(2,1)} fusion(bf16[1536,768]{1,0:T(8,128)(2,1)S(1)} %copy-done, bf16[256,768]{1,0:T(8,128)(2,1)S(1)} %all_gather.30, bf16[768,1536]{1,0:T(8,128)(2,1)} %param.17), kind=kOutput, calls=%fused_computation.20 | convolution fusion | flops 1211695104 | bytes 5505024 | tf_op jit(solution)/shard_map/dot_general | solution.py:147
  204.4 11.5 %reduce-scatter.2.cloned.1.call-done = bf16[128,768]{1,0:T(8,128)(2,1)} async-done(((bf16[256,768]{1,0:T(8,128)(2,1)}), bf16[128,768]{1,0:T(8,128)(2,1)}) %reduce-scatter.2.cloned.1.call-update) | async-done | bytes 196624 | tf_op jit(solution)/shard_map/reduce_scatter | solution.py:146
  215.9 1.4 compare_select_fusion
  217.3 0.7 reduce_window_sum.11
  218.1 0.1 copy.63
  218.3 4.3 %all-gather.2 = f32[8,4,1]{1,2,0:T(1,128)S(1)} all-gather(f32[4,4,1]{1,2,0:T(1,128)S(1)} %copy.63), channel_id=4, replica_groups=mesh['gx'=16,'gz'=2] {'gz'}, dimensions={0}, use_global_device_ids=true | all-gather | bytes 192 | tf_op jit(solution)/shard_map/all_gather | solution.py:16
  222.6 0.7 broadcast_add_fusion
  223.3 1.6 fusion.28
  (39 shorter events, 1.0 us)
Async XLA Ops:
  7.2 192.5 %copy-start = (bf16[1536,768]{1,0:T(8,128)(2,1)S(1)}, bf16[1536,768]{1,0:T(8,128)(2,1)}, u32[]{:S(2)}) copy-start(bf16[1536,768]{1,0:T(8,128)(2,1)} %param.18) | copy-start | bytes 7077892
  7.2 53.0 %all-gather.8.cloned.1.call-start = ((), (), s32[]{:S(2)}) async-start(), calls=%async_computation.5 | async-start | bytes 3760128 | tf_op jit(solution)/shard_map/all_gather | solution.py:94
  7.9 126.2 %all-gather.10.cloned.1.call-start = ((), (), s32[]{:S(2)}) async-start(), calls=%async_computation.6 | async-start | bytes 1253376 | tf_op jit(solution)/shard_map/all_gather | solution.py:115
  8.7 141.8 %all-gather.12.cloned.1.call-start = ((), (), s32[]{:S(2)}) async-start(), calls=%async_computation.7 | async-start | bytes 3760128 | tf_op jit(solution)/shard_map/all_gather | solution.py:121
  16.6 4.4 %copy-start.3 = (bf16[4,4,8,768]{3,2,1,0:T(8,128)(2,1)S(1)}, bf16[4,4,8,768]{3,2,1,0:T(8,128)(2,1)}, u32[]{:S(2)}) copy-start(bf16[4,4,8,768]{3,2,1,0:T(8,128)(2,1)} %param.12) | copy-start | bytes 589828
  16.6 4.7 %copy-start.4 = (f32[3,768]{1,0:T(4,128)S(1)}, f32[3,768]{1,0:T(4,128)}, u32[]{:S(2)}) copy-start(f32[3,768]{1,0:T(4,128)} %param.19) | copy-start | bytes 27652
  71.0 13.0 %all-to-all-start.1 = ((bf16[16,2,3072]{2,1,0:T(2,128)(2,1)}), bf16[16,2,3072]{2,1,0:T(2,128)(2,1)S(1)}, u32[]{:S(2)}, u32[]{:S(2)}) async-start(bf16[16,2,3072]{2,1,0:T(2,128)(2,1)} %reshape.167), calls=%async_computation.1 | async-start | bytes 393216 | tf_op jit(solution)/shard_map/all_to_all | solution.py:104
  84.0 15.0 %all-to-all-start = ((bf16[16,2,3072]{2,1,0:T(2,128)(2,1)}), bf16[16,2,3072]{2,1,0:T(2,128)(2,1)}, u32[]{:S(2)}, u32[]{:S(2)}) async-start(bf16[16,2,3072]{2,1,0:T(2,128)(2,1)} %reshape.165), calls=%async_computation | async-start | bytes 393216 | tf_op jit(solution)/shard_map/all_to_all | solution.py:103
  99.0 13.2 %all-to-all-start.2 = ((bf16[16,2,3072]{2,1,0:T(2,128)(2,1)}), bf16[16,2,3072]{2,1,0:T(2,128)(2,1)}, u32[]{:S(2)}, u32[]{:S(2)}) async-start(bf16[16,2,3072]{2,1,0:T(2,128)(2,1)} %reshape.163), calls=%async_computation.2 | async-start | bytes 393216 | tf_op jit(solution)/shard_map/all_to_all | solution.py:105
  114.4 2.1 copy-start.2
  120.8 12.5 %all-to-all-start.3 = ((bf16[16,2,3072]{2,1,0:T(2,128)(2,1)}), bf16[16,2,3072]{2,1,0:T(2,128)(2,1)S(1)}, u32[]{:S(2)}, u32[]{:S(2)}) async-start(bf16[16,2,3072]{2,1,0:T(2,128)(2,1)} %reshape.169), calls=%async_computation.3 | async-start | bytes 393216 | tf_op jit(solution)/shard_map/all_to_all | solution.py:108
  124.3 66.8 %all-gather.14.cloned.1.call-start = ((), (), s32[]{:S(2)}) async-start(), calls=%async_computation.8 | async-start | bytes 1253376 | tf_op jit(solution)/shard_map/all_gather | solution.py:135
  124.9 91.0 %reduce-scatter.2.cloned.1.call-start = ((), (), s32[]{:S(2)}) async-start(), calls=%async_computation.9 | async-start | bytes 589824 | tf_op jit(solution)/shard_map/reduce_scatter | solution.py:146
  182.9 0.9 copy-start.1
  199.7 4.0 %copy-start.5 = (f32[768]{0:T(1024)S(1)}, f32[768]{0:T(1024)}, u32[]{:S(2)}) copy-start(f32[768]{0:T(1024)} %param.20) | copy-start | bytes 9220
Sparse Core Ops, SparseCore 0:
  10.3 49.8 all-gather.7
  62.5 39.1 all-gather.9
  104.0 46.4 all-gather.11
  152.6 37.4 all-gather.13
  203.8 11.9 reduce-scatter.1
where the time goes:
time: 233 us; the launch traced here: 231 us
  waiting for transfers between devices  95.2 us (41%)
  local copies, waits for them, and re-layouts  40.3 us (17%)
  blocking collectives  34.4 us (15%)
  matrix products  26.3 us (11%)
  starting transfers between devices  15.8 us (7%)
  between operations  14.8 us (6%)
  other arithmetic  4.77 us (2%)
    all_gather x1, waiting for transfers between devices, body(): lax.all_gather(cross_qkv, 'gx', axis=1, tiled=True)  38.8 us
    all_gather x1, waiting for transfers between devices, body(): lax.all_gather(depth_qkv, 'gx', axis=1, tiled=True)  14.6 us
    all_gather x1, blocking collectives, body(): lax.all_gather(lined[1], 'gz', axis=3, tiled=True)  11.9 us
    reduce_scatter x1, waiting for transfers between devices, body(): lax.psum_scatter(jnp.dot(hidden, down_proj, preferred_element_type=jnp.fl...  11.5 us
    all_gather x1, blocking collectives, body(): lax.all_gather(lined[2], 'gz', axis=3, tiled=True)  11.3 us
    unnamed x21, local copies, waits for them, and re-layouts  10.6 us
    all_to_all x1, waiting for transfers between devices, body(): mixed = lax.all_to_all(mixed, 'gx', split_axis=2, concat_axis=0, tiled=True)  8.34 us
    all_to_all x1, waiting for transfers between devices, body(): lax.all_to_all(lined[0], 'gx', split_axis=0, concat_axis=2, tiled=True)  7.78 us
  transfers between devices with their start and end apart: 9, of which 7 were waited for; matrix products, arithmetic and copies ran while one was open for 26% of the time, Pallas kernels for 0%

commit v1 on v0

--- a/solution.py
+++ b/solution.py
@@ -2,7 +2,10 @@
 
 import jax
 import jax.numpy as jnp
+import numpy as np
 from jax import lax
+from jax.experimental import pallas as pl
+from jax.experimental.pallas import tpu as pltpu
 from jax.sharding import PartitionSpec as P
 
 HDIM = 64
@@ -63,7 +66,7 @@
     return attend(trio[0], trio[1], trio[2])
 
 
-def body(
+def general_body(
     tokens,
     cross_qkv,
     cross_out,
@@ -162,7 +165,369 @@
     return (features, geotime)
 
 
+F32 = jnp.float32
+BF16 = jnp.bfloat16
+VMEM = pl.BlockSpec(memory_space=pltpu.VMEM)
+SMEM = pl.BlockSpec(memory_space=pltpu.SMEM)
+ANY = pl.BlockSpec(memory_space=pl.ANY)
+NT = (((1,), (1,)), ((), ()))
+NEG = -1e30
+
+
+def call(kernel, outs, in_specs, scratch=(), flops=0, nbytes=0, vmem=40):
+    return pl.pallas_call(
+        kernel,
+        out_shape=outs,
+        in_specs=in_specs,
+        out_specs=jax.tree.map(lambda _: VMEM, outs),
+        scratch_shapes=list(scratch),
+        compiler_params=pltpu.CompilerParams(vmem_limit_bytes=vmem * 2**20),
+        cost_estimate=pl.CostEstimate(flops=flops, bytes_accessed=nbytes, transcendentals=0),
+    )
+
+
+class Plan:
+    def __init__(self, inlines, cross_dev, depth_dev, peers):
+        self.rows = rows = inlines * cross_dev * depth_dev
+        self.lines = inlines * depth_dev // peers
+        index = np.arange(rows)
+        line = index // (cross_dev * self.lines) * self.lines + index % self.lines
+        self.cross = index // self.lines % cross_dev
+        self.inline, self.depth = line // depth_dev, line % depth_dev
+        natural = (self.inline * cross_dev + self.cross) * depth_dev + self.depth
+        self.to_rows = (natural[:, None] == index[None, :]).astype(np.float32)
+        self.natural = natural
+        column = self.inline * cross_dev + self.cross
+        self.same_column = column[:, None] == column[None, :]
+        nat_column, nat_depth = index // depth_dev, index % depth_dev
+        below = self.depth[:, None] <= nat_depth[None, :]
+        on_column = column[:, None] == nat_column[None, :]
+        self.cumulative = (on_column & below).astype(np.float32)
+        self.carried = on_column.astype(np.float32)
+        self.same_line = index[:, None] % self.lines == index[None, :] % self.lines
+
+
+def rms(stream, gain):
+    scale = lax.rsqrt(jnp.mean(stream * stream, -1, keepdims=True) + 1e-05)
+    return (stream * scale * gain).astype(BF16)
+
+
+def as_column(row, eye):
+    return jnp.sum(row * eye, axis=1, keepdims=True)
+
+
+def as_row(column, eye):
+    return jnp.sum(column * eye, axis=0, keepdims=True)
+
+
+def softplus(value):
+    return jnp.maximum(value, 0.0) + jnp.log1p(jnp.exp(-jnp.abs(value)))
+
+
+def encode_kernel(tokens_ref, encoding_ref, to_rows_ref, gain_ref, stream_ref, normed_ref):
+    rows = jnp.dot(to_rows_ref[...], tokens_ref[...], preferred_element_type=F32)
+    stream = rows + encoding_ref[...]
+    stream_ref[...] = stream
+    normed_ref[...] = rms(stream, gain_ref[...])
+
+
+def head_pair(queries, keys, values, bias):
+    lane = lax.broadcasted_iota(jnp.int32, queries.shape, 1)
+    outs = []
+    for head in range(2):
+        own = (lane < HDIM) if head == 0 else (lane >= HDIM)
+        masked = jnp.where(own, queries, jnp.zeros_like(queries))
+        scores = lax.dot_general(masked, keys, NT, preferred_element_type=F32)
+        scores = scores * (HDIM**-0.5) + bias
+        scores = scores - jnp.max(scores, -1, keepdims=True)
+        expo = jnp.exp(scores)
+        weights = (expo / jnp.sum(expo, -1, keepdims=True)).astype(BF16)
+        outs.append(jnp.dot(weights, values, preferred_element_type=F32))
+    return jnp.where(lane < HDIM, outs[0], outs[1]).astype(BF16)
+
+
+def pieces(start, size, chunk):
+    out, at = [], start
+    while at < start + size:
+        n = min(chunk - at % chunk, start + size - at)
+        out.append((at // chunk, at % chunk, at - start, n))
+        at += n
+    return out
+
+
+def qkv_copies(weights_ref, held_ref, sems, width, group, chunk, base):
+    copies, at = [], 0
+    for g in range(width // group):
+        of_group = []
+        for kind in range(3):
+            for block, row, to, n in pieces(kind * width + g * group, group, chunk):
+                of_group.append(
+                    pltpu.make_async_copy(
+                        weights_ref.at[block, pl.ds(base + row, n), :],
+                        held_ref.at[g, kind, pl.ds(to, n), :],
+                        sems.at[at],
+                    )
+                )
+                at += 1
+        copies.append(of_group)
+    return copies
+
+
+def qkv_copy_count(width, group, chunk):
+    return sum(
+        len(pieces(kind * width + g * group, group, chunk))
+        for g in range(width // group)
+        for kind in range(3)
+    )
+
+
+def cross_kernel(normed_ref, weights_ref, bias_ref, mixed_ref, held_ref, sems):
+    width, group = normed_ref.shape[1], held_ref.shape[2]
+    copies = qkv_copies(weights_ref, held_ref, sems, width, group, weights_ref.shape[1], 0)
+    for of_group in copies:
+        for copy in of_group:
+            copy.start()
+    bias = bias_ref[...]
+    for g, of_group in enumerate(copies):
+        for copy in of_group:
+            copy.wait()
+        normed = normed_ref[...]
+        q, k, v = (
+            lax.dot_general(normed, held_ref[g, kind], NT, preferred_element_type=F32).astype(BF16)
+            for kind in range(3)
+        )
+        for pair in range(group // 128):
+            at = slice(pair * 128, pair * 128 + 128)
+            mixed_ref[:, g * group + pair * 128 : g * group + pair * 128 + 128] = head_pair(
+                q[:, at], k[:, at], v[:, at], bias
+            )
+
+
+def row_copies(weights_ref, held_ref, sems, base, count):
+    return [
+        pltpu.make_async_copy(
+            weights_ref.at[block, pl.ds(base, count), :],
+            held_ref.at[pl.ds(block * count, count), :],
+            sems.at[block],
+        )
+        for block in range(weights_ref.shape[0])
+    ]
+
+
+def cross_out_kernel(
+    mixed_ref, stream_ref, weights_ref, gain_ref, out_ref, normed_ref, held_ref, sems, *, base, count
+):
+    copies = row_copies(weights_ref, held_ref, sems, base, count)
+    for copy in copies:
+        copy.start()
+    for copy in copies:
+        copy.wait()
+    stream = stream_ref[...] + jnp.dot(mixed_ref[...], held_ref[...], preferred_element_type=F32)
+    out_ref[...] = stream
+    normed_ref[...] = rms(stream, gain_ref[...])
+
+
+def depth_kernel(
+    own_ref,
+    peer_ref,
+    stream_ref,
+    weights_ref,
+    bias_ref,
+    gain_ref,
+    out_ref,
+    normed_ref,
+    held_ref,
+    out_held_ref,
+    sems,
+    out_sems,
+    *,
+    chunk,
+    base,
+    count,
+):
+    width, group = own_ref.shape[1], held_ref.shape[2]
+    copies = qkv_copies(weights_ref, held_ref, sems, width, group, chunk, 0)
+    out_copies = row_copies(weights_ref, out_held_ref, out_sems, base, count)
+    for of_group in copies:
+        for copy in of_group:
+            copy.start()
+    for copy in out_copies:
+        copy.start()
+    bias = bias_ref[...]
+    mixed = []
+    for g, of_group in enumerate(copies):
+        for copy in of_group:
+            copy.wait()
+        own = own_ref[...]
+        both = jnp.concatenate([own, peer_ref[...]], axis=0)
+        q = lax.dot_general(own, held_ref[g, 0], NT, preferred_element_type=F32).astype(BF16)
+        k, v = (
+            lax.dot_general(both, held_ref[g, kind], NT, preferred_element_type=F32).astype(BF16)
+            for kind in (1, 2)
+        )
+        for pair in range(group // 128):
+            at = slice(pair * 128, pair * 128 + 128)
+            mixed.append(head_pair(q[:, at], k[:, at], v[:, at], bias))
+    for copy in out_copies:
+        copy.wait()
+    stream = stream_ref[...] + jnp.dot(
+        jnp.concatenate(mixed, axis=1), out_held_ref[...], preferred_element_type=F32
+    )
+    out_ref[...] = stream
+    normed_ref[...] = rms(stream, gain_ref[...])
+
+
+def mlp_kernel(
+    own_ref, peer_ref, stream_ref, up_ref, down_ref, head_ref, eye_ref,
+    own_part_ref, peer_part_ref, own_head_ref, peer_head_ref,
+):
+    rows = own_ref.shape[0]
+    both = jnp.concatenate([own_ref[...], peer_ref[...]], axis=0)
+    hidden = jnp.dot(both, up_ref[...], preferred_element_type=F32)
+    hidden = jax.nn.gelu(hidden).astype(BF16)
+    part = jnp.dot(hidden, down_ref[...], preferred_element_type=F32).astype(BF16)
+    own_part_ref[...] = part[:rows]
+    peer_part_ref[...] = part[rows:]
+    head, eye = head_ref[...], eye_ref[...]
+    own = jnp.sum((stream_ref[...] + part[:rows].astype(F32)) * head, axis=1, keepdims=True)
+    peer = jnp.sum(part[rows:].astype(F32) * head, axis=1, keepdims=True)
+    own_head_ref[...] = as_row(own, eye)
+    peer_head_ref[...] = as_row(peer, eye)
+
+
+def final_kernel(
+    stream_ref, own_ref, got_ref, own_head_ref, got_head_ref, peer_head_ref,
+    head_ref, bias_ref, later_ref, from_rows_ref, eye_ref, cumulative_ref, carried_ref,
+    features_ref, time_ref,
+):
+    got = got_ref[...].astype(F32)
+    stream = stream_ref[...] + own_ref[...].astype(F32) + got
+    features_ref[...] = jnp.dot(
+        from_rows_ref[...], stream.astype(BF16), preferred_element_type=F32
+    ).astype(BF16)
+    eye = eye_ref[...]
+    bias = bias_ref[0]
+    own = as_column(own_head_ref[...], eye) + jnp.sum(got * head_ref[...], axis=1, keepdims=True)
+    own = softplus(own + bias)
+    before = softplus(as_column(got_head_ref[...] + peer_head_ref[...], eye) + bias) * later_ref[0]
+    time_ref[...] = jnp.sum(
+        own * cumulative_ref[...] + before * carried_ref[...], axis=0, keepdims=True
+    )
+
+
+def fast_body(
+    tokens, cross_qkv, cross_out, depth_qkv, depth_out,
+    up_proj, down_proj, gains, head_weight, head_bias,
+):
+    inlines, cross_dev, depth_dev, width = tokens.shape
+    peers = lax.axis_size("gx")
+    plan = Plan(inlines, cross_dev, depth_dev, peers)
+    rows, group = plan.rows, 256
+    chunk, count = cross_qkv.shape[1], cross_out.shape[0]
+    swap = [(0, 1), (1, 0)]
+    def const(a, dtype=F32):
+        return jnp.asarray(np.asarray(a, np.float32), dtype)
+    eye = const(np.eye(rows))
+
+    cross_w = lax.all_gather(cross_qkv.T, "gx", axis=0)
+    rest = jnp.concatenate([depth_qkv.T, cross_out, depth_out], axis=0)
+    rest_w = lax.all_gather(rest, "gx", axis=0)
+
+    with jax.named_scope("encoding"):
+        pairs = width // 2
+        feature = jnp.arange(width)
+        pair = feature // 2
+        freq = math.pi * jnp.exp(-log_span * pair.astype(F32) / pairs)
+        which = pair % 3
+        at_cross = const(plan.cross) + (lax.axis_index("gx") * cross_dev).astype(F32)
+        at_depth = const(plan.depth) + (lax.axis_index("gz") * depth_dev).astype(F32)
+        position = jnp.where(
+            which == 0,
+            const(plan.inline)[:, None],
+            jnp.where(which == 1, at_cross[:, None], at_depth[:, None]),
+        )
+        angle = position * freq
+        encoding = jnp.where(feature % 2 == 0, jnp.sin(angle), jnp.cos(angle))
+
+    shape = jax.ShapeDtypeStruct
+    wide, narrow = shape((rows, width), F32), shape((rows, width), BF16)
+    row = shape((1, rows), F32)
+    stream, normed = call(encode_kernel, (wide, narrow), [VMEM] * 4)(
+        tokens.reshape(rows, width), encoding, const(plan.to_rows, BF16), gains[0:1]
+    )
+    lined = lax.all_to_all(
+        normed.reshape(peers, rows // peers, width), "gx", split_axis=0, concat_axis=0, tiled=True
+    )
+    n_copies = qkv_copy_count(width, group, chunk)
+    held = pltpu.VMEM((width // group, 3, group, width), BF16)
+    mixed = call(
+        cross_kernel,
+        narrow,
+        [VMEM, ANY, VMEM],
+        [held, pltpu.SemaphoreType.DMA((n_copies,))],
+    )(lined.reshape(rows, width), cross_w, const(np.where(plan.same_line, 0.0, NEG)))
+    mixed = lax.all_to_all(
+        mixed.reshape(peers, rows // peers, width), "gx", split_axis=0, concat_axis=0, tiled=True
+    )
+    out_held = pltpu.VMEM((width, width), BF16)
+
+    def cross_out_step(*refs):
+        cross_out_kernel(*refs, base=chunk, count=count)
+
+    stream, normed = call(
+        cross_out_step,
+        (wide, narrow),
+        [VMEM, VMEM, ANY, VMEM],
+        [out_held, pltpu.SemaphoreType.DMA((peers,))],
+    )(mixed.reshape(rows, width), stream, rest_w, gains[1:2])
+    peer = lax.ppermute(normed, "gz", swap)
+
+    def depth_step(*refs):
+        depth_kernel(*refs, chunk=chunk, base=chunk + count, count=count)
+
+    depth_bias = np.where(plan.same_column, 0.0, NEG)
+    stream, normed = call(
+        depth_step,
+        (wide, narrow),
+        [VMEM, VMEM, VMEM, ANY, VMEM, VMEM],
+        [held, out_held, pltpu.SemaphoreType.DMA((n_copies,)), pltpu.SemaphoreType.DMA((peers,))],
+    )(
+        normed, peer, stream, rest_w,
+        const(np.concatenate([depth_bias, depth_bias], axis=1)), gains[2:3],
+    )
+    peer = lax.ppermute(normed, "gz", swap)
+    head = head_weight.reshape(1, width)
+    own_part, peer_part, own_head, peer_head = call(
+        mlp_kernel, (narrow, narrow, row, row), [VMEM] * 7
+    )(normed, peer, stream, up_proj, down_proj, head, eye)
+    got_part = lax.ppermute(peer_part, "gz", swap)
+    got_head = lax.ppermute(own_head, "gz", swap)
+    later = (lax.axis_index("gz") > 0).astype(F32).reshape(1)
+    features, geotime = call(
+        final_kernel, (narrow, row), [VMEM] * 7 + [SMEM, SMEM] + [VMEM] * 4
+    )(
+        stream, own_part, got_part, own_head, got_head, peer_head,
+        head, head_bias, later, const(plan.to_rows.T, BF16), eye,
+        const(plan.cumulative), const(plan.carried),
+    )
+    return features.reshape(tokens.shape), geotime.reshape(tokens.shape[:3])
+
+
 def solution(mesh):
+    def body(*args):
+        tokens = args[0]
+        inlines, cross_dev, depth_dev, width = tokens.shape
+        peers = mesh.shape["gx"]
+        fits = (
+            mesh.shape["gz"] == 2
+            and inlines * depth_dev % peers == 0
+            and inlines * cross_dev * depth_dev == 128
+            and width % 256 == 0
+            and 3 * width % (16 * peers) == 0
+            and width % (16 * peers) == 0
+        )
+        return (fast_body if fits else general_body)(*args)
+
     return jax.shard_map(
         body,
         mesh=mesh,

time: 233 us -> 175 us (0.75)
  local copies, waits for them, and re-layouts: 40.3 us -> 9.29 us
  Pallas kernels: 0 us -> 27 us
  matrix products: 26.3 us -> 0 us
  waiting for transfers between devices: 95.2 us -> 76.9 us
  starting transfers between devices: 15.8 us -> 5.23 us
    all_to_all x0 -> x2, blocking collectives: none -> 35.8 us  [the longest x1 19.7 us: fast_body(): lax.all_to_all(normed.reshape(peers, rows // peers, width), 'gx', split_a...]
    all_gather x4 -> x0, blocking collectives: 34.4 us -> none  [the longest x1 11.9 us: body(): lax.all_gather(lined[1], 'gz', axis=3, tiled=True)]
    all_to_all x4 -> x0, waiting for transfers between devices: 27.7 us -> none  [the longest x1 8.34 us: body(): mixed = lax.all_to_all(mixed, 'gx', split_axis=2, concat_axis=0, tiled=True)]
    pallas_call x0 -> x6, Pallas kernels: none -> 27 us  [the longest x1 11.9 us: fast_body(): call(depth_step, (wide, narrow), [VMEM, VMEM, VMEM, ANY, VMEM, VMEM], [he...]
    dot_general x10 -> x0, matrix products: 24.2 us -> none  [the longest x2 6.33 us: attend(): jnp.einsum('...qk,...ke->...qe', weights, values, preferred_element_type=...]
    all_to_all x4 -> x0, starting transfers between devices: 15.6 us -> none  [the longest x1 4.17 us: body(): lax.all_to_all(lined[2], 'gx', split_axis=0, concat_axis=2, tiled=True)]
    ppermute x0 -> x4, waiting for transfers between devices: none -> 13.4 us  [the longest x2 10.4 us: fast_body(): peer = lax.ppermute(normed, 'gz', swap)]
    reshape x7 -> x2, local copies, waits for them, and re-layouts: 12.6 us -> 0.7 us  [the longest x1 0.7 us: fast_body(): return (features.reshape(tokens.shape), geotime.reshape(tokens.shape[:3]))]
  transfers between devices with their start and end apart: 9 -> 6, of which waited for: 7 -> 5; matrix products, arithmetic and copies ran while one was open for 26% -> 3% of each run, Pallas kernels for 0% -> 6%
where the time goes in v1:
time: 175 us; the launch traced here: 174 us
  waiting for transfers between devices  76.9 us (44%)
  blocking collectives  35.8 us (20%)
  Pallas kernels  27 us (15%)
  between operations  14.9 us (9%)
  local copies, waits for them, and re-layouts  9.29 us (5%)
  other arithmetic  5.33 us (3%)
  starting transfers between devices  5.23 us (3%)
    all_gather x1, waiting for transfers between devices, fast_body(): rest_w = lax.all_gather(rest, 'gx', axis=0)  35.9 us
    all_gather x1, waiting for transfers between devices, fast_body(): cross_w = lax.all_gather(cross_qkv.T, 'gx', axis=0)  26.9 us
    all_to_all x1, blocking collectives, fast_body(): lax.all_to_all(normed.reshape(peers, rows // peers, width), 'gx', split_a...  19.7 us
    all_to_all x1, blocking collectives, fast_body(): lax.all_to_all(mixed.reshape(peers, rows // peers, width), 'gx', split_ax...  16.1 us
    pallas_call x1, Pallas kernels, fast_body(): call(depth_step, (wide, narrow), [VMEM, VMEM, VMEM, ANY, VMEM, VMEM], [he...  11.9 us
    ppermute x2, waiting for transfers between devices, fast_body(): peer = lax.ppermute(normed, 'gz', swap)  10.4 us
    pallas_call x1, Pallas kernels, fast_body(): call(cross_kernel, narrow, [VMEM, ANY, VMEM], [held, pltpu.SemaphoreType....  10.1 us
    unnamed x28, local copies, waits for them, and re-layouts  7.25 us
  transfers between devices with their start and end apart: 6, of which 5 were waited for; matrix products, arithmetic and copies ran while one was open for 3% of the time, Pallas kernels for 6%

profile of v1, /device:TPU:0, one launch (start us, length us, event | category | flops | bytes accessed | tf_op | source)
XLA Modules:
  0.0 174.4 jit_solution(15416978236746571806)
XLA Ops:
  7.2 0.0 all-gather.5.cloned.1.call-start
  7.2 0.7 all-gather.5.cloned.1.call-update
  7.9 0.0 all-gather.7.cloned.1.call-start
  7.9 1.8 %pad_maximum_fusion = bf16[240,768]{1,0:T(8,128)(2,1)} fusion(bf16[48,768]{1,0:T(8,128)(2,1)} %param.24, bf16[48,768]{1,0:T(8,128)(2,1)} %param.22, bf16[144,768]{1,0:T(8,128)(2,1)} %bitcast.19), kind=kLoop, calls=%fused_computation.1 | loop fusion | flops 1105920 | bytes 737280 | tf_op jit(solution)/shard_map/concatenate | solution.py:433
  9.7 0.0 all-gather.7.cloned.1.call-update
  9.8 0.7 broadcast_add_fusion
  10.5 0.8 fusion.14
  11.3 2.2 %cosine_select_fusion.encoding_ref = f32[128,768]{1,0:T(8,128)S(1)} fusion(f32[768]{0:T(1024)S(1)} %fusion.8, f32[128]{0:T(128)S(1)} %get-tuple-element.31, f32[128]{0:T(128)S(1)} %get-tuple-element.32, f32[128]{0:T(128)} %constant.82.clone, pred[768]{0:T(1024)(128)(4,1)S(1)} %broadcast_compare_fusion.1, pred[768]{0:T(1024)(128)(4,1)S(1)} %get-tuple-element.30, ...), kind=kLoop, calls=%fused_computation | loop fusion | flops 393216 | bytes 400128 | tf_op jit(solution)/shard_map/encoding/jit(_where)/select_n | solution.py:450
  13.5 0.0 copy-start.6
  13.5 0.9 copy-done.6
  14.4 0.0 copy-start.8
  14.4 0.8 copy-done.8
  15.2 0.3 shard_map.203
  15.5 19.7 %all_to_all.10 = bf16[16,8,768]{2,1,0:T(8,128)(2,1)S(1)} all-to-all(bf16[16,8,768]{2,1,0:T(8,128)(2,1)S(1)} %bitcast.18), channel_id=1, replica_groups=mesh['gx'=16,'gz'=2] {'gx'}, dimensions={0} | all-to-all | bytes 393216 | tf_op jit(solution)/shard_map/all_to_all | solution.py:458
  35.1 26.9 %all-gather.5.cloned.1.call-done = bf16[2304,768]{1,0:T(8,128)(2,1)} async-done(((bf16[144,768]{1,0:T(8,128)(2,1)}), bf16[2304,768]{1,0:T(8,128)(2,1)}) %all-gather.5.cloned.1.call-update) | async-done | bytes 3538960 | tf_op jit(solution)/shard_map/all_gather | solution.py:432
  62.0 0.0 copy-start.2
  62.0 2.0 %copy-done.2 = bf16[2304,768]{1,0:T(8,128)(2,1)S(1)} copy-done((bf16[2304,768]{1,0:T(8,128)(2,1)S(1)}, bf16[2304,768]{1,0:T(8,128)(2,1)}, u32[]{:S(2)}) %copy-start.2) | copy-done | bytes 3538968
  64.0 0.0 copy-start.10
  64.0 0.8 copy-done.10
  64.8 10.1 %shard_map.204 = bf16[128,768]{1,0:T(8,128)(2,1)S(1)} custom-call(bf16[128,768]{1,0:T(8,128)(2,1)S(1)} %bitcast.15, bf16[16,144,768]{2,1,0:T(8,128)(2,1)S(1)} %bitcast.13, f32[128,128]{1,0:T(8,128)S(1)} %copy-done.10), custom_call_target="tpu_custom_call" | custom-call | tf_op jit(solution)/shard_map/pallas_call | solution.py:463
  75.0 0.0 copy-start.7
  75.0 16.1 %all_to_all.11 = bf16[16,8,768]{2,1,0:T(8,128)(2,1)S(1)} all-to-all(bf16[16,8,768]{2,1,0:T(8,128)(2,1)S(1)} %bitcast.16), channel_id=1, replica_groups=mesh['gx'=16,'gz'=2] {'gx'}, dimensions={0} | all-to-all | bytes 393216 | tf_op jit(solution)/shard_map/all_to_all | solution.py:469
  91.1 35.9 %all-gather.7.cloned.1.call-done = bf16[3840,768]{1,0:T(8,128)(2,1)} async-done(((bf16[240,768]{1,0:T(8,128)(2,1)}), bf16[3840,768]{1,0:T(8,128)(2,1)}) %all-gather.7.cloned.1.call-update) | async-done | bytes 5898256 | tf_op jit(solution)/shard_map/all_gather | solution.py:434
  127.0 0.0 copy-start
  127.0 2.7 %copy-done = bf16[3840,768]{1,0:T(8,128)(2,1)S(1)} copy-done((bf16[3840,768]{1,0:T(8,128)(2,1)S(1)}, bf16[3840,768]{1,0:T(8,128)(2,1)}, u32[]{:S(2)}) %copy-start) | copy-done | bytes 5898264
  129.6 0.0 copy-start.1
  129.6 2.1 %shard_map.205 = (f32[128,768]{1,0:T(8,128)S(1)}, bf16[128,768]{1,0:T(8,128)(2,1)S(1)}) custom-call(bf16[128,768]{1,0:T(8,128)(2,1)S(1)} %bitcast.14, f32[128,768]{1,0:T(8,128)S(1)} %get-tuple-element.15.refs_1_, bf16[16,240,768]{2,1,0:T(8,128)(2,1)S(1)} %bitcast.11, f32[1,768]{1,0:T(1,128)S(1)} %get-tuple-element.28.refs_3_), custom_call_target="tpu_custom_call" | custom-call | tf_op jit(solution)/shard_map/pallas_call | solution.py:477
  131.8 0.0 copy-start.13
  131.8 0.0 copy-start.3
  131.8 0.0 copy-start.4
  131.8 0.0 copy-start.5
  131.8 1.5 collective-permute-start
  133.3 5.6 %collective-permute-done.refs_1_ = bf16[128,768]{1,0:T(8,128)(2,1)S(1)} collective-permute-done((bf16[128,768]{1,0:T(8,128)(2,1)S(1)}, bf16[128,768]{1,0:T(8,128)(2,1)S(1)}, u32[]{:S(2)}, u32[]{:S(2)}) %collective-permute-start) | collective-permute-done | bytes 196640 | tf_op jit(solution)/shard_map/ppermute | solution.py:483
  138.9 0.0 copy-done.7
  138.9 0.0 copy-done.1
  138.9 11.9 %shard_map.206 = (f32[128,768]{1,0:T(8,128)S(1)}, bf16[128,768]{1,0:T(8,128)(2,1)S(1)}) custom-call(bf16[128,768]{1,0:T(8,128)(2,1)S(1)} %get-tuple-element.16.refs_0_, bf16[128,768]{1,0:T(8,128)(2,1)S(1)} %collective-permute-done.refs_1_, f32[128,768]{1,0:T(8,128)S(1)} %get-tuple-element.17.refs_2_, bf16[16,240,768]{2,1,0:T(8,128)(2,1)S(1)} %bitcast.12, ...), custom_call_target="tpu_custom_call" | custom-call | tf_op jit(solution)/shard_map/pallas_call | solution.py:489
  150.9 0.0 copy-start.9
  150.9 0.0 copy-start.11
  150.9 0.0 copy-start.12
  150.9 1.5 collective-permute-start.1
  152.4 0.0 copy-done.13
  152.4 4.8 %collective-permute-done.1.peer_ref = bf16[128,768]{1,0:T(8,128)(2,1)S(1)} collective-permute-done((bf16[128,768]{1,0:T(8,128)(2,1)S(1)}, bf16[128,768]{1,0:T(8,128)(2,1)S(1)}, u32[]{:S(2)}, u32[]{:S(2)}) %collective-permute-start.1) | collective-permute-done | bytes 196640 | tf_op jit(solution)/shard_map/ppermute | solution.py:498
  157.2 0.0 copy-done.3
  157.2 0.0 copy-done.4
  157.2 0.0 copy-done.5
  157.2 1.7 shard_map.207
  158.9 1.5 collective-permute-start.2
  160.4 0.6 collective-permute-start.3
  161.7 3.1 %collective-permute-done.3.got_head_ref = f32[1,128]{1,0:T(1,128)S(1)} collective-permute-done((f32[1,128]{1,0:T(1,128)S(1)}, f32[1,128]{1,0:T(1,128)S(1)}, u32[]{:S(2)}, u32[]{:S(2)}) %collective-permute-start.3) | collective-permute-done | bytes 544 | tf_op jit(solution)/shard_map/ppermute | solution.py:504
  164.7 0.0 collective-permute-done.2.got_ref
  164.7 0.0 copy-done.9
  164.7 0.0 copy-done.11
  164.7 0.0 copy-done.12
  164.7 0.9 shard_map.208
  165.7 0.5 broadcast.64
  166.2 0.7 reduce.3
  166.8 0.7 reshape.62
  (4 shorter events, 0.0 us)
Async XLA Ops:
  7.2 54.8 %all-gather.5.cloned.1.call-start = ((), (), s32[]{:S(2)}) async-start(), calls=%async_computation.2 | async-start | bytes 3760128 | tf_op jit(solution)/shard_map/all_gather | solution.py:432
  7.9 119.1 %all-gather.7.cloned.1.call-start = ((), (), s32[]{:S(2)}) async-start(), calls=%async_computation.3 | async-start | bytes 6266880 | tf_op jit(solution)/shard_map/all_gather | solution.py:434
  13.5 0.9 copy-start.6
  14.4 0.8 copy-start.8
  62.0 2.0 %copy-start.2 = (bf16[2304,768]{1,0:T(8,128)(2,1)S(1)}, bf16[2304,768]{1,0:T(8,128)(2,1)}, u32[]{:S(2)}) copy-start(bf16[2304,768]{1,0:T(8,128)(2,1)} %all-gather.5.cloned.1.call-done) | copy-start | bytes 10616836
  64.0 0.8 copy-start.10
  75.0 64.0 %copy-start.7 = (f32[128,256]{1,0:T(8,128)S(1)}, f32[128,256]{1,0:T(8,128)}, u32[]{:S(2)}) copy-start(f32[128,256]{1,0:T(8,128)} %constant.85.clone.refs_4_) | copy-start | bytes 393220
  127.0 2.7 %copy-start = (bf16[3840,768]{1,0:T(8,128)(2,1)S(1)}, bf16[3840,768]{1,0:T(8,128)(2,1)}, u32[]{:S(2)}) copy-start(bf16[3840,768]{1,0:T(8,128)(2,1)} %all-gather.7.cloned.1.call-done) | copy-start | bytes 17694724
  129.6 9.3 %copy-start.1 = (bf16[3840,768]{1,0:T(8,128)(2,1)S(1)}, bf16[3840,768]{1,0:T(8,128)(2,1)}, u32[]{:S(2)}) copy-start(bf16[3840,768]{1,0:T(8,128)(2,1)} %all-gather.7.cloned.1.call-done) | copy-start | bytes 17694724
  131.8 20.7 %copy-start.13 = (f32[768]{0:T(1024)S(1)}, f32[768]{0:T(1024)}, u32[]{:S(2)}) copy-start(f32[768]{0:T(1024)} %param.28) | copy-start | bytes 9220
  131.8 25.5 %copy-start.3 = (bf16[768,1536]{1,0:T(8,128)(2,1)S(1)}, bf16[768,1536]{1,0:T(8,128)(2,1)}, u32[]{:S(2)}) copy-start(bf16[768,1536]{1,0:T(8,128)(2,1)} %up_ref.1) | copy-start | bytes 7077892
  131.8 25.5 %copy-start.4 = (bf16[1536,768]{1,0:T(8,128)(2,1)S(1)}, bf16[1536,768]{1,0:T(8,128)(2,1)}, u32[]{:S(2)}) copy-start(bf16[1536,768]{1,0:T(8,128)(2,1)} %down_ref.1) | copy-start | bytes 7077892
  131.8 25.4 %copy-start.5 = (f32[128,128]{1,0:T(8,128)S(1)}, f32[128,128]{1,0:T(8,128)}, u32[]{:S(2)}) copy-start(f32[128,128]{1,0:T(8,128)} %constant.79.clone.eye_ref) | copy-start | bytes 196612
  131.8 7.1 %collective-permute-start = (bf16[128,768]{1,0:T(8,128)(2,1)S(1)}, bf16[128,768]{1,0:T(8,128)(2,1)S(1)}, u32[]{:S(2)}, u32[]{:S(2)}) collective-permute-start(bf16[128,768]{1,0:T(8,128)(2,1)S(1)} %get-tuple-element.16.refs_0_), channel_id=1, source_target_pairs={{0,1},{1,0},{2,3},{3,2},{4,5},{5,4},{6,7},{7,6},{8,9},{9,8},{10,11... | collective-permute-start | bytes 589832 | tf_op jit(solution)/shard_map/ppermute | solution.py:483
  150.9 13.8 %copy-start.9 = (bf16[128,128]{1,0:T(8,128)(2,1)S(1)}, bf16[128,128]{1,0:T(8,128)(2,1)}, u32[]{:S(2)}) copy-start(bf16[128,128]{1,0:T(8,128)(2,1)} %constant.83.clone.to_rows_ref.from_rows_ref) | copy-start | bytes 98308
  150.9 13.8 %copy-start.11 = (f32[128,128]{1,0:T(8,128)S(1)}, f32[128,128]{1,0:T(8,128)}, u32[]{:S(2)}) copy-start(f32[128,128]{1,0:T(8,128)} %constant.86.clone.cumulative_ref) | copy-start | bytes 196612
  150.9 13.8 %copy-start.12 = (f32[128,128]{1,0:T(8,128)S(1)}, f32[128,128]{1,0:T(8,128)}, u32[]{:S(2)}) copy-start(f32[128,128]{1,0:T(8,128)} %constant.87.clone.carried_ref) | copy-start | bytes 196612
  150.9 6.3 %collective-permute-start.1 = (bf16[128,768]{1,0:T(8,128)(2,1)S(1)}, bf16[128,768]{1,0:T(8,128)(2,1)S(1)}, u32[]{:S(2)}, u32[]{:S(2)}) collective-permute-start(bf16[128,768]{1,0:T(8,128)(2,1)S(1)} %get-tuple-element.19.own_ref), channel_id=1, source_target_pairs={{0,1},{1,0},{2,3},{3,2},{4,5},{5,4},{6,7},{7,6},{8,9},{9,8},{10,11... | collective-permute-start | bytes 589832 | tf_op jit(solution)/shard_map/ppermute | solution.py:498
  158.9 5.8 %collective-permute-start.2 = (bf16[128,768]{1,0:T(8,128)(2,1)S(1)}, bf16[128,768]{1,0:T(8,128)(2,1)S(1)}, u32[]{:S(2)}, u32[]{:S(2)}) collective-permute-start(bf16[128,768]{1,0:T(8,128)(2,1)S(1)} %get-tuple-element.21), channel_id=1, source_target_pairs={{0,1},{1,0},{2,3},{3,2},{4,5},{5,4},{6,7},{7,6},{8,9},{9,8},{10,11... | collective-permute-start | bytes 589832 | tf_op jit(solution)/shard_map/ppermute | solution.py:503
  160.4 4.3 %collective-permute-start.3 = (f32[1,128]{1,0:T(1,128)S(1)}, f32[1,128]{1,0:T(1,128)S(1)}, u32[]{:S(2)}, u32[]{:S(2)}) collective-permute-start(f32[1,128]{1,0:T(1,128)S(1)} %get-tuple-element.22.own_head_ref), channel_id=1, source_target_pairs={{0,1},{1,0},{2,3},{3,2},{4,5},{5,4},{6,7},{7,6},{8,9},{9,8},{10,11... | collective-permute-start | bytes 1544 | tf_op jit(solution)/shard_map/ppermute | solution.py:504
Sparse Core Ops, SparseCore 0:
  10.3 51.6 all-gather.4
  64.3 62.6 all-gather.6

commit v2 on v1

--- a/solution.py
+++ b/solution.py
@@ -169,7 +169,7 @@
 BF16 = jnp.bfloat16
 VMEM = pl.BlockSpec(memory_space=pltpu.VMEM)
 SMEM = pl.BlockSpec(memory_space=pltpu.SMEM)
-ANY = pl.BlockSpec(memory_space=pl.ANY)
+HBM = pl.BlockSpec(memory_space=pltpu.HBM)
 NT = (((1,), (1,)), ((), ()))
 NEG = -1e30
 
@@ -231,150 +231,117 @@
     normed_ref[...] = rms(stream, gain_ref[...])
 
 
-def head_pair(queries, keys, values, bias):
-    lane = lax.broadcasted_iota(jnp.int32, queries.shape, 1)
+def attend_heads(queries, keys, values, bias):
+    lane = lax.broadcasted_iota(jnp.int32, (queries.shape[0], 128), 1)
+    ones = jnp.ones((keys.shape[0], 128), BF16)
     outs = []
-    for head in range(2):
-        own = (lane < HDIM) if head == 0 else (lane >= HDIM)
-        masked = jnp.where(own, queries, jnp.zeros_like(queries))
-        scores = lax.dot_general(masked, keys, NT, preferred_element_type=F32)
-        scores = scores * (HDIM**-0.5) + bias
-        scores = scores - jnp.max(scores, -1, keepdims=True)
-        expo = jnp.exp(scores)
-        weights = (expo / jnp.sum(expo, -1, keepdims=True)).astype(BF16)
-        outs.append(jnp.dot(weights, values, preferred_element_type=F32))
-    return jnp.where(lane < HDIM, outs[0], outs[1]).astype(BF16)
-
-
-def pieces(start, size, chunk):
-    out, at = [], start
-    while at < start + size:
-        n = min(chunk - at % chunk, start + size - at)
-        out.append((at // chunk, at % chunk, at - start, n))
-        at += n
-    return out
-
-
-def qkv_copies(weights_ref, held_ref, sems, width, group, chunk, base):
-    copies, at = [], 0
-    for g in range(width // group):
-        of_group = []
-        for kind in range(3):
-            for block, row, to, n in pieces(kind * width + g * group, group, chunk):
-                of_group.append(
-                    pltpu.make_async_copy(
-                        weights_ref.at[block, pl.ds(base + row, n), :],
-                        held_ref.at[g, kind, pl.ds(to, n), :],
-                        sems.at[at],
-                    )
-                )
-                at += 1
-        copies.append(of_group)
-    return copies
-
-
-def qkv_copy_count(width, group, chunk):
-    return sum(
-        len(pieces(kind * width + g * group, group, chunk))
-        for g in range(width // group)
-        for kind in range(3)
-    )
-
-
-def cross_kernel(normed_ref, weights_ref, bias_ref, mixed_ref, held_ref, sems):
-    width, group = normed_ref.shape[1], held_ref.shape[2]
-    copies = qkv_copies(weights_ref, held_ref, sems, width, group, weights_ref.shape[1], 0)
-    for of_group in copies:
-        for copy in of_group:
-            copy.start()
-    bias = bias_ref[...]
-    for g, of_group in enumerate(copies):
-        for copy in of_group:
-            copy.wait()
-        normed = normed_ref[...]
-        q, k, v = (
-            lax.dot_general(normed, held_ref[g, kind], NT, preferred_element_type=F32).astype(BF16)
-            for kind in range(3)
-        )
-        for pair in range(group // 128):
-            at = slice(pair * 128, pair * 128 + 128)
-            mixed_ref[:, g * group + pair * 128 : g * group + pair * 128 + 128] = head_pair(
-                q[:, at], k[:, at], v[:, at], bias
-            )
-
-
-def row_copies(weights_ref, held_ref, sems, base, count):
-    return [
-        pltpu.make_async_copy(
-            weights_ref.at[block, pl.ds(base, count), :],
-            held_ref.at[pl.ds(block * count, count), :],
-            sems.at[block],
-        )
-        for block in range(weights_ref.shape[0])
-    ]
+    for at in range(0, queries.shape[1], 128):
+        at = slice(at, at + 128)
+        wide = jnp.concatenate([values[:, at], ones], axis=1)
+        pair = []
+        for own in (lane < HDIM, lane >= HDIM):
+            masked = jnp.where(own, queries[:, at], jnp.zeros_like(queries[:, at]))
+            scores = lax.dot_general(masked, keys[:, at], NT, preferred_element_type=F32) + bias
+            expo = jnp.exp(scores - jnp.max(scores, -1, keepdims=True)).astype(BF16)
+            mixed = jnp.dot(expo, wide, preferred_element_type=F32)
+            pair.append(mixed[:, :128] / mixed[:, 128:])
+        outs.append(jnp.where(lane < HDIM, pair[0], pair[1]).astype(BF16))
+    return jnp.concatenate(outs, axis=1)
+
+
+def project(normed, weights):
+    return lax.dot_general(normed, weights, NT, preferred_element_type=F32).astype(BF16)
+
+
+def cross_kernel(*refs, places):
+    position_ref, normed_ref, bias_ref = refs[:3]
+    piece_refs, (mixed_ref, held_ref) = refs[3:-2], refs[-2:]
+    width = normed_ref.shape[1]
+    y, c, x = position_ref[0], position_ref[1], position_ref[2]
+    for piece_ref, (first, other_y, other_c, other_x) in zip(piece_refs, places):
+        planes, rows, lanes = piece_ref.shape
+        at_y = 1 - y if other_y else y
+        at_c = 1 - c if other_c else c
+        at_x = 1 - x if other_x else x
+        at_lane = pl.multiple_of(at_x * lanes, 128)
+        for plane in range(planes):
+            block = (first + plane) * 4 + at_y * 2 + at_c
+            at_row = pl.multiple_of(block * rows, 16)
+            held_ref[pl.ds(at_row, rows), pl.ds(at_lane, lanes)] = piece_ref[plane]
+    normed = normed_ref[...]
+    q = project(normed, held_ref[:width]) * BF16(HDIM**-0.5)
+    k = project(normed, held_ref[width : 2 * width])
+    v = project(normed, held_ref[2 * width :])
+    mixed_ref[...] = attend_heads(q, k, v, bias_ref[...])
+
+
+def chunk_copy(weights_ref, held_ref, sem, base, count):
+    return pltpu.make_async_copy(weights_ref.at[:, pl.ds(base, count), :], held_ref, sem)
+
+
+def flat(ref):
+    held = ref[...]
+    return held.reshape(held.shape[0] * held.shape[1], held.shape[2])
 
 
 def cross_out_kernel(
-    mixed_ref, stream_ref, weights_ref, gain_ref, out_ref, normed_ref, held_ref, sems, *, base, count
+    mixed_ref, stream_ref, weights_ref, gain_ref, out_ref, normed_ref, held_ref, sem, *, base, count
 ):
-    copies = row_copies(weights_ref, held_ref, sems, base, count)
-    for copy in copies:
-        copy.start()
-    for copy in copies:
-        copy.wait()
-    stream = stream_ref[...] + jnp.dot(mixed_ref[...], held_ref[...], preferred_element_type=F32)
+    copy = chunk_copy(weights_ref, held_ref, sem, base, count)
+    copy.start()
+    copy.wait()
+    stream = stream_ref[...] + jnp.dot(mixed_ref[...], flat(held_ref), preferred_element_type=F32)
     out_ref[...] = stream
     normed_ref[...] = rms(stream, gain_ref[...])
 
 
 def depth_kernel(
-    own_ref,
-    peer_ref,
-    stream_ref,
-    weights_ref,
-    bias_ref,
-    gain_ref,
-    out_ref,
-    normed_ref,
-    held_ref,
-    out_held_ref,
-    sems,
-    out_sems,
-    *,
-    chunk,
-    base,
-    count,
+    own_ref, peer_ref, stream_ref, weights_ref, bias_ref, gain_ref,
+    out_ref, normed_ref, held_ref, out_held_ref, sem, out_sem, *, chunk, base, count,
 ):
-    width, group = own_ref.shape[1], held_ref.shape[2]
-    copies = qkv_copies(weights_ref, held_ref, sems, width, group, chunk, 0)
-    out_copies = row_copies(weights_ref, out_held_ref, out_sems, base, count)
-    for of_group in copies:
-        for copy in of_group:
-            copy.start()
-    for copy in out_copies:
-        copy.start()
-    bias = bias_ref[...]
-    mixed = []
-    for g, of_group in enumerate(copies):
-        for copy in of_group:
-            copy.wait()
-        own = own_ref[...]
-        both = jnp.concatenate([own, peer_ref[...]], axis=0)
-        q = lax.dot_general(own, held_ref[g, 0], NT, preferred_element_type=F32).astype(BF16)
-        k, v = (
-            lax.dot_general(both, held_ref[g, kind], NT, preferred_element_type=F32).astype(BF16)
-            for kind in (1, 2)
-        )
-        for pair in range(group // 128):
-            at = slice(pair * 128, pair * 128 + 128)
-            mixed.append(head_pair(q[:, at], k[:, at], v[:, at], bias))
-    for copy in out_copies:
-        copy.wait()
-    stream = stream_ref[...] + jnp.dot(
-        jnp.concatenate(mixed, axis=1), out_held_ref[...], preferred_element_type=F32
-    )
+    width = own_ref.shape[1]
+    copy = chunk_copy(weights_ref, held_ref, sem, 0, chunk)
+    out_copy = chunk_copy(weights_ref, out_held_ref, out_sem, base, count)
+    copy.start()
+    out_copy.start()
+    own = own_ref[...]
+    both = jnp.concatenate([own, peer_ref[...]], axis=0)
+    copy.wait()
+    weights = flat(held_ref)
+    q = project(own, weights[:width]) * BF16(HDIM**-0.5)
+    k = project(both, weights[width : 2 * width])
+    v = project(both, weights[2 * width :])
+    mixed = attend_heads(q, k, v, bias_ref[...])
+    out_copy.wait()
+    stream = stream_ref[...] + jnp.dot(mixed, flat(out_held_ref), preferred_element_type=F32)
     out_ref[...] = stream
     normed_ref[...] = rms(stream, gain_ref[...])
+
+
+def gather_planes(shard, peers):
+    lanes = shard.shape[1] // 2
+    half = lax.dynamic_slice_in_dim(shard, lax.axis_index("gz") * lanes, lanes, axis=1)
+    planes = peers // 4
+    groups = [[4 * z + k for z in range(planes)] for k in range(4)]
+    own = lax.all_gather(half, "gx", axis=0, axis_index_groups=groups)
+
+    def to_x(a):
+        return lax.ppermute(a, "gz", [(0, 1), (1, 0)])
+
+    def to_y(a):
+        return lax.ppermute(a, "gx", [(i, i ^ 2) for i in range(peers)])
+
+    def to_core(a):
+        return lax.ppermute(a, "gx", [(i, i ^ 1) for i in range(peers)])
+
+    low, high = own[: planes // 2], own[planes // 2 :]
+    at = planes // 2
+    low_x, high_y, low_y, high_x = to_x(low), to_y(high), to_y(low), to_x(high)
+    low_xy, high_xy = to_y(low_x), to_x(high_y)
+    pieces = [own, low_x, high_y, low_y, high_x, low_xy, high_xy]
+    places = [(0, 0, 0), (0, 0, 1), (at, 1, 0), (0, 1, 0), (at, 0, 1), (0, 1, 1), (at, 1, 1)]
+    both = [(f, y, 0, x) for f, y, x in places] + [(f, y, 1, x) for f, y, x in places]
+    return pieces + [to_core(piece) for piece in pieces], both
 
 
 def mlp_kernel(
@@ -422,16 +389,18 @@
     inlines, cross_dev, depth_dev, width = tokens.shape
     peers = lax.axis_size("gx")
     plan = Plan(inlines, cross_dev, depth_dev, peers)
-    rows, group = plan.rows, 256
+    rows = plan.rows
     chunk, count = cross_qkv.shape[1], cross_out.shape[0]
     swap = [(0, 1), (1, 0)]
     def const(a, dtype=F32):
         return jnp.asarray(np.asarray(a, np.float32), dtype)
     eye = const(np.eye(rows))
 
-    cross_w = lax.all_gather(cross_qkv.T, "gx", axis=0)
     rest = jnp.concatenate([depth_qkv.T, cross_out, depth_out], axis=0)
     rest_w = lax.all_gather(rest, "gx", axis=0)
+    cross_pieces, places = gather_planes(cross_qkv.T, peers)
+    gx = lax.axis_index("gx")
+    place = jnp.stack([gx // 2 % 2, gx % 2, lax.axis_index("gz")]).astype(jnp.int32)
 
     with jax.named_scope("encoding"):
         pairs = width // 2
@@ -458,18 +427,23 @@
     lined = lax.all_to_all(
         normed.reshape(peers, rows // peers, width), "gx", split_axis=0, concat_axis=0, tiled=True
     )
-    n_copies = qkv_copy_count(width, group, chunk)
-    held = pltpu.VMEM((width // group, 3, group, width), BF16)
+
+    def cross_step(*refs):
+        cross_kernel(*refs, places=places)
+
     mixed = call(
-        cross_kernel,
+        cross_step,
         narrow,
-        [VMEM, ANY, VMEM],
-        [held, pltpu.SemaphoreType.DMA((n_copies,))],
-    )(lined.reshape(rows, width), cross_w, const(np.where(plan.same_line, 0.0, NEG)))
+        [SMEM] + [VMEM] * (2 + len(cross_pieces)),
+        [pltpu.VMEM((3 * width, width), BF16)],
+    )(
+        place, lined.reshape(rows, width), const(np.where(plan.same_line, 0.0, NEG)), *cross_pieces
+    )
     mixed = lax.all_to_all(
         mixed.reshape(peers, rows // peers, width), "gx", split_axis=0, concat_axis=0, tiled=True
     )
-    out_held = pltpu.VMEM((width, width), BF16)
+    out_held = pltpu.VMEM((peers, count, width), BF16)
+    held = pltpu.VMEM((peers, chunk, width), BF16)
 
     def cross_out_step(*refs):
         cross_out_kernel(*refs, base=chunk, count=count)
@@ -477,8 +451,8 @@
     stream, normed = call(
         cross_out_step,
         (wide, narrow),
-        [VMEM, VMEM, ANY, VMEM],
-        [out_held, pltpu.SemaphoreType.DMA((peers,))],
+        [VMEM, VMEM, HBM, VMEM],
+        [out_held, pltpu.SemaphoreType.DMA],
     )(mixed.reshape(rows, width), stream, rest_w, gains[1:2])
     peer = lax.ppermute(normed, "gz", swap)
 
@@ -489,8 +463,8 @@
     stream, normed = call(
         depth_step,
         (wide, narrow),
-        [VMEM, VMEM, VMEM, ANY, VMEM, VMEM],
-        [held, out_held, pltpu.SemaphoreType.DMA((n_copies,)), pltpu.SemaphoreType.DMA((peers,))],
+        [VMEM, VMEM, VMEM, HBM, VMEM, VMEM],
+        [held, out_held, pltpu.SemaphoreType.DMA, pltpu.SemaphoreType.DMA],
     )(
         normed, peer, stream, rest_w,
         const(np.concatenate([depth_bias, depth_bias], axis=1)), gains[2:3],
@@ -523,6 +497,7 @@
             and inlines * depth_dev % peers == 0
             and inlines * cross_dev * depth_dev == 128
             and width % 256 == 0
+            and peers == 16
             and 3 * width % (16 * peers) == 0
             and width % (16 * peers) == 0
         )

time: 175 us -> 117 us (0.67)
  waiting for transfers between devices: 76.9 us -> 29.5 us
  Pallas kernels: 27 us -> 10.5 us
  starting transfers between devices: 5.23 us -> 19.7 us
  local copies, waits for them, and re-layouts: 9.29 us -> 5.55 us
  blocking collectives: 35.8 us -> 32.4 us
    all_gather x1, waiting for transfers between devices: 35.9 us -> 0.83 us  [fast_body(): rest_w = lax.all_gather(rest, 'gx', axis=0)]
    all_gather x1 -> x0, waiting for transfers between devices: 26.9 us -> none  [fast_body(): cross_w = lax.all_gather(cross_qkv.T, 'gx', axis=0)]
    all_to_all x1 -> x0, blocking collectives: 19.7 us -> none  [fast_body(): lax.all_to_all(normed.reshape(peers, rows // peers, width), 'gx', split_a...]
    all_gather x0 -> x1, blocking collectives: none -> 18.1 us  [gather_planes(): own = lax.all_gather(half, 'gx', axis=0, axis_index_groups=groups)]
    pallas_call x3, Pallas kernels: 24.1 us -> 7.57 us  [the longest x1 3.99 us: fast_body(): call(cross_step, narrow, [SMEM] + [VMEM] * (2 + len(cross_pieces)), [pltp...]
    all_to_all x0 -> x1, waiting for transfers between devices: none -> 11.3 us  [fast_body(): lax.all_to_all(normed.reshape(peers, rows // peers, width), 'gx', split_a...]
    ppermute x0 -> x13, starting transfers between devices: none -> 7.43 us  [the longest x3 3.58 us: to_x(): return lax.ppermute(a, 'gz', [(0, 1), (1, 0)])]
    all_to_all x0 -> x1, starting transfers between devices: none -> 6.44 us  [fast_body(): lax.all_to_all(normed.reshape(peers, rows // peers, width), 'gx', split_a...]
  transfers between devices with their start and end apart: 6 -> 19, of which waited for: 5 -> 6; matrix products, arithmetic and copies ran while one was open for 3% -> 1% of each run, Pallas kernels for 6% -> 4%
where the time goes in v2:
time: 117 us
  blocking collectives  32.4 us (28%)
  waiting for transfers between devices  29.5 us (25%)
  starting transfers between devices  19.7 us (17%)
  between operations  15 us (13%)
  Pallas kernels  10.5 us (9%)
  local copies, waits for them, and re-layouts  5.55 us (5%)
  other arithmetic  4.22 us (4%)
    all_gather x1, blocking collectives, gather_planes(): own = lax.all_gather(half, 'gx', axis=0, axis_index_groups=groups)  18.1 us
    all_to_all x1, blocking collectives, fast_body(): lax.all_to_all(mixed.reshape(peers, rows // peers, width), 'gx', split_ax...  14.3 us
    all_to_all x1, waiting for transfers between devices, fast_body(): lax.all_to_all(normed.reshape(peers, rows // peers, width), 'gx', split_a...  11.3 us
    ppermute x2, waiting for transfers between devices, fast_body(): peer = lax.ppermute(normed, 'gz', swap)  9.93 us
    all_to_all x1, starting transfers between devices, fast_body(): lax.all_to_all(normed.reshape(peers, rows // peers, width), 'gx', split_a...  6.44 us
    ppermute x3, waiting for transfers between devices, to_x(): return lax.ppermute(a, 'gz', [(0, 1), (1, 0)])  4.31 us
    unnamed x36, local copies, waits for them, and re-layouts  4.27 us
    pallas_call x1, Pallas kernels, fast_body(): call(cross_step, narrow, [SMEM] + [VMEM] * (2 + len(cross_pieces)), [pltp...  3.99 us
  transfers between devices with their start and end apart: 19, of which 6 were waited for; matrix products, arithmetic and copies ran while one was open for 1% of the time, Pallas kernels for 4%

profile of v2, /device:TPU:0, one launch (start us, length us, event | category | flops | bytes accessed | tf_op | source)
XLA Modules:
  0.0 116.8 jit_solution(3282439254908551146)
XLA Ops:
  7.2 0.0 copy-start
  7.2 0.0 copy-start.16
  7.2 0.0 copy-start.17
  7.2 0.0 copy-start.15
  7.2 0.0 copy-start.9
  7.3 0.0 all-gather.4.cloned.1.call-start
  7.3 1.9 %pad_maximum_fusion = bf16[240,768]{1,0:T(8,128)(2,1)} fusion(bf16[48,768]{1,0:T(8,128)(2,1)} %param.24, bf16[48,768]{1,0:T(8,128)(2,1)} %param.22, bf16[144,768]{1,0:T(8,128)(2,1)} %bitcast.30), kind=kLoop, calls=%fused_computation.1 | loop fusion | flops 1105920 | bytes 737280 | tf_op jit(solution)/shard_map/concatenate | solution.py:399
  9.2 0.0 all-gather.4.cloned.1.call-update
  9.3 18.1 %all-gather = bf16[576,384]{1,0:T(8,128)(2,1)S(1)} all-gather(bf16[144,384]{1,0:T(8,128)(2,1)S(1)} %dynamic-slice_bitcast_fusion), channel_id=2, replica_groups={{0,8,16,24},{2,10,18,26},{4,12,20,28},{6,14,22,30},{1,9,17,25},{3,11,19..., dimensions={0}, use_global_device_ids=true | all-gather | bytes 552960 | tf_op jit(solution)/shard_map/all_gather | solution.py:326
  27.4 1.5 %collective-permute-start.1 = (bf16[2,144,384]{2,1,0:T(8,128)(2,1)S(1)}, bf16[2,144,384]{2,1,0:T(8,128)(2,1)S(1)}, u32[]{:S(2)}, u32[]{:S(2)}) collective-permute-start(bf16[2,144,384]{2,1,0:T(8,128)(2,1)S(1)} %bitcast.28), channel_id=1, source_target_pairs={{0,4},{2,6},{4,0},{6,2},{8,12},{10,14},{12,8},{14,10},{16,20},{18,... | collective-permute-start | bytes 663560 | tf_op jit(solution)/shard_map/ppermute | solution.py:332
  29.0 1.5 %collective-permute-start.3 = (bf16[2,144,384]{2,1,0:T(8,128)(2,1)S(1)}, bf16[2,144,384]{2,1,0:T(8,128)(2,1)S(1)}, u32[]{:S(2)}, u32[]{:S(2)}) collective-permute-start(bf16[2,144,384]{2,1,0:T(8,128)(2,1)S(1)} %bitcast.29), channel_id=1, source_target_pairs={{0,1},{1,0},{2,3},{3,2},{4,5},{5,4},{6,7},{7,6},{8,9},{9,8},{10,11... | collective-permute-start | bytes 663560 | tf_op jit(solution)/shard_map/ppermute | solution.py:329
  30.5 0.5 collective-permute-start
  31.0 0.6 collective-permute-start.2
  31.6 0.0 collective-permute-start.6
  31.6 1.5 %cosine_select_fusion.encoding_ref = f32[128,768]{1,0:T(8,128)S(1)} fusion(f32[768]{0:T(1024)S(1)} %fusion.8, f32[128]{0:T(128)S(1)} %get-tuple-element.33, f32[128]{0:T(128)S(1)} %get-tuple-element.34, f32[128]{0:T(128)S(1)} %copy-done.15, pred[768]{0:T(1024)(128)(4,1)S(1)} %broadcast_compare_fusion.1, pred[768]{0:T(1024)(128)(4,1)S(1)} %get-tuple-element.32, ...), kind=kLoop, calls=%fused_computation | loop fusion | flops 393216 | bytes 400128 | tf_op jit(solution)/shard_map/encoding/jit(_where)/select_n | solution.py:419
  33.2 4.3 %collective-permute-done.refs_4_ = bf16[2,144,384]{2,1,0:T(8,128)(2,1)S(1)} collective-permute-done((bf16[2,144,384]{2,1,0:T(8,128)(2,1)S(1)}, bf16[2,144,384]{2,1,0:T(8,128)(2,1)S(1)}, u32[]{:S(2)}, u32[]{:S(2)}) %collective-permute-start) | collective-permute-done | bytes 221216 | tf_op jit(solution)/shard_map/ppermute | solution.py:329
  37.5 0.5 collective-permute-start.4
  38.0 0.0 collective-permute-done.1.refs_5_
  38.0 0.0 collective-permute-start.7
  38.0 0.0 collective-permute-done.3.refs_7_
  38.0 1.6 %collective-permute-start.5 = (bf16[2,144,384]{2,1,0:T(8,128)(2,1)S(1)}, bf16[2,144,384]{2,1,0:T(8,128)(2,1)S(1)}, u32[]{:S(2)}, u32[]{:S(2)}) collective-permute-start(bf16[2,144,384]{2,1,0:T(8,128)(2,1)S(1)} %collective-permute-done.1.refs_5_), channel_id=1, source_target_pairs={{0,1},{1,0},{2,3},{3,2},{4,5},{5,4},{6,7},{7,6},{8,9},{9,8},{10,11... | collective-permute-start | bytes 663560 | tf_op jit(solution)/shard_map/ppermute | solution.py:329
  39.5 0.0 collective-permute-done.2.refs_6_
  39.5 0.2 collective-permute-start.8
  39.7 0.3 shard_map.203
  40.1 0.0 copy-start.7
  40.1 0.7 copy-done.7
  40.7 6.4 %all-to-all-start = ((bf16[16,8,768]{2,1,0:T(8,128)(2,1)}), bf16[16,8,768]{2,1,0:T(8,128)(2,1)S(1)}, u32[]{:S(2)}, u32[]{:S(2)}) async-start(bf16[16,8,768]{2,1,0:T(8,128)(2,1)} %bitcast.25), calls=%async_computation | async-start | bytes 393216 | tf_op jit(solution)/shard_map/all_to_all | solution.py:427
  47.2 0.0 collective-permute-done.4.refs_8_
  47.2 0.5 collective-permute-start.10
  47.7 0.0 collective-permute-done.5.refs_9_
  47.7 0.1 collective-permute-start.9
  47.8 0.0 collective-permute-done.7.refs_11_
  47.8 0.4 collective-permute-start.11
  48.2 0.0 collective-permute-done.8.refs_12_
  48.2 0.1 collective-permute-start.12
  48.3 0.1 pad_add_fusion.refs_0_
  48.4 11.3 %all-to-all-done = bf16[16,8,768]{2,1,0:T(8,128)(2,1)S(1)} async-done(((bf16[16,8,768]{2,1,0:T(8,128)(2,1)}), bf16[16,8,768]{2,1,0:T(8,128)(2,1)S(1)}, u32[]{:S(2)}, u32[]{:S(2)}) %all-to-all-start) | async-done | bytes 196640 | tf_op jit(solution)/shard_map/all_to_all | solution.py:427
  59.7 0.0 collective-permute-done.10.refs_14_
  59.7 0.0 collective-permute-done.9.refs_13_
  59.7 0.0 copy-start.10
  59.7 0.8 copy-done.10
  60.5 4.0 %shard_map.204 = bf16[128,768]{1,0:T(8,128)(2,1)S(1)} custom-call(s32[3]{0:T(128)S(1)} %pad_add_fusion.refs_0_, bf16[128,768]{1,0:T(8,128)(2,1)S(1)} %bitcast.21, f32[128,128]{1,0:T(8,128)S(1)} %copy-done.10, bf16[4,144,384]{2,1,0:T(8,128)(2,1)S(1)} %bitcast.20, bf16[2,144,384]{2,1,0:T(8,128)(2,1)S(1)} %collective-permute-done.refs_4_, ...), custom_call_target="tpu_custom_call" | custom-call | tf_op jit(solution)/shard_map/pallas_call | solution.py:434
  64.5 14.3 %all_to_all.10 = bf16[16,8,768]{2,1,0:T(8,128)(2,1)S(1)} all-to-all(bf16[16,8,768]{2,1,0:T(8,128)(2,1)S(1)} %bitcast.22), channel_id=1, replica_groups=mesh['gx'=16,'gz'=2] {'gx'}, dimensions={0} | all-to-all | bytes 393216 | tf_op jit(solution)/shard_map/all_to_all | solution.py:442
  78.9 0.8 all-gather.4.cloned.1.call-done
  79.7 2.7 %copy-done.1 = bf16[3840,768]{1,0:T(8,128)(2,1)S(1)} copy-done((bf16[3840,768]{1,0:T(8,128)(2,1)S(1)}, bf16[3840,768]{1,0:T(8,128)(2,1)}, u32[]{:S(2)}) %copy-start.1) | copy-done | bytes 5898264
  82.4 0.5 shard_map.205
  82.9 1.9 %collective-permute-start.13 = (bf16[128,768]{1,0:T(8,128)(2,1)S(1)}, bf16[128,768]{1,0:T(8,128)(2,1)S(1)}, u32[]{:S(2)}, u32[]{:S(2)}) collective-permute-start(bf16[128,768]{1,0:T(8,128)(2,1)S(1)} %get-tuple-element.16.refs_0_), channel_id=1, source_target_pairs={{0,1},{1,0},{2,3},{3,2},{4,5},{5,4},{6,7},{7,6},{8,9},{9,8},{10,11... | collective-permute-start | bytes 589832 | tf_op jit(solution)/shard_map/ppermute | solution.py:457
  84.8 5.3 %collective-permute-done.13.refs_1_ = bf16[128,768]{1,0:T(8,128)(2,1)S(1)} collective-permute-done((bf16[128,768]{1,0:T(8,128)(2,1)S(1)}, bf16[128,768]{1,0:T(8,128)(2,1)S(1)}, u32[]{:S(2)}, u32[]{:S(2)}) %collective-permute-start.13) | collective-permute-done | bytes 196640 | tf_op jit(solution)/shard_map/ppermute | solution.py:457
  90.1 0.0 copy-start.4
  90.1 0.0 copy-start.5
  90.2 3.0 %shard_map.206 = (f32[128,768]{1,0:T(8,128)S(1)}, bf16[128,768]{1,0:T(8,128)(2,1)S(1)}) custom-call(bf16[128,768]{1,0:T(8,128)(2,1)S(1)} %get-tuple-element.16.refs_0_, bf16[128,768]{1,0:T(8,128)(2,1)S(1)} %collective-permute-done.13.refs_1_, f32[128,768]{1,0:T(8,128)S(1)} %get-tuple-element.17.refs_2_, bf16[16,240,768]{2,1,0:T(8,128)(2,1)S(1)} %bitcast.18, ...), custom_call_target="tpu_custom_call" | custom-call | tf_op jit(solution)/shard_map/pallas_call | solution.py:463
  93.2 1.8 %collective-permute-start.14 = (bf16[128,768]{1,0:T(8,128)(2,1)S(1)}, bf16[128,768]{1,0:T(8,128)(2,1)S(1)}, u32[]{:S(2)}, u32[]{:S(2)}) collective-permute-start(bf16[128,768]{1,0:T(8,128)(2,1)S(1)} %get-tuple-element.19.own_ref), channel_id=1, source_target_pairs={{0,1},{1,0},{2,3},{3,2},{4,5},{5,4},{6,7},{7,6},{8,9},{9,8},{10,11... | collective-permute-start | bytes 589832 | tf_op jit(solution)/shard_map/ppermute | solution.py:472
  95.0 4.6 %collective-permute-done.14.peer_ref = bf16[128,768]{1,0:T(8,128)(2,1)S(1)} collective-permute-done((bf16[128,768]{1,0:T(8,128)(2,1)S(1)}, bf16[128,768]{1,0:T(8,128)(2,1)S(1)}, u32[]{:S(2)}, u32[]{:S(2)}) %collective-permute-start.14) | collective-permute-done | bytes 196640 | tf_op jit(solution)/shard_map/ppermute | solution.py:472
  99.6 0.0 copy-start.11
  99.6 0.0 copy-start.12
  99.7 1.7 %shard_map.207 = (bf16[128,768]{1,0:T(8,128)(2,1)S(1)}, bf16[128,768]{1,0:T(8,128)(2,1)S(1)}, f32[1,128]{1,0:T(1,128)S(1)}, f32[1,128]{1,0:T(1,128)S(1)}) custom-call(bf16[128,768]{1,0:T(8,128)(2,1)S(1)} %get-tuple-element.19.own_ref, bf16[128,768]{1,0:T(8,128)(2,1)S(1)} %collective-permute-done.14.peer_ref, f32[128,768]{1,0:T(8,128)S(1)} %get-tuple-element.18.stream_ref, ...), custom_call_target="tpu_custom_call" | custom-call | tf_op jit(solution)/shard_map/pallas_call | solution.py:474
  101.3 1.7 %collective-permute-start.15 = (bf16[128,768]{1,0:T(8,128)(2,1)S(1)}, bf16[128,768]{1,0:T(8,128)(2,1)S(1)}, u32[]{:S(2)}, u32[]{:S(2)}) collective-permute-start(bf16[128,768]{1,0:T(8,128)(2,1)S(1)} %get-tuple-element.21), channel_id=1, source_target_pairs={{0,1},{1,0},{2,3},{3,2},{4,5},{5,4},{6,7},{7,6},{8,9},{9,8},{10,11... | collective-permute-start | bytes 589832 | tf_op jit(solution)/shard_map/ppermute | solution.py:477
  103.0 0.4 collective-permute-start.16
  104.1 3.1 %collective-permute-done.16.got_head_ref = f32[1,128]{1,0:T(1,128)S(1)} collective-permute-done((f32[1,128]{1,0:T(1,128)S(1)}, f32[1,128]{1,0:T(1,128)S(1)}, u32[]{:S(2)}, u32[]{:S(2)}) %collective-permute-start.16) | collective-permute-done | bytes 544 | tf_op jit(solution)/shard_map/ppermute | solution.py:478
  107.1 0.0 collective-permute-done.15.got_ref
  107.1 0.9 shard_map.208
  108.1 0.5 broadcast.67
  108.6 0.7 reduce.3
  109.2 0.7 reshape.62
  (33 shorter events, 0.2 us)
Async XLA Ops:
  7.2 2.1 %copy-start = (bf16[768,144]{0,1:T(8,128)(2,1)S(1)}, bf16[768,144]{0,1:T(8,128)(2,1)}, u32[]{:S(2)}) copy-start(bf16[768,144]{0,1:T(8,128)(2,1)} %param.21) | copy-start | bytes 663556
  7.2 24.4 %copy-start.16 = (f32[128]{0:T(128)S(1)}, f32[128]{0:T(128)}, u32[]{:S(2)}) copy-start(f32[128]{0:T(128)} %constant.103.clone) | copy-start | bytes 1540
  7.2 24.4 %copy-start.17 = (f32[128]{0:T(128)S(1)}, f32[128]{0:T(128)}, u32[]{:S(2)}) copy-start(f32[128]{0:T(128)} %constant.104.clone) | copy-start | bytes 1540
  7.2 24.4 %copy-start.15 = (f32[128]{0:T(128)S(1)}, f32[128]{0:T(128)}, u32[]{:S(2)}) copy-start(f32[128]{0:T(128)} %constant.105.clone) | copy-start | bytes 1540
  7.2 32.5 %copy-start.9 = (bf16[128,128]{1,0:T(8,128)(2,1)S(1)}, bf16[128,128]{1,0:T(8,128)(2,1)}, u32[]{:S(2)}) copy-start(bf16[128,128]{1,0:T(8,128)(2,1)} %constant.106.clone.to_rows_ref.from_rows_ref) | copy-start | bytes 98308
  7.2 32.5 %copy-start.13 = (f32[3,768]{1,0:T(4,128)S(1)}, f32[3,768]{1,0:T(4,128)}, u32[]{:S(2)}) copy-start(f32[3,768]{1,0:T(4,128)} %param.27) | copy-start | bytes 27652
  7.2 32.5 %copy-start.6 = (bf16[4,4,8,768]{3,2,1,0:T(8,128)(2,1)S(1)}, bf16[4,4,8,768]{3,2,1,0:T(8,128)(2,1)}, u32[]{:S(2)}) copy-start(bf16[4,4,8,768]{3,2,1,0:T(8,128)(2,1)} %param.20) | copy-start | bytes 589828
  7.3 72.4 %all-gather.4.cloned.1.call-start = ((), (), s32[]{:S(2)}) async-start(), calls=%async_computation.2 | async-start | bytes 6266880 | tf_op jit(solution)/shard_map/all_gather | solution.py:400
  27.4 10.5 %collective-permute-start.1 = (bf16[2,144,384]{2,1,0:T(8,128)(2,1)S(1)}, bf16[2,144,384]{2,1,0:T(8,128)(2,1)S(1)}, u32[]{:S(2)}, u32[]{:S(2)}) collective-permute-start(bf16[2,144,384]{2,1,0:T(8,128)(2,1)S(1)} %bitcast.28), channel_id=1, source_target_pairs={{0,4},{2,6},{4,0},{6,2},{8,12},{10,14},{12,8},{14,10},{16,20},{18,... | collective-permute-start | bytes 663560 | tf_op jit(solution)/shard_map/ppermute | solution.py:332
  29.0 9.0 %collective-permute-start.3 = (bf16[2,144,384]{2,1,0:T(8,128)(2,1)S(1)}, bf16[2,144,384]{2,1,0:T(8,128)(2,1)S(1)}, u32[]{:S(2)}, u32[]{:S(2)}) collective-permute-start(bf16[2,144,384]{2,1,0:T(8,128)(2,1)S(1)} %bitcast.29), channel_id=1, source_target_pairs={{0,1},{1,0},{2,3},{3,2},{4,5},{5,4},{6,7},{7,6},{8,9},{9,8},{10,11... | collective-permute-start | bytes 663560 | tf_op jit(solution)/shard_map/ppermute | solution.py:329
  30.5 7.0 %collective-permute-start = (bf16[2,144,384]{2,1,0:T(8,128)(2,1)S(1)}, bf16[2,144,384]{2,1,0:T(8,128)(2,1)S(1)}, u32[]{:S(2)}, u32[]{:S(2)}) collective-permute-start(bf16[2,144,384]{2,1,0:T(8,128)(2,1)S(1)} %bitcast.26), channel_id=1, source_target_pairs={{0,1},{1,0},{2,3},{3,2},{4,5},{5,4},{6,7},{7,6},{8,9},{9,8},{10,11... | collective-permute-start | bytes 663560 | tf_op jit(solution)/shard_map/ppermute | solution.py:329
  31.0 8.6 %collective-permute-start.2 = (bf16[2,144,384]{2,1,0:T(8,128)(2,1)S(1)}, bf16[2,144,384]{2,1,0:T(8,128)(2,1)S(1)}, u32[]{:S(2)}, u32[]{:S(2)}) collective-permute-start(bf16[2,144,384]{2,1,0:T(8,128)(2,1)S(1)} %bitcast.27), channel_id=1, source_target_pairs={{0,4},{2,6},{4,0},{6,2},{8,12},{10,14},{12,8},{14,10},{16,20},{18,... | collective-permute-start | bytes 663560 | tf_op jit(solution)/shard_map/ppermute | solution.py:332
  31.6 28.1 %collective-permute-start.6 = (bf16[4,144,384]{2,1,0:T(8,128)(2,1)S(1)}, bf16[4,144,384]{2,1,0:T(8,128)(2,1)S(1)}, u32[]{:S(2)}, u32[]{:S(2)}) collective-permute-start(bf16[4,144,384]{2,1,0:T(8,128)(2,1)S(1)} %bitcast.19), channel_id=1, source_target_pairs={{0,2},{2,0},{4,6},{6,4},{8,10},{10,8},{12,14},{14,12},{16,18},{18,... | collective-permute-start | bytes 1327112 | tf_op jit(solution)/shard_map/ppermute | solution.py:335
  37.5 9.7 %collective-permute-start.4 = (bf16[2,144,384]{2,1,0:T(8,128)(2,1)S(1)}, bf16[2,144,384]{2,1,0:T(8,128)(2,1)S(1)}, u32[]{:S(2)}, u32[]{:S(2)}) collective-permute-start(bf16[2,144,384]{2,1,0:T(8,128)(2,1)S(1)} %collective-permute-done.refs_4_), channel_id=1, source_target_pairs={{0,4},{2,6},{4,0},{6,2},{8,12},{10,14},{12,8},{14,10},{16,20},{18,... | collective-permute-start | bytes 663560 | tf_op jit(solution)/shard_map/ppermute | solution.py:332
  38.0 9.8 %collective-permute-start.7 = (bf16[2,144,384]{2,1,0:T(8,128)(2,1)S(1)}, bf16[2,144,384]{2,1,0:T(8,128)(2,1)S(1)}, u32[]{:S(2)}, u32[]{:S(2)}) collective-permute-start(bf16[2,144,384]{2,1,0:T(8,128)(2,1)S(1)} %collective-permute-done.refs_4_), channel_id=1, source_target_pairs={{0,2},{2,0},{4,6},{6,4},{8,10},{10,8},{12,14},{14,12},{16,18},{18,... | collective-permute-start | bytes 663560 | tf_op jit(solution)/shard_map/ppermute | solution.py:335
  38.0 9.7 %collective-permute-start.5 = (bf16[2,144,384]{2,1,0:T(8,128)(2,1)S(1)}, bf16[2,144,384]{2,1,0:T(8,128)(2,1)S(1)}, u32[]{:S(2)}, u32[]{:S(2)}) collective-permute-start(bf16[2,144,384]{2,1,0:T(8,128)(2,1)S(1)} %collective-permute-done.1.refs_5_), channel_id=1, source_target_pairs={{0,1},{1,0},{2,3},{3,2},{4,5},{5,4},{6,7},{7,6},{8,9},{9,8},{10,11... | collective-permute-start | bytes 663560 | tf_op jit(solution)/shard_map/ppermute | solution.py:329
  39.5 8.6 %collective-permute-start.8 = (bf16[2,144,384]{2,1,0:T(8,128)(2,1)S(1)}, bf16[2,144,384]{2,1,0:T(8,128)(2,1)S(1)}, u32[]{:S(2)}, u32[]{:S(2)}) collective-permute-start(bf16[2,144,384]{2,1,0:T(8,128)(2,1)S(1)} %collective-permute-done.1.refs_5_), channel_id=1, source_target_pairs={{0,2},{2,0},{4,6},{6,4},{8,10},{10,8},{12,14},{14,12},{16,18},{18,... | collective-permute-start | bytes 663560 | tf_op jit(solution)/shard_map/ppermute | solution.py:335
  40.1 0.7 copy-start.7
  40.7 18.9 %all-to-all-start = ((bf16[16,8,768]{2,1,0:T(8,128)(2,1)}), bf16[16,8,768]{2,1,0:T(8,128)(2,1)S(1)}, u32[]{:S(2)}, u32[]{:S(2)}) async-start(bf16[16,8,768]{2,1,0:T(8,128)(2,1)} %bitcast.25), calls=%async_computation | async-start | bytes 393216 | tf_op jit(solution)/shard_map/all_to_all | solution.py:427
  47.2 12.5 %collective-permute-start.10 = (bf16[2,144,384]{2,1,0:T(8,128)(2,1)S(1)}, bf16[2,144,384]{2,1,0:T(8,128)(2,1)}, u32[]{:S(2)}, u32[]{:S(2)}) collective-permute-start(bf16[2,144,384]{2,1,0:T(8,128)(2,1)S(1)} %collective-permute-done.3.refs_7_), channel_id=1, source_target_pairs={{0,2},{2,0},{4,6},{6,4},{8,10},{10,8},{12,14},{14,12},{16,18},{18,... | collective-permute-start | bytes 663560 | tf_op jit(solution)/shard_map/ppermute | solution.py:335
  47.7 12.0 %collective-permute-start.9 = (bf16[2,144,384]{2,1,0:T(8,128)(2,1)S(1)}, bf16[2,144,384]{2,1,0:T(8,128)(2,1)}, u32[]{:S(2)}, u32[]{:S(2)}) collective-permute-start(bf16[2,144,384]{2,1,0:T(8,128)(2,1)S(1)} %collective-permute-done.2.refs_6_), channel_id=1, source_target_pairs={{0,2},{2,0},{4,6},{6,4},{8,10},{10,8},{12,14},{14,12},{16,18},{18,... | collective-permute-start | bytes 663560 | tf_op jit(solution)/shard_map/ppermute | solution.py:335
  47.8 11.9 %collective-permute-start.11 = (bf16[2,144,384]{2,1,0:T(8,128)(2,1)S(1)}, bf16[2,144,384]{2,1,0:T(8,128)(2,1)}, u32[]{:S(2)}, u32[]{:S(2)}) collective-permute-start(bf16[2,144,384]{2,1,0:T(8,128)(2,1)S(1)} %collective-permute-done.4.refs_8_), channel_id=1, source_target_pairs={{0,2},{2,0},{4,6},{6,4},{8,10},{10,8},{12,14},{14,12},{16,18},{18,... | collective-permute-start | bytes 663560 | tf_op jit(solution)/shard_map/ppermute | solution.py:335
  48.2 11.5 %collective-permute-start.12 = (bf16[2,144,384]{2,1,0:T(8,128)(2,1)S(1)}, bf16[2,144,384]{2,1,0:T(8,128)(2,1)}, u32[]{:S(2)}, u32[]{:S(2)}) collective-permute-start(bf16[2,144,384]{2,1,0:T(8,128)(2,1)S(1)} %collective-permute-done.5.refs_9_), channel_id=1, source_target_pairs={{0,2},{2,0},{4,6},{6,4},{8,10},{10,8},{12,14},{14,12},{16,18},{18,... | collective-permute-start | bytes 663560 | tf_op jit(solution)/shard_map/ppermute | solution.py:335
  59.7 0.8 copy-start.10
  79.7 2.7 %copy-start.1 = (bf16[3840,768]{1,0:T(8,128)(2,1)S(1)}, bf16[3840,768]{1,0:T(8,128)(2,1)}, u32[]{:S(2)}) copy-start(bf16[3840,768]{1,0:T(8,128)(2,1)} %all-gather.4.cloned.1.call-done) | copy-start | bytes 17694724
  82.4 7.8 %copy-start.2 = (bf16[3840,768]{1,0:T(8,128)(2,1)S(1)}, bf16[3840,768]{1,0:T(8,128)(2,1)}, u32[]{:S(2)}) copy-start(bf16[3840,768]{1,0:T(8,128)(2,1)} %all-gather.4.cloned.1.call-done) | copy-start | bytes 17694724
  82.4 7.8 %copy-start.8 = (f32[128,256]{1,0:T(8,128)S(1)}, f32[128,256]{1,0:T(8,128)}, u32[]{:S(2)}) copy-start(f32[128,256]{1,0:T(8,128)} %constant.108.clone.refs_4_) | copy-start | bytes 393220
  82.9 7.2 %collective-permute-start.13 = (bf16[128,768]{1,0:T(8,128)(2,1)S(1)}, bf16[128,768]{1,0:T(8,128)(2,1)S(1)}, u32[]{:S(2)}, u32[]{:S(2)}) collective-permute-start(bf16[128,768]{1,0:T(8,128)(2,1)S(1)} %get-tuple-element.16.refs_0_), channel_id=1, source_target_pairs={{0,1},{1,0},{2,3},{3,2},{4,5},{5,4},{6,7},{7,6},{8,9},{9,8},{10,11... | collective-permute-start | bytes 589832 | tf_op jit(solution)/shard_map/ppermute | solution.py:457
  90.1 4.9 %copy-start.14 = (f32[768]{0:T(1024)S(1)}, f32[768]{0:T(1024)}, u32[]{:S(2)}) copy-start(f32[768]{0:T(1024)} %param.28) | copy-start | bytes 9220
  90.1 9.5 %copy-start.3 = (bf16[768,1536]{1,0:T(8,128)(2,1)S(1)}, bf16[768,1536]{1,0:T(8,128)(2,1)}, u32[]{:S(2)}) copy-start(bf16[768,1536]{1,0:T(8,128)(2,1)} %up_ref.1) | copy-start | bytes 7077892
  90.1 9.5 %copy-start.4 = (bf16[1536,768]{1,0:T(8,128)(2,1)S(1)}, bf16[1536,768]{1,0:T(8,128)(2,1)}, u32[]{:S(2)}) copy-start(bf16[1536,768]{1,0:T(8,128)(2,1)} %down_ref.1) | copy-start | bytes 7077892
  90.1 9.5 %copy-start.5 = (f32[128,128]{1,0:T(8,128)S(1)}, f32[128,128]{1,0:T(8,128)}, u32[]{:S(2)}) copy-start(f32[128,128]{1,0:T(8,128)} %constant.102.clone.eye_ref) | copy-start | bytes 196612
  93.2 6.4 %collective-permute-start.14 = (bf16[128,768]{1,0:T(8,128)(2,1)S(1)}, bf16[128,768]{1,0:T(8,128)(2,1)S(1)}, u32[]{:S(2)}, u32[]{:S(2)}) collective-permute-start(bf16[128,768]{1,0:T(8,128)(2,1)S(1)} %get-tuple-element.19.own_ref), channel_id=1, source_target_pairs={{0,1},{1,0},{2,3},{3,2},{4,5},{5,4},{6,7},{7,6},{8,9},{9,8},{10,11... | collective-permute-start | bytes 589832 | tf_op jit(solution)/shard_map/ppermute | solution.py:472
  99.6 7.5 %copy-start.11 = (f32[128,128]{1,0:T(8,128)S(1)}, f32[128,128]{1,0:T(8,128)}, u32[]{:S(2)}) copy-start(f32[128,128]{1,0:T(8,128)} %constant.109.clone.cumulative_ref) | copy-start | bytes 196612
  99.6 7.5 %copy-start.12 = (f32[128,128]{1,0:T(8,128)S(1)}, f32[128,128]{1,0:T(8,128)}, u32[]{:S(2)}) copy-start(f32[128,128]{1,0:T(8,128)} %constant.110.clone.carried_ref) | copy-start | bytes 196612
  101.3 5.8 %collective-permute-start.15 = (bf16[128,768]{1,0:T(8,128)(2,1)S(1)}, bf16[128,768]{1,0:T(8,128)(2,1)S(1)}, u32[]{:S(2)}, u32[]{:S(2)}) collective-permute-start(bf16[128,768]{1,0:T(8,128)(2,1)S(1)} %get-tuple-element.21), channel_id=1, source_target_pairs={{0,1},{1,0},{2,3},{3,2},{4,5},{5,4},{6,7},{7,6},{8,9},{9,8},{10,11... | collective-permute-start | bytes 589832 | tf_op jit(solution)/shard_map/ppermute | solution.py:477
  103.0 4.1 %collective-permute-start.16 = (f32[1,128]{1,0:T(1,128)S(1)}, f32[1,128]{1,0:T(1,128)S(1)}, u32[]{:S(2)}, u32[]{:S(2)}) collective-permute-start(f32[1,128]{1,0:T(1,128)S(1)} %get-tuple-element.22.own_head_ref), channel_id=1, source_target_pairs={{0,1},{1,0},{2,3},{3,2},{4,5},{5,4},{6,7},{7,6},{8,9},{9,8},{10,11... | collective-permute-start | bytes 1544 | tf_op jit(solution)/shard_map/ppermute | solution.py:478
Sparse Core Ops, SparseCore 0:
  10.4 69.2 all-gather.3

commit v3 on v0

--- a/solution.py
+++ b/solution.py
@@ -1,8 +1,11 @@
 import math
+import functools
 
 import jax
 import jax.numpy as jnp
 from jax import lax
+from jax.experimental import pallas as pl
+from jax.experimental.pallas import tpu as pltpu
 from jax.sharding import PartitionSpec as P
 
 HDIM = 64
@@ -63,7 +66,7 @@
     return attend(trio[0], trio[1], trio[2])
 
 
-def body(
+def general_body(
     tokens,
     cross_qkv,
     cross_out,
@@ -162,7 +165,398 @@
     return (features, geotime)
 
 
+F32 = jnp.float32
+BF16 = jnp.bfloat16
+VMEM = pl.BlockSpec(memory_space=pltpu.VMEM)
+SMEM = pl.BlockSpec(memory_space=pltpu.SMEM)
+NT = (((1,), (1,)), ((), ()))
+NEG = -1e30
+
+
+def call(kernel, outs, in_specs, scratch=(), us=1, vmem=40):
+    return pl.pallas_call(
+        kernel,
+        out_shape=outs,
+        in_specs=in_specs,
+        out_specs=jax.tree.map(lambda _: VMEM, outs),
+        scratch_shapes=list(scratch),
+        compiler_params=pltpu.CompilerParams(vmem_limit_bytes=vmem * 2**20),
+        cost_estimate=pl.CostEstimate(
+            flops=us * 10**9, bytes_accessed=us * 3 * 10**6, transcendentals=0
+        ),
+    )
+
+
+class Plan:
+    def __init__(self, inlines, cross_dev, depth_dev):
+        self.rows = inlines * cross_dev * depth_dev
+        self.cross_dev, self.depth_dev = cross_dev, depth_dev
+
+    def inline(self, row):
+        return row // (self.cross_dev * self.depth_dev)
+
+    def depth(self, row):
+        return row // self.cross_dev % self.depth_dev
+
+    def cross(self, row):
+        return row % self.cross_dev
+
+    def column(self, row):
+        return self.inline(row) * self.cross_dev + self.cross(row)
+
+    def natural(self, row):
+        return self.column(row) * self.depth_dev + self.depth(row)
+
+
+def down(n, of=lambda row: row):
+    return of(lax.broadcasted_iota(jnp.int32, (n, 1), 0))
+
+
+def along(n, of=lambda row: row):
+    return of(lax.broadcasted_iota(jnp.int32, (1, n), 1))
+
+
+def one_where(mask, dtype=F32):
+    return jnp.where(mask, 1.0, 0.0).astype(dtype)
+
+
+def bias_where(mask):
+    return jnp.where(mask, 0.0, NEG)
+
+
+def rms(stream, gain):
+    scale = lax.rsqrt(jnp.mean(stream * stream, -1, keepdims=True) + 1e-05)
+    return (stream * scale * gain).astype(BF16)
+
+
+def as_column(row):
+    n = row.shape[1]
+    return jnp.sum(jnp.where(down(n) == along(n), row, 0.0), axis=1, keepdims=True)
+
+
+def as_row(column):
+    n = column.shape[0]
+    return jnp.sum(jnp.where(down(n) == along(n), column, 0.0), axis=0, keepdims=True)
+
+
+def softplus(value):
+    return jnp.maximum(value, 0.0) + jnp.log1p(jnp.exp(-jnp.abs(value)))
+
+
+def encode_kernel(
+    tokens_ref, encoding_ref, gains_ref, head_ref, stream_ref, normed_ref, out_gains_ref, out_head_ref, *, plan
+):
+    n = plan.rows
+    to_rows = one_where(down(n, plan.natural) == along(n), BF16)
+    rows = jnp.dot(to_rows, tokens_ref[...], preferred_element_type=F32)
+    stream = rows + encoding_ref[...]
+    stream_ref[...] = stream
+    normed_ref[...] = rms(stream, gains_ref[0:1])
+    out_gains_ref[...] = gains_ref[...]
+    out_head_ref[...] = head_ref[...]
+
+
+def attend_heads(queries, keys, values, bias, heads):
+    lane = lax.broadcasted_iota(jnp.int32, (queries.shape[0], 128), 1)
+    ones = jnp.ones((keys.shape[0], 128), BF16)
+    outs = []
+    for at in range(0, heads * HDIM, 128):
+        at = slice(at, at + 128)
+        wide = jnp.concatenate([values[:, at], ones], axis=1)
+        pair = []
+        for own in (lane < HDIM, lane >= HDIM)[: heads - at.start // HDIM]:
+            masked = jnp.where(own, queries[:, at], jnp.zeros_like(queries[:, at]))
+            scores = lax.dot_general(masked, keys[:, at], NT, preferred_element_type=F32) + bias
+            expo = jnp.exp(scores - jnp.max(scores, -1, keepdims=True)).astype(BF16)
+            mixed = jnp.dot(expo, wide, preferred_element_type=F32)
+            pair.append(mixed[:, :128] / mixed[:, 128:])
+        outs.append(jnp.where(lane < HDIM, pair[0], pair[-1]))
+    return jnp.concatenate(outs, axis=1)
+
+
+def project(normed, weights):
+    return lax.dot_general(normed, weights, NT, preferred_element_type=F32).astype(BF16)
+
+
+def assemble(place_ref, piece_refs, first_plane, held_ref, row, rows):
+    y, c, x = place_ref[0], place_ref[1], place_ref[2]
+    for n, piece_ref in enumerate(piece_refs):
+        at_c = c if n < 4 else 1 - c
+        flip_x, flip_y = ((0, 0), (1 - at_c, at_c), (at_c, 1 - at_c), (1, 1))[n % 4]
+        at_x, at_y = x + flip_x - 2 * x * flip_x, y + flip_y - 2 * y * flip_y
+        planes, _, lanes = piece_ref.shape
+        at_lane = pl.multiple_of(at_x * lanes, 128)
+        for plane in range(planes):
+            z = place_ref[3 + first_plane + plane]
+            at_row = pl.multiple_of((z * 4 + at_y * 2 + at_c) * rows, 16)
+            held_ref[pl.ds(at_row, rows), pl.ds(at_lane, lanes)] = piece_ref[plane, row : row + rows]
+
+
+def assemble_both(place_ref, near_refs, far_refs, held_ref, row, rows):
+    assemble(place_ref, near_refs, 0, held_ref, row, rows)
+    assemble(place_ref, far_refs, 2, held_ref, row, rows)
+
+
+def cross_kernel(*refs, plan, rows):
+    place_ref, normed_ref = refs[:2]
+    piece_refs, (mixed_ref, held_ref) = refs[2:10], refs[10:]
+    width = normed_ref.shape[1]
+    assemble(place_ref, piece_refs, 0, held_ref, 0, rows)
+    normed = normed_ref[...]
+    q = project(normed, held_ref[:width]) * BF16(HDIM**-0.5)
+    k = project(normed, held_ref[width : 2 * width])
+    v = project(normed, held_ref[2 * width :])
+    n, cross = plan.rows, plan.cross_dev
+    bias = bias_where(down(n) // cross % 2 == along(n) // cross % 2)
+    mixed_ref[...] = attend_heads(q, k, v, bias, width // HDIM).astype(BF16)
+
+
+def cross_out_kernel(*refs, chunk, count):
+    place_ref, mixed_ref, stream_ref, gains_ref = refs[:4]
+    near_refs, far_refs, (out_ref, normed_ref, held_ref) = refs[4:12], refs[12:20], refs[20:]
+    assemble_both(place_ref, near_refs, far_refs, held_ref, chunk, count)
+    stream = stream_ref[...] + jnp.dot(mixed_ref[...], held_ref[...], preferred_element_type=F32)
+    out_ref[...] = stream
+    normed_ref[...] = rms(stream, gains_ref[1:2])
+
+
+def depth_kernel(*refs, plan, chunk, count):
+    place_ref, own_ref, peer_ref, stream_ref, gains_ref = refs[:5]
+    near_refs, far_refs = refs[5:13], refs[13:21]
+    out_ref, normed_ref, held_ref, out_held_ref = refs[21:]
+    width = own_ref.shape[1]
+    assemble_both(place_ref, near_refs, far_refs, held_ref, 0, chunk)
+    assemble_both(place_ref, near_refs, far_refs, out_held_ref, chunk + count, count)
+    own = own_ref[...]
+    both = jnp.concatenate([own, peer_ref[...]], axis=0)
+    q = project(own, held_ref[:width]) * BF16(HDIM**-0.5)
+    k = project(both, held_ref[width : 2 * width])
+    v = project(both, held_ref[2 * width :])
+    n = plan.rows
+    columns = along(2 * n, lambda row: plan.column(row % n))
+    bias = bias_where(down(n, plan.column) == columns)
+    mixed = attend_heads(q, k, v, bias, width // HDIM).astype(BF16)
+    stream = stream_ref[...] + jnp.dot(mixed, out_held_ref[...], preferred_element_type=F32)
+    out_ref[...] = stream
+    normed_ref[...] = rms(stream, gains_ref[2:3])
+
+
+def shift(a, step, peers):
+    return lax.ppermute(a, "gx", [(i, i ^ step) for i in range(peers)])
+
+
+def swap_x(a):
+    return lax.ppermute(a, "gz", [(0, 1), (1, 0)])
+
+
+def lane_half(shard):
+    lanes = shard.shape[1] // 2
+    return lax.dynamic_slice_in_dim(shard, lax.axis_index("gz") * lanes, lanes, axis=1)
+
+
+def stack_kernel(*refs):
+    for n, ref in enumerate(refs[:-1]):
+        refs[-1][n] = ref[...]
+
+
+def stack(*pieces, us=1):
+    first = pieces[0]
+    return call(
+        stack_kernel,
+        jax.ShapeDtypeStruct((len(pieces), *first.shape), first.dtype),
+        [VMEM] * len(pieces),
+        us=us,
+        vmem=8,
+    )(*pieces)
+
+
+def after(value, *others):
+    return lax.optimization_barrier((value, *others))[0]
+
+
+def mlp_kernel(
+    own_ref, peer_ref, stream_ref, up_ref, down_ref, head_ref,
+    own_part_ref, peer_part_ref, own_head_ref, peer_head_ref,
+):
+    rows = own_ref.shape[0]
+    both = jnp.concatenate([own_ref[...], peer_ref[...]], axis=0)
+    hidden = jnp.dot(both, up_ref[...], preferred_element_type=F32)
+    hidden = jax.nn.gelu(hidden).astype(BF16)
+    part = jnp.dot(hidden, down_ref[...], preferred_element_type=F32).astype(BF16)
+    own_part_ref[...] = part[:rows]
+    peer_part_ref[...] = part[rows:]
+    head = head_ref[...]
+    own = jnp.sum((stream_ref[...] + part[:rows].astype(F32)) * head, axis=1, keepdims=True)
+    peer = jnp.sum(part[rows:].astype(F32) * head, axis=1, keepdims=True)
+    own_head_ref[...] = as_row(own)
+    peer_head_ref[...] = as_row(peer)
+
+
+def final_kernel(
+    stream_ref, own_ref, got_ref, own_head_ref, got_head_ref, peer_head_ref, head_ref, bias_ref, later_ref,
+    features_ref, time_ref, *, plan,
+):
+    n = plan.rows
+    got = got_ref[...].astype(F32)
+    stream = stream_ref[...] + own_ref[...].astype(F32) + got
+    from_rows = one_where(down(n) == along(n, plan.natural), BF16)
+    features_ref[...] = jnp.dot(
+        from_rows, stream.astype(BF16), preferred_element_type=F32
+    ).astype(BF16)
+    bias = bias_ref[0]
+    own = as_column(own_head_ref[...]) + jnp.sum(got * head_ref[...], axis=1, keepdims=True)
+    own = softplus(own + bias)
+    before = softplus(as_column(got_head_ref[...] + peer_head_ref[...]) + bias) * later_ref[0]
+    inlines, cross_dev, depth_dev = time_ref.shape
+    on_line = one_where(down(inlines * cross_dev) == along(n, plan.column))
+    reached = jnp.where(down(n, plan.depth) <= along(depth_dev), own, 0.0)
+    times = jnp.dot(
+        on_line, reached + before, precision=lax.Precision.HIGHEST, preferred_element_type=F32
+    )
+    for inline in range(inlines):
+        time_ref[inline] = times[inline * cross_dev : (inline + 1) * cross_dev]
+
+
+def fast_body(
+    tokens, cross_qkv, cross_out, depth_qkv, depth_out,
+    up_proj, down_proj, gains, head_weight, head_bias,
+):
+    inlines, cross_dev, depth_dev, width = tokens.shape
+    peers = lax.axis_size("gx")
+    plan = Plan(inlines, cross_dev, depth_dev)
+    rows = plan.rows
+    chunk, count = cross_qkv.shape[1], cross_out.shape[0]
+    shape = jax.ShapeDtypeStruct
+    wide, narrow = shape((rows, width), F32), shape((rows, width), BF16)
+    row = shape((1, rows), F32)
+
+    def to(a, step, name):
+        with jax.named_scope(name):
+            return shift(a, step, peers)
+
+    def to_x(a, name):
+        with jax.named_scope(name):
+            return swap_x(a)
+
+    with jax.named_scope("encoding"):
+        index = jnp.arange(rows)
+        pairs = width // 2
+        feature = jnp.arange(width)
+        pair = feature // 2
+        freq = math.pi * jnp.exp(-log_span * pair.astype(F32) / pairs)
+        which = pair % 3
+        at_cross = plan.cross(index) + lax.axis_index("gx") * cross_dev
+        at_depth = plan.depth(index) + lax.axis_index("gz") * depth_dev
+        position = jnp.where(
+            which == 0,
+            plan.inline(index)[:, None],
+            jnp.where(which == 1, at_cross[:, None], at_depth[:, None]),
+        )
+        angle = position.astype(F32) * freq
+        encoding = jnp.where(feature % 2 == 0, jnp.sin(angle), jnp.cos(angle))
+
+    gx, x = lax.axis_index("gx"), lax.axis_index("gz")
+    z, y, c = gx // 4, gx // 2 % 2, gx % 2
+    planes = [z, z ^ 1, z ^ 2, z ^ 3]
+
+    def cross_over(a, turn, name):
+        pairs = []
+        for device in range(2 * peers):
+            of_core = device // 2 % 2
+            pairs.append((device, device ^ (1 if of_core == turn else 4)))
+        with jax.named_scope(name):
+            return lax.ppermute(a, ("gx", "gz"), pairs)
+
+    first_half = lane_half(cross_qkv.T)
+    half = lane_half(jnp.concatenate([depth_qkv.T, cross_out, depth_out], axis=0))
+    pieces = first_half, to(first_half, 4, "cross_z1"), to(first_half, 8, "cross_z2"), to(first_half, 12, "cross_z3")
+    near = to(half, 4, "rest_z1")
+    stream, normed, gains, head = call(
+        functools.partial(encode_kernel, plan=plan),
+        (wide, narrow, shape(gains.shape, F32), shape((1, width), F32)),
+        [VMEM] * 4,
+    )(tokens.reshape(rows, width), encoding, gains, head_weight.reshape(1, width))
+
+    pieces, near, half, normed = lax.optimization_barrier((pieces, near, half, normed))
+    far = to(half, 8, "rest_z2"), to(half, 12, "rest_z3")
+    pieces = stack(*pieces)
+    pieces_1, pieces_2 = cross_over(pieces, 0, "cross_1"), cross_over(pieces, 1, "cross_2")
+    near = stack(half, near)
+    near_1, near_2 = cross_over(near, 0, "near_1"), cross_over(near, 1, "near_2")
+    lined = lax.all_to_all(
+        normed.reshape(peers, rows // peers, width), "gx", split_axis=0, concat_axis=0, tiled=True
+    ).reshape(rows, width)
+
+    pieces, pieces_1, pieces_2, near, near_1, near_2, far, lined = lax.optimization_barrier(
+        (pieces, pieces_1, pieces_2, near, near_1, near_2, far, lined)
+    )
+    pieces_3 = cross_over(pieces_1, 1, "cross_3")
+    cross_pieces = [to(piece, 1, "cross_core") for piece in (pieces, pieces_1, pieces_2)]
+
+    pieces, pieces_1, pieces_2, pieces_3, cross_pieces, near, near_1, near_2, far, lined = lax.optimization_barrier(
+        (pieces, pieces_1, pieces_2, pieces_3, cross_pieces, near, near_1, near_2, far, lined)
+    )
+    cross_pieces = [pieces, pieces_1, pieces_2, pieces_3, *cross_pieces, to(pieces_3, 1, "cross_core")]
+    near_3 = cross_over(near_1, 1, "near_3")
+    far = stack(*far)
+    far_1, far_2 = cross_over(far, 0, "far_1"), cross_over(far, 1, "far_2")
+    near_pieces = [near, near_1, near_2, near_3]
+    near_pieces += [to(piece, 1, "near_core") for piece in near_pieces]
+    place = jnp.stack([y, c, x] + planes).astype(jnp.int32)
+    mixed = call(
+        functools.partial(cross_kernel, plan=plan, rows=chunk),
+        narrow,
+        [SMEM] + [VMEM] * 9,
+        [pltpu.VMEM((3 * width, width), BF16)],
+        us=30,
+    )(place, lined, *cross_pieces)
+    attended = mixed
+    mixed = lax.all_to_all(
+        mixed.reshape(peers, rows // peers, width), "gx", split_axis=0, concat_axis=0, tiled=True
+    ).reshape(rows, width)
+    far_3 = cross_over(after(far_1, far_2, attended), 1, "far_3")
+    far_pieces = [far, far_1, far_2, after(far_3, mixed)]
+    far_pieces += [to(piece, 1, "far_core") for piece in far_pieces]
+    stream, normed = call(
+        functools.partial(cross_out_kernel, chunk=chunk, count=count),
+        (wide, narrow),
+        [SMEM] + [VMEM] * 19,
+        [pltpu.VMEM((width, width), BF16)],
+        us=2,
+    )(place, mixed, stream, gains, *near_pieces, *far_pieces)
+    peer = to_x(normed, "normed2_x")
+    stream, normed = call(
+        functools.partial(depth_kernel, plan=plan, chunk=chunk, count=count),
+        (wide, narrow),
+        [SMEM] + [VMEM] * 20,
+        [pltpu.VMEM((3 * width, width), BF16), pltpu.VMEM((width, width), BF16)],
+    )(place, normed, peer, stream, gains, *near_pieces, *far_pieces)
+    peer = to_x(normed, "normed3_x")
+    own_part, peer_part, own_head, peer_head = call(
+        mlp_kernel, (narrow, narrow, row, row), [VMEM] * 6
+    )(normed, peer, stream, up_proj, down_proj, head)
+    got_part, got_head = to_x(peer_part, "part_x"), to_x(own_head, "head_x")
+    later = (lax.axis_index("gz") > 0).astype(F32).reshape(1)
+    features, geotime = call(
+        functools.partial(final_kernel, plan=plan),
+        (narrow, shape(tokens.shape[:3], F32)),
+        [VMEM] * 7 + [SMEM, SMEM],
+    )(stream, own_part, got_part, own_head, got_head, peer_head, head, head_bias, later)
+    return features.reshape(tokens.shape), geotime
+
+
 def solution(mesh):
+    def body(*args):
+        tokens = args[0]
+        inlines, cross_dev, depth_dev, width = tokens.shape
+        peers = mesh.shape["gx"]
+        fits = (
+            (peers, mesh.shape["gz"]) == (16, 2)
+            and (inlines, cross_dev, depth_dev) == (4, 4, 8)
+            and width == 12 * HDIM
+        )
+        return (fast_body if fits else general_body)(*args)
+
     return jax.shard_map(
         body,
         mesh=mesh,

time: 233 us -> 115 us (0.49)
  waiting for transfers between devices: 95.2 us -> 43.5 us
  blocking collectives: 34.4 us -> 0 us
  local copies, waits for them, and re-layouts: 40.3 us -> 10.8 us
  matrix products: 26.3 us -> 0 us
  starting transfers between devices: 15.8 us -> 40.9 us
  Pallas kernels: 0 us -> 14.7 us
  between operations: 14.8 us -> 1.51 us
    all_gather x4 -> x0, waiting for transfers between devices: 53.4 us -> none  [the longest x1 38.8 us: body(): lax.all_gather(cross_qkv, 'gx', axis=1, tiled=True)]
    ppermute x0 -> x31, waiting for transfers between devices: none -> 37.2 us  [the longest x18 14.7 us: shift(): return lax.ppermute(a, 'gx', [(i, i ^ step) for i in range(peers)])]
    all_gather x4 -> x0, blocking collectives: 34.4 us -> none  [the longest x1 11.9 us: body(): lax.all_gather(lined[1], 'gz', axis=3, tiled=True)]
    ppermute x0 -> x31, starting transfers between devices: none -> 30.4 us  [the longest x18 13.4 us: shift(): return lax.ppermute(a, 'gx', [(i, i ^ step) for i in range(peers)])]
    dot_general x10 -> x0, matrix products: 24.2 us -> none  [the longest x2 6.33 us: attend(): jnp.einsum('...qk,...ke->...qe', weights, values, preferred_element_type=...]
    all_to_all x4 -> x2, waiting for transfers between devices: 27.7 us -> 6.36 us  [the longest x1 6.35 us: fast_body(): lax.all_to_all(mixed.reshape(peers, rows // peers, width), 'gx', split_ax...]
    pallas_call x0 -> x9, Pallas kernels: none -> 14.7 us  [the longest x1 4.58 us: fast_body(): call(functools.partial(cross_kernel, plan=plan, rows=chunk), narrow, [SME...]
    reshape x7 -> x1, local copies, waits for them, and re-layouts: 12.6 us -> 0.69 us  [fast_body(): head_weight.reshape(1, width)]
  transfers between devices with their start and end apart: 9 -> 33, of which waited for: 7 -> 16; matrix products, arithmetic and copies ran while one was open for 26% -> 3% of each run, Pallas kernels for 0% -> 5%
where the time goes in v3:
time: 115 us; the launch traced here: 114 us
  waiting for transfers between devices  43.5 us (38%)
  starting transfers between devices  40.9 us (36%)
  Pallas kernels  14.7 us (13%)
  local copies, waits for them, and re-layouts  10.8 us (9%)
  other arithmetic  2.5 us (2%)
  between operations  1.51 us (1%)
    ppermute x18, waiting for transfers between devices, shift(): return lax.ppermute(a, 'gx', [(i, i ^ step) for i in range(peers)])  14.7 us
    ppermute x4, waiting for transfers between devices, swap_x(): return lax.ppermute(a, 'gz', [(0, 1), (1, 0)])  13.5 us
    ppermute x18, starting transfers between devices, shift(): return lax.ppermute(a, 'gx', [(i, i ^ step) for i in range(peers)])  13.4 us
    ppermute x9, starting transfers between devices, cross_over(): return lax.ppermute(a, ('gx', 'gz'), pairs)  12.2 us
    unnamed x42, local copies, waits for them, and re-layouts  10 us
    ppermute x9, waiting for transfers between devices, cross_over(): return lax.ppermute(a, ('gx', 'gz'), pairs)  8.97 us
    all_to_all x1, waiting for transfers between devices, fast_body(): lax.all_to_all(mixed.reshape(peers, rows // peers, width), 'gx', split_ax...  6.35 us
    all_to_all x1, starting transfers between devices, fast_body(): lax.all_to_all(mixed.reshape(peers, rows // peers, width), 'gx', split_ax...  6.23 us
  transfers between devices with their start and end apart: 33, of which 16 were waited for; matrix products, arithmetic and copies ran while one was open for 3% of the time, Pallas kernels for 5%

profile of v3, /device:TPU:0, one launch (start us, length us, event | category | flops | bytes accessed | tf_op | source)
XLA Modules:
  0.0 113.9 jit_solution(17521927599153623490)
XLA Ops:
  0.6 0.0 copy-start
  0.6 0.9 copy-done
  1.6 3.1 %collective-permute-start = (bf16[144,384]{1,0:T(8,128)(2,1)S(1)}, bf16[144,384]{1,0:T(8,128)(2,1)S(1)}, u32[]{:S(2)}, u32[]{:S(2)}) collective-permute-start(bf16[144,384]{1,0:T(8,128)(2,1)S(1)} %dynamic-slice_bitcast_fusion.refs_0_), channel_id=1, source_target_pairs={{0,8},{2,10},{4,12},{6,14},{8,0},{10,2},{12,4},{14,6},{16,24},{18,... | collective-permute-start | bytes 331784 | tf_op jit(solution)/shard_map/cross_z1/ppermute | solution.py:345
  4.7 2.6 %collective-permute-start.1 = (bf16[144,384]{1,0:T(8,128)(2,1)S(1)}, bf16[144,384]{1,0:T(8,128)(2,1)S(1)}, u32[]{:S(2)}, u32[]{:S(2)}) collective-permute-start(bf16[144,384]{1,0:T(8,128)(2,1)S(1)} %dynamic-slice_bitcast_fusion.refs_0_), channel_id=1, source_target_pairs={{0,16},{2,18},{4,20},{6,22},{8,24},{10,26},{12,28},{14,30},{16,0},... | collective-permute-start | bytes 331784 | tf_op jit(solution)/shard_map/cross_z2/ppermute | solution.py:345
  7.3 0.9 fusion.1.refs_0_
  8.2 1.0 collective-permute-start.3
  9.2 1.5 %cosine_select_fusion.encoding_ref = f32[128,768]{1,0:T(8,128)S(1)} fusion(f32[768]{0:T(1024)S(1)} %fusion.10, s32[128]{0:T(128)S(1)} %fusion.17, s32[128]{0:T(128)S(1)} %get-tuple-element.93, s32[128]{0:T(128)S(1)} %get-tuple-element.92, pred[768]{0:T(1024)(128)(4,1)S(1)} %broadcast_compare_fusion.1, pred[768]{0:T(1024)(128)(4,1)S(1)} %get-tuple-element.95, ...), kind=kLoop, calls=%fused_computation | loop fusion | flops 491520 | bytes 400128 | tf_op jit(solution)/shard_map/encoding/jit(_where)/select_n | solution.py:456
  10.8 0.7 reshape.94.head_ref
  11.5 0.9 copy-done.15
  12.4 0.7 copy-done.18
  13.1 1.0 shard_map.113
  14.1 2.0 %collective-permute-done.1.refs_2_ = bf16[144,384]{1,0:T(8,128)(2,1)S(1)} collective-permute-done((bf16[144,384]{1,0:T(8,128)(2,1)S(1)}, bf16[144,384]{1,0:T(8,128)(2,1)S(1)}, u32[]{:S(2)}, u32[]{:S(2)}) %collective-permute-start.1) | collective-permute-done | bytes 110624 | tf_op jit(solution)/shard_map/cross_z2/ppermute | solution.py:345
  16.0 1.4 %collective-permute-done.3.refs_1_ = bf16[240,384]{1,0:T(8,128)(2,1)S(1)} collective-permute-done((bf16[240,384]{1,0:T(8,128)(2,1)S(1)}, bf16[240,384]{1,0:T(8,128)(2,1)S(1)}, u32[]{:S(2)}, u32[]{:S(2)}) %collective-permute-start.3) | collective-permute-done | bytes 184352 | tf_op jit(solution)/shard_map/rest_z1/ppermute | solution.py:345
  17.5 1.6 %collective-permute-start.4 = (bf16[4,144,384]{2,1,0:T(8,128)(2,1)S(1)}, bf16[4,144,384]{2,1,0:T(8,128)(2,1)S(1)}, u32[]{:S(2)}, u32[]{:S(2)}) collective-permute-start(bf16[4,144,384]{2,1,0:T(8,128)(2,1)S(1)} %shard_map.114.refs_2_), channel_id=1, source_target_pairs={{0,1},{1,0},{2,6},{3,7},{4,5},{5,4},{6,2},{7,3},{8,9},{9,8},{10,14... | collective-permute-start | bytes 1327112 | tf_op jit(solution)/shard_map/cross_1/ppermute | solution.py:468
  19.0 1.5 %collective-permute-start.5 = (bf16[4,144,384]{2,1,0:T(8,128)(2,1)S(1)}, bf16[4,144,384]{2,1,0:T(8,128)(2,1)S(1)}, u32[]{:S(2)}, u32[]{:S(2)}) collective-permute-start(bf16[4,144,384]{2,1,0:T(8,128)(2,1)S(1)} %shard_map.114.refs_2_), channel_id=1, source_target_pairs={{0,4},{1,5},{2,3},{3,2},{4,0},{5,1},{6,7},{7,6},{8,12},{9,13},{10,... | collective-permute-start | bytes 1327112 | tf_op jit(solution)/shard_map/cross_2/ppermute | solution.py:468
  20.5 1.8 %collective-permute-start.8 = (bf16[240,384]{1,0:T(8,128)(2,1)S(1)}, bf16[240,384]{1,0:T(8,128)(2,1)S(1)}, u32[]{:S(2)}, u32[]{:S(2)}) collective-permute-start(bf16[240,384]{1,0:T(8,128)(2,1)S(1)} %fusion.1.refs_0_), channel_id=1, source_target_pairs={{0,16},{2,18},{4,20},{6,22},{8,24},{10,26},{12,28},{14,30},{16,0},... | collective-permute-start | bytes 552968 | tf_op jit(solution)/shard_map/rest_z2/ppermute | solution.py:345
  22.4 0.6 collective-permute-start.6
  23.0 0.5 collective-permute-start.7
  23.5 4.2 %all-to-all-start = ((bf16[16,8,768]{2,1,0:T(8,128)(2,1)}), bf16[16,8,768]{2,1,0:T(8,128)(2,1)S(1)}, u32[]{:S(2)}, u32[]{:S(2)}) async-start(bf16[16,8,768]{2,1,0:T(8,128)(2,1)} %bitcast.10), calls=%async_computation | async-start | bytes 393216 | tf_op jit(solution)/shard_map/all_to_all | solution.py:486
  27.8 2.4 %collective-permute-done.8.refs_0_ = bf16[240,384]{1,0:T(8,128)(2,1)S(1)} collective-permute-done((bf16[240,384]{1,0:T(8,128)(2,1)S(1)}, bf16[240,384]{1,0:T(8,128)(2,1)S(1)}, u32[]{:S(2)}, u32[]{:S(2)}) %collective-permute-start.8) | collective-permute-done | bytes 184352 | tf_op jit(solution)/shard_map/rest_z2/ppermute | solution.py:345
  30.2 2.9 %collective-permute-start.9 = (bf16[240,384]{1,0:T(8,128)(2,1)S(1)}, bf16[240,384]{1,0:T(8,128)(2,1)S(1)}, u32[]{:S(2)}, u32[]{:S(2)}) collective-permute-start(bf16[240,384]{1,0:T(8,128)(2,1)S(1)} %fusion.1.refs_0_), channel_id=1, source_target_pairs={{0,24},{2,26},{4,28},{6,30},{8,16},{10,18},{12,20},{14,22},{16,8},... | collective-permute-start | bytes 552968 | tf_op jit(solution)/shard_map/rest_z3/ppermute | solution.py:345
  33.0 6.8 %collective-permute-done.9.refs_1_ = bf16[240,384]{1,0:T(8,128)(2,1)S(1)} collective-permute-done((bf16[240,384]{1,0:T(8,128)(2,1)S(1)}, bf16[240,384]{1,0:T(8,128)(2,1)S(1)}, u32[]{:S(2)}, u32[]{:S(2)}) %collective-permute-start.9) | collective-permute-done | bytes 184352 | tf_op jit(solution)/shard_map/rest_z3/ppermute | solution.py:345
  39.8 0.7 copy-done.16
  40.5 1.5 %collective-permute-start.10 = (bf16[4,144,384]{2,1,0:T(8,128)(2,1)S(1)}, bf16[4,144,384]{2,1,0:T(8,128)(2,1)}, u32[]{:S(2)}, u32[]{:S(2)}) collective-permute-start(bf16[4,144,384]{2,1,0:T(8,128)(2,1)S(1)} %collective-permute-done.4.refs_3_), channel_id=1, source_target_pairs={{0,4},{1,5},{2,3},{3,2},{4,0},{5,1},{6,7},{7,6},{8,12},{9,13},{10,... | collective-permute-start | bytes 1327112 | tf_op jit(solution)/shard_map/cross_3/ppermute | solution.py:468
  42.1 0.8 copy-done.5
  42.8 0.5 collective-permute-start.11
  43.3 0.8 copy-done.7
  44.1 4.9 %collective-permute-done.10.refs_5_ = bf16[4,144,384]{2,1,0:T(8,128)(2,1)} collective-permute-done((bf16[4,144,384]{2,1,0:T(8,128)(2,1)S(1)}, bf16[4,144,384]{2,1,0:T(8,128)(2,1)}, u32[]{:S(2)}, u32[]{:S(2)}) %collective-permute-start.10) | collective-permute-done | bytes 442400 | tf_op jit(solution)/shard_map/cross_3/ppermute | solution.py:468
  49.0 0.8 copy-done.11
  49.8 0.8 copy-done.9
  50.5 0.8 copy-done.13
  51.3 0.1 stack.31.refs_0_
  51.4 0.9 copy-done.17
  52.4 1.6 %collective-permute-start.20 = (bf16[2,240,384]{2,1,0:T(8,128)(2,1)S(1)}, bf16[2,240,384]{2,1,0:T(8,128)(2,1)S(1)}, u32[]{:S(2)}, u32[]{:S(2)}) collective-permute-start(bf16[2,240,384]{2,1,0:T(8,128)(2,1)S(1)} %shard_map.117.refs_12_.refs_13_), channel_id=1, source_target_pairs={{0,1},{1,0},{2,6},{3,7},{4,5},{5,4},{6,2},{7,3},{8,9},{9,8},{10,14... | collective-permute-start | bytes 1105928 | tf_op jit(solution)/shard_map/far_1/ppermute | solution.py:468
  53.9 1.5 %collective-permute-start.21 = (bf16[2,240,384]{2,1,0:T(8,128)(2,1)S(1)}, bf16[2,240,384]{2,1,0:T(8,128)(2,1)S(1)}, u32[]{:S(2)}, u32[]{:S(2)}) collective-permute-start(bf16[2,240,384]{2,1,0:T(8,128)(2,1)S(1)} %shard_map.117.refs_12_.refs_13_), channel_id=1, source_target_pairs={{0,4},{1,5},{2,3},{3,2},{4,0},{5,1},{6,7},{7,6},{8,12},{9,13},{10,... | collective-permute-start | bytes 1105928 | tf_op jit(solution)/shard_map/far_2/ppermute | solution.py:468
  55.4 4.6 %shard_map.116 = bf16[128,768]{1,0:T(8,128)(2,1)} custom-call(s32[7]{0:T(128)S(1)} %stack.31.refs_0_, bf16[128,768]{1,0:T(8,128)(2,1)S(1)} %bitcast.17, bf16[4,144,384]{2,1,0:T(8,128)(2,1)S(1)} %shard_map.114.refs_2_, bf16[4,144,384]{2,1,0:T(8,128)(2,1)S(1)} %copy-done.6, bf16[4,144,384]{2,1,0:T(8,128)(2,1)S(1)} %copy-done.8, ...), custom_call_target="tpu_custom_call" | custom-call | flops 30000001024 | bytes 90000000 | tf_op jit(solution)/shard_map/pallas_call | solution.py:506
  60.0 3.2 %collective-permute-done.20.refs_13_.refs_14_ = bf16[2,240,384]{2,1,0:T(8,128)(2,1)S(1)} collective-permute-done((bf16[2,240,384]{2,1,0:T(8,128)(2,1)S(1)}, bf16[2,240,384]{2,1,0:T(8,128)(2,1)S(1)}, u32[]{:S(2)}, u32[]{:S(2)}) %collective-permute-start.20) | collective-permute-done | bytes 368672 | tf_op jit(solution)/shard_map/far_1/ppermute | solution.py:468
  63.2 0.2 collective-permute-done.21.refs_14_.refs_15_
  63.4 1.8 %collective-permute-start.22 = (bf16[2,240,384]{2,1,0:T(8,128)(2,1)S(1)}, bf16[2,240,384]{2,1,0:T(8,128)(2,1)S(1)}, u32[]{:S(2)}, u32[]{:S(2)}) collective-permute-start(bf16[2,240,384]{2,1,0:T(8,128)(2,1)S(1)} %collective-permute-done.20.refs_13_.refs_14_), channel_id=1, source_target_pairs={{0,4},{1,5},{2,3},{3,2},{4,0},{5,1},{6,7},{7,6},{8,12},{9,13},{10,... | collective-permute-start | bytes 1105928 | tf_op jit(solution)/shard_map/far_3/ppermute | solution.py:468
  65.2 6.2 %all-to-all-start.1 = ((bf16[16,8,768]{2,1,0:T(8,128)(2,1)}), bf16[16,8,768]{2,1,0:T(8,128)(2,1)S(1)}, u32[]{:S(2)}, u32[]{:S(2)}) async-start(bf16[16,8,768]{2,1,0:T(8,128)(2,1)} %bitcast.12), calls=%async_computation.1 | async-start | bytes 393216 | tf_op jit(solution)/shard_map/all_to_all | solution.py:514
  71.4 0.5 collective-permute-start.23
  71.9 1.7 %collective-permute-start.15 = (bf16[2,240,384]{2,1,0:T(8,128)(2,1)S(1)}, bf16[2,240,384]{2,1,0:T(8,128)(2,1)}, u32[]{:S(2)}, u32[]{:S(2)}) collective-permute-start(bf16[2,240,384]{2,1,0:T(8,128)(2,1)S(1)} %collective-permute-done.6.refs_5_.refs_6_), channel_id=1, source_target_pairs={{0,4},{1,5},{2,3},{3,2},{4,0},{5,1},{6,7},{7,6},{8,12},{9,13},{10,... | collective-permute-start | bytes 1105928 | tf_op jit(solution)/shard_map/near_3/ppermute | solution.py:468
  73.6 0.5 collective-permute-start.17
  74.1 6.4 %all-to-all-done.1 = bf16[16,8,768]{2,1,0:T(8,128)(2,1)S(1)} async-done(((bf16[16,8,768]{2,1,0:T(8,128)(2,1)}), bf16[16,8,768]{2,1,0:T(8,128)(2,1)S(1)}, u32[]{:S(2)}, u32[]{:S(2)}) %all-to-all-start.1) | async-done | bytes 196640 | tf_op jit(solution)/shard_map/all_to_all | solution.py:514
  80.5 0.6 collective-permute-done.15.refs_7_.refs_8_
  81.1 0.5 collective-permute-start.19
  81.6 0.1 collective-permute-start.26
  81.7 0.4 collective-permute-done.24.refs_17_.refs_18_
  82.1 1.1 collective-permute-done.25.refs_18_.refs_19_
  83.2 0.4 collective-permute-done.19.refs_11_.refs_12_
  83.6 0.2 collective-permute-done.26.refs_19_.refs_20_
  83.8 1.0 copy-done.20
  84.8 1.9 %shard_map.118 = (f32[128,768]{1,0:T(8,128)S(1)}, bf16[128,768]{1,0:T(8,128)(2,1)S(1)}) custom-call(s32[7]{0:T(128)S(1)} %stack.31.refs_0_, bf16[128,768]{1,0:T(8,128)(2,1)S(1)} %bitcast.18, f32[128,768]{1,0:T(8,128)S(1)} %copy-done.20, f32[3,768]{1,0:T(4,128)S(1)} %get-tuple-element.73.refs_3_.refs_4_, bf16[2,240,384]{2,1,0:T(8,128)(2,1)S(1)} %shard_map.115.refs_4_.refs_5_, ...), custom_call_target="tpu_custom_call" | custom-call | flops 2000000000 | bytes 6000000 | tf_op jit(solution)/shard_map/pallas_call | solution.py:520
  86.8 1.4 %collective-permute-start.27 = (bf16[128,768]{1,0:T(8,128)(2,1)S(1)}, bf16[128,768]{1,0:T(8,128)(2,1)S(1)}, u32[]{:S(2)}, u32[]{:S(2)}) collective-permute-start(bf16[128,768]{1,0:T(8,128)(2,1)S(1)} %get-tuple-element.81.refs_1_), channel_id=1, source_target_pairs={{0,1},{1,0},{2,3},{3,2},{4,5},{5,4},{6,7},{7,6},{8,9},{9,8},{10,11... | collective-permute-start | bytes 589832 | tf_op jit(solution)/shard_map/normed2_x/ppermute | solution.py:349
  88.1 5.6 %collective-permute-done.27.refs_2_ = bf16[128,768]{1,0:T(8,128)(2,1)S(1)} collective-permute-done((bf16[128,768]{1,0:T(8,128)(2,1)S(1)}, bf16[128,768]{1,0:T(8,128)(2,1)S(1)}, u32[]{:S(2)}, u32[]{:S(2)}) %collective-permute-start.27) | collective-permute-done | bytes 196640 | tf_op jit(solution)/shard_map/normed2_x/ppermute | solution.py:349
  93.8 1.0 copy-done.4
  94.8 4.4 %shard_map.119 = (f32[128,768]{1,0:T(8,128)S(1)}, bf16[128,768]{1,0:T(8,128)(2,1)S(1)}) custom-call(s32[7]{0:T(128)S(1)} %stack.31.refs_0_, bf16[128,768]{1,0:T(8,128)(2,1)S(1)} %get-tuple-element.81.refs_1_, bf16[128,768]{1,0:T(8,128)(2,1)S(1)} %collective-permute-done.27.refs_2_, f32[128,768]{1,0:T(8,128)S(1)} %get-tuple-element.82.refs_3_, ...), custom_call_target="tpu_custom_call" | custom-call | flops 1000000000 | bytes 3000000 | tf_op jit(solution)/shard_map/pallas_call | solution.py:528
  99.2 1.4 %collective-permute-start.28 = (bf16[128,768]{1,0:T(8,128)(2,1)S(1)}, bf16[128,768]{1,0:T(8,128)(2,1)S(1)}, u32[]{:S(2)}, u32[]{:S(2)}) collective-permute-start(bf16[128,768]{1,0:T(8,128)(2,1)S(1)} %get-tuple-element.84.own_ref), channel_id=1, source_target_pairs={{0,1},{1,0},{2,3},{3,2},{4,5},{5,4},{6,7},{7,6},{8,9},{9,8},{10,11... | collective-permute-start | bytes 589832 | tf_op jit(solution)/shard_map/normed3_x/ppermute | solution.py:349
  100.6 4.8 %collective-permute-done.28.peer_ref = bf16[128,768]{1,0:T(8,128)(2,1)S(1)} collective-permute-done((bf16[128,768]{1,0:T(8,128)(2,1)S(1)}, bf16[128,768]{1,0:T(8,128)(2,1)S(1)}, u32[]{:S(2)}, u32[]{:S(2)}) %collective-permute-start.28) | collective-permute-done | bytes 196640 | tf_op jit(solution)/shard_map/normed3_x/ppermute | solution.py:349
  105.4 1.7 %shard_map.120 = (bf16[128,768]{1,0:T(8,128)(2,1)S(1)}, bf16[128,768]{1,0:T(8,128)(2,1)S(1)}, f32[1,128]{1,0:T(1,128)S(1)}, f32[1,128]{1,0:T(1,128)S(1)}) custom-call(bf16[128,768]{1,0:T(8,128)(2,1)S(1)} %get-tuple-element.84.own_ref, bf16[128,768]{1,0:T(8,128)(2,1)S(1)} %collective-permute-done.28.peer_ref, f32[128,768]{1,0:T(8,128)S(1)} %get-tuple-element.83.stream_ref, ...), custom_call_target="tpu_custom_call" | custom-call | flops 1000000000 | bytes 3000000 | tf_op jit(solution)/shard_map/pallas_call | solution.py:535
  107.0 1.4 %collective-permute-start.29 = (bf16[128,768]{1,0:T(8,128)(2,1)S(1)}, bf16[128,768]{1,0:T(8,128)(2,1)S(1)}, u32[]{:S(2)}, u32[]{:S(2)}) collective-permute-start(bf16[128,768]{1,0:T(8,128)(2,1)S(1)} %get-tuple-element.87), channel_id=1, source_target_pairs={{0,1},{1,0},{2,3},{3,2},{4,5},{5,4},{6,7},{7,6},{8,9},{9,8},{10,11... | collective-permute-start | bytes 589832 | tf_op jit(solution)/shard_map/part_x/ppermute | solution.py:349
  108.4 0.7 collective-permute-start.30
  109.8 3.1 %collective-permute-done.30.got_head_ref = f32[1,128]{1,0:T(1,128)S(1)} collective-permute-done((f32[1,128]{1,0:T(1,128)S(1)}, f32[1,128]{1,0:T(1,128)S(1)}, u32[]{:S(2)}, u32[]{:S(2)}) %collective-permute-start.30) | collective-permute-done | bytes 544 | tf_op jit(solution)/shard_map/head_x/ppermute | solution.py:349
  112.8 1.1 shard_map.121
  (63 shorter events, 0.3 us)
Async XLA Ops:
  0.6 0.9 copy-start
  1.6 12.5 %collective-permute-start = (bf16[144,384]{1,0:T(8,128)(2,1)S(1)}, bf16[144,384]{1,0:T(8,128)(2,1)S(1)}, u32[]{:S(2)}, u32[]{:S(2)}) collective-permute-start(bf16[144,384]{1,0:T(8,128)(2,1)S(1)} %dynamic-slice_bitcast_fusion.refs_0_), channel_id=1, source_target_pairs={{0,8},{2,10},{4,12},{6,14},{8,0},{10,2},{12,4},{14,6},{16,24},{18,... | collective-permute-start | bytes 331784 | tf_op jit(solution)/shard_map/cross_z1/ppermute | solution.py:345
  4.7 11.4 %collective-permute-start.1 = (bf16[144,384]{1,0:T(8,128)(2,1)S(1)}, bf16[144,384]{1,0:T(8,128)(2,1)S(1)}, u32[]{:S(2)}, u32[]{:S(2)}) collective-permute-start(bf16[144,384]{1,0:T(8,128)(2,1)S(1)} %dynamic-slice_bitcast_fusion.refs_0_), channel_id=1, source_target_pairs={{0,16},{2,18},{4,20},{6,22},{8,24},{10,26},{12,28},{14,30},{16,0},... | collective-permute-start | bytes 331784 | tf_op jit(solution)/shard_map/cross_z2/ppermute | solution.py:345
  7.3 8.8 %collective-permute-start.2 = (bf16[144,384]{1,0:T(8,128)(2,1)S(1)}, bf16[144,384]{1,0:T(8,128)(2,1)S(1)}, u32[]{:S(2)}, u32[]{:S(2)}) collective-permute-start(bf16[144,384]{1,0:T(8,128)(2,1)S(1)} %dynamic-slice_bitcast_fusion.refs_0_), channel_id=1, source_target_pairs={{0,24},{2,26},{4,28},{6,30},{8,16},{10,18},{12,20},{14,22},{16,8},... | collective-permute-start | bytes 331784 | tf_op jit(solution)/shard_map/cross_z3/ppermute | solution.py:345
  8.2 9.2 %collective-permute-start.3 = (bf16[240,384]{1,0:T(8,128)(2,1)S(1)}, bf16[240,384]{1,0:T(8,128)(2,1)S(1)}, u32[]{:S(2)}, u32[]{:S(2)}) collective-permute-start(bf16[240,384]{1,0:T(8,128)(2,1)S(1)} %fusion.1.refs_0_), channel_id=1, source_target_pairs={{0,8},{2,10},{4,12},{6,14},{8,0},{10,2},{12,4},{14,6},{16,24},{18,... | collective-permute-start | bytes 552968 | tf_op jit(solution)/shard_map/rest_z1/ppermute | solution.py:345
  11.5 0.9 copy-start.15
  12.4 0.7 copy-start.18
  14.1 8.3 %copy-start.19 = (f32[128,768]{1,0:T(8,128)}, f32[128,768]{1,0:T(8,128)S(1)}, u32[]{:S(2)}) copy-start(f32[128,768]{1,0:T(8,128)S(1)} %get-tuple-element.72.refs_2_) | copy-start | bytes 1179652
  17.5 23.0 %collective-permute-start.4 = (bf16[4,144,384]{2,1,0:T(8,128)(2,1)S(1)}, bf16[4,144,384]{2,1,0:T(8,128)(2,1)S(1)}, u32[]{:S(2)}, u32[]{:S(2)}) collective-permute-start(bf16[4,144,384]{2,1,0:T(8,128)(2,1)S(1)} %shard_map.114.refs_2_), channel_id=1, source_target_pairs={{0,1},{1,0},{2,6},{3,7},{4,5},{5,4},{6,2},{7,3},{8,9},{9,8},{10,14... | collective-permute-start | bytes 1327112 | tf_op jit(solution)/shard_map/cross_1/ppermute | solution.py:468
  19.0 21.5 %collective-permute-start.5 = (bf16[4,144,384]{2,1,0:T(8,128)(2,1)S(1)}, bf16[4,144,384]{2,1,0:T(8,128)(2,1)S(1)}, u32[]{:S(2)}, u32[]{:S(2)}) collective-permute-start(bf16[4,144,384]{2,1,0:T(8,128)(2,1)S(1)} %shard_map.114.refs_2_), channel_id=1, source_target_pairs={{0,4},{1,5},{2,3},{3,2},{4,0},{5,1},{6,7},{7,6},{8,12},{9,13},{10,... | collective-permute-start | bytes 1327112 | tf_op jit(solution)/shard_map/cross_2/ppermute | solution.py:468
  20.5 9.6 %collective-permute-start.8 = (bf16[240,384]{1,0:T(8,128)(2,1)S(1)}, bf16[240,384]{1,0:T(8,128)(2,1)S(1)}, u32[]{:S(2)}, u32[]{:S(2)}) collective-permute-start(bf16[240,384]{1,0:T(8,128)(2,1)S(1)} %fusion.1.refs_0_), channel_id=1, source_target_pairs={{0,16},{2,18},{4,20},{6,22},{8,24},{10,26},{12,28},{14,30},{16,0},... | collective-permute-start | bytes 552968 | tf_op jit(solution)/shard_map/rest_z2/ppermute | solution.py:345
  22.4 18.1 %collective-permute-start.6 = (bf16[2,240,384]{2,1,0:T(8,128)(2,1)S(1)}, bf16[2,240,384]{2,1,0:T(8,128)(2,1)S(1)}, u32[]{:S(2)}, u32[]{:S(2)}) collective-permute-start(bf16[2,240,384]{2,1,0:T(8,128)(2,1)S(1)} %shard_map.115.refs_4_.refs_5_), channel_id=1, source_target_pairs={{0,1},{1,0},{2,6},{3,7},{4,5},{5,4},{6,2},{7,3},{8,9},{9,8},{10,14... | collective-permute-start | bytes 1105928 | tf_op jit(solution)/shard_map/near_1/ppermute | solution.py:468
  23.0 17.5 %collective-permute-start.7 = (bf16[2,240,384]{2,1,0:T(8,128)(2,1)S(1)}, bf16[2,240,384]{2,1,0:T(8,128)(2,1)S(1)}, u32[]{:S(2)}, u32[]{:S(2)}) collective-permute-start(bf16[2,240,384]{2,1,0:T(8,128)(2,1)S(1)} %shard_map.115.refs_4_.refs_5_), channel_id=1, source_target_pairs={{0,4},{1,5},{2,3},{3,2},{4,0},{5,1},{6,7},{7,6},{8,12},{9,13},{10,... | collective-permute-start | bytes 1105928 | tf_op jit(solution)/shard_map/near_2/ppermute | solution.py:468
  23.5 17.0 %all-to-all-start = ((bf16[16,8,768]{2,1,0:T(8,128)(2,1)}), bf16[16,8,768]{2,1,0:T(8,128)(2,1)S(1)}, u32[]{:S(2)}, u32[]{:S(2)}) async-start(bf16[16,8,768]{2,1,0:T(8,128)(2,1)} %bitcast.10), calls=%async_computation | async-start | bytes 393216 | tf_op jit(solution)/shard_map/all_to_all | solution.py:486
  30.2 9.6 %collective-permute-start.9 = (bf16[240,384]{1,0:T(8,128)(2,1)S(1)}, bf16[240,384]{1,0:T(8,128)(2,1)S(1)}, u32[]{:S(2)}, u32[]{:S(2)}) collective-permute-start(bf16[240,384]{1,0:T(8,128)(2,1)S(1)} %fusion.1.refs_0_), channel_id=1, source_target_pairs={{0,24},{2,26},{4,28},{6,30},{8,16},{10,18},{12,20},{14,22},{16,8},... | collective-permute-start | bytes 552968 | tf_op jit(solution)/shard_map/rest_z3/ppermute | solution.py:345
  39.8 0.7 copy-start.16
  40.5 8.5 %collective-permute-start.10 = (bf16[4,144,384]{2,1,0:T(8,128)(2,1)S(1)}, bf16[4,144,384]{2,1,0:T(8,128)(2,1)}, u32[]{:S(2)}, u32[]{:S(2)}) collective-permute-start(bf16[4,144,384]{2,1,0:T(8,128)(2,1)S(1)} %collective-permute-done.4.refs_3_), channel_id=1, source_target_pairs={{0,4},{1,5},{2,3},{3,2},{4,0},{5,1},{6,7},{7,6},{8,12},{9,13},{10,... | collective-permute-start | bytes 1327112 | tf_op jit(solution)/shard_map/cross_3/ppermute | solution.py:468
  42.0 7.7 %collective-permute-start.12 = (bf16[4,144,384]{2,1,0:T(8,128)(2,1)S(1)}, bf16[4,144,384]{2,1,0:T(8,128)(2,1)S(1)}, u32[]{:S(2)}, u32[]{:S(2)}) collective-permute-start(bf16[4,144,384]{2,1,0:T(8,128)(2,1)S(1)} %collective-permute-done.4.refs_3_), channel_id=1, source_target_pairs={{0,2},{2,0},{4,6},{6,4},{8,10},{10,8},{12,14},{14,12},{16,18},{18,... | collective-permute-start | bytes 1327112 | tf_op jit(solution)/shard_map/cross_core/ppermute | solution.py:345
  42.1 0.8 copy-start.5
  42.8 6.2 %collective-permute-start.11 = (bf16[4,144,384]{2,1,0:T(8,128)(2,1)S(1)}, bf16[4,144,384]{2,1,0:T(8,128)(2,1)S(1)}, u32[]{:S(2)}, u32[]{:S(2)}) collective-permute-start(bf16[4,144,384]{2,1,0:T(8,128)(2,1)S(1)} %shard_map.114.refs_2_), channel_id=1, source_target_pairs={{0,2},{2,0},{4,6},{6,4},{8,10},{10,8},{12,14},{14,12},{16,18},{18,... | collective-permute-start | bytes 1327112 | tf_op jit(solution)/shard_map/cross_core/ppermute | solution.py:345
  43.3 7.2 %collective-permute-start.13 = (bf16[4,144,384]{2,1,0:T(8,128)(2,1)S(1)}, bf16[4,144,384]{2,1,0:T(8,128)(2,1)S(1)}, u32[]{:S(2)}, u32[]{:S(2)}) collective-permute-start(bf16[4,144,384]{2,1,0:T(8,128)(2,1)S(1)} %collective-permute-done.5.refs_4_), channel_id=1, source_target_pairs={{0,2},{2,0},{4,6},{6,4},{8,10},{10,8},{12,14},{14,12},{16,18},{18,... | collective-permute-start | bytes 1327112 | tf_op jit(solution)/shard_map/cross_core/ppermute | solution.py:345
  43.3 0.8 copy-start.7
  49.0 0.8 copy-start.11
  49.8 0.8 copy-start.9
  50.5 0.8 copy-start.13
  51.3 4.1 %collective-permute-start.14 = (bf16[4,144,384]{2,1,0:T(8,128)(2,1)}, bf16[4,144,384]{2,1,0:T(8,128)(2,1)}, u32[]{:S(2)}, u32[]{:S(2)}) collective-permute-start(bf16[4,144,384]{2,1,0:T(8,128)(2,1)} %collective-permute-done.10.refs_5_), channel_id=1, source_target_pairs={{0,2},{2,0},{4,6},{6,4},{8,10},{10,8},{12,14},{14,12},{16,18},{18,... | collective-permute-start | bytes 1327112 | tf_op jit(solution)/shard_map/cross_core/ppermute | solution.py:345
  51.4 0.9 copy-start.17
  52.3 3.1 %copy-start.6 = (bf16[4,144,384]{2,1,0:T(8,128)(2,1)S(1)}, bf16[4,144,384]{2,1,0:T(8,128)(2,1)}, u32[]{:S(2)}) copy-start(bf16[4,144,384]{2,1,0:T(8,128)(2,1)} %copy-done.5) | copy-start | bytes 1327108
  52.3 3.1 %copy-start.8 = (bf16[4,144,384]{2,1,0:T(8,128)(2,1)S(1)}, bf16[4,144,384]{2,1,0:T(8,128)(2,1)}, u32[]{:S(2)}) copy-start(bf16[4,144,384]{2,1,0:T(8,128)(2,1)} %copy-done.7) | copy-start | bytes 1327108
  52.3 3.1 %copy-start.10 = (bf16[4,144,384]{2,1,0:T(8,128)(2,1)S(1)}, bf16[4,144,384]{2,1,0:T(8,128)(2,1)}, u32[]{:S(2)}) copy-start(bf16[4,144,384]{2,1,0:T(8,128)(2,1)} %copy-done.9) | copy-start | bytes 1327108
  52.3 3.1 %copy-start.12 = (bf16[4,144,384]{2,1,0:T(8,128)(2,1)S(1)}, bf16[4,144,384]{2,1,0:T(8,128)(2,1)}, u32[]{:S(2)}) copy-start(bf16[4,144,384]{2,1,0:T(8,128)(2,1)} %copy-done.11) | copy-start | bytes 1327108
  52.3 3.1 %copy-start.14 = (bf16[4,144,384]{2,1,0:T(8,128)(2,1)S(1)}, bf16[4,144,384]{2,1,0:T(8,128)(2,1)}, u32[]{:S(2)}) copy-start(bf16[4,144,384]{2,1,0:T(8,128)(2,1)} %copy-done.13) | copy-start | bytes 1327108
  52.4 10.8 %collective-permute-start.20 = (bf16[2,240,384]{2,1,0:T(8,128)(2,1)S(1)}, bf16[2,240,384]{2,1,0:T(8,128)(2,1)S(1)}, u32[]{:S(2)}, u32[]{:S(2)}) collective-permute-start(bf16[2,240,384]{2,1,0:T(8,128)(2,1)S(1)} %shard_map.117.refs_12_.refs_13_), channel_id=1, source_target_pairs={{0,1},{1,0},{2,6},{3,7},{4,5},{5,4},{6,2},{7,3},{8,9},{9,8},{10,14... | collective-permute-start | bytes 1105928 | tf_op jit(solution)/shard_map/far_1/ppermute | solution.py:468
  53.9 9.5 %collective-permute-start.21 = (bf16[2,240,384]{2,1,0:T(8,128)(2,1)S(1)}, bf16[2,240,384]{2,1,0:T(8,128)(2,1)S(1)}, u32[]{:S(2)}, u32[]{:S(2)}) collective-permute-start(bf16[2,240,384]{2,1,0:T(8,128)(2,1)S(1)} %shard_map.117.refs_12_.refs_13_), channel_id=1, source_target_pairs={{0,4},{1,5},{2,3},{3,2},{4,0},{5,1},{6,7},{7,6},{8,12},{9,13},{10,... | collective-permute-start | bytes 1105928 | tf_op jit(solution)/shard_map/far_2/ppermute | solution.py:468
  63.4 10.6 %collective-permute-start.22 = (bf16[2,240,384]{2,1,0:T(8,128)(2,1)S(1)}, bf16[2,240,384]{2,1,0:T(8,128)(2,1)S(1)}, u32[]{:S(2)}, u32[]{:S(2)}) collective-permute-start(bf16[2,240,384]{2,1,0:T(8,128)(2,1)S(1)} %collective-permute-done.20.refs_13_.refs_14_), channel_id=1, source_target_pairs={{0,4},{1,5},{2,3},{3,2},{4,0},{5,1},{6,7},{7,6},{8,12},{9,13},{10,... | collective-permute-start | bytes 1105928 | tf_op jit(solution)/shard_map/far_3/ppermute | solution.py:468
  65.2 15.2 %all-to-all-start.1 = ((bf16[16,8,768]{2,1,0:T(8,128)(2,1)}), bf16[16,8,768]{2,1,0:T(8,128)(2,1)S(1)}, u32[]{:S(2)}, u32[]{:S(2)}) async-start(bf16[16,8,768]{2,1,0:T(8,128)(2,1)} %bitcast.12), calls=%async_computation.1 | async-start | bytes 393216 | tf_op jit(solution)/shard_map/all_to_all | solution.py:514
  71.4 9.0 %collective-permute-start.23 = (bf16[2,240,384]{2,1,0:T(8,128)(2,1)S(1)}, bf16[2,240,384]{2,1,0:T(8,128)(2,1)S(1)}, u32[]{:S(2)}, u32[]{:S(2)}) collective-permute-start(bf16[2,240,384]{2,1,0:T(8,128)(2,1)S(1)} %shard_map.117.refs_12_.refs_13_), channel_id=1, source_target_pairs={{0,2},{2,0},{4,6},{6,4},{8,10},{10,8},{12,14},{14,12},{16,18},{18,... | collective-permute-start | bytes 1105928 | tf_op jit(solution)/shard_map/far_core/ppermute | solution.py:345
  71.9 9.2 %collective-permute-start.15 = (bf16[2,240,384]{2,1,0:T(8,128)(2,1)S(1)}, bf16[2,240,384]{2,1,0:T(8,128)(2,1)}, u32[]{:S(2)}, u32[]{:S(2)}) collective-permute-start(bf16[2,240,384]{2,1,0:T(8,128)(2,1)S(1)} %collective-permute-done.6.refs_5_.refs_6_), channel_id=1, source_target_pairs={{0,4},{1,5},{2,3},{3,2},{4,0},{5,1},{6,7},{7,6},{8,12},{9,13},{10,... | collective-permute-start | bytes 1105928 | tf_op jit(solution)/shard_map/near_3/ppermute | solution.py:468
  73.6 7.5 %collective-permute-start.16 = (bf16[2,240,384]{2,1,0:T(8,128)(2,1)S(1)}, bf16[2,240,384]{2,1,0:T(8,128)(2,1)}, u32[]{:S(2)}, u32[]{:S(2)}) collective-permute-start(bf16[2,240,384]{2,1,0:T(8,128)(2,1)S(1)} %shard_map.115.refs_4_.refs_5_), channel_id=1, source_target_pairs={{0,2},{2,0},{4,6},{6,4},{8,10},{10,8},{12,14},{14,12},{16,18},{18,... | collective-permute-start | bytes 1105928 | tf_op jit(solution)/shard_map/near_core/ppermute | solution.py:345
  73.6 8.0 %collective-permute-start.17 = (bf16[2,240,384]{2,1,0:T(8,128)(2,1)S(1)}, bf16[2,240,384]{2,1,0:T(8,128)(2,1)}, u32[]{:S(2)}, u32[]{:S(2)}) collective-permute-start(bf16[2,240,384]{2,1,0:T(8,128)(2,1)S(1)} %collective-permute-done.6.refs_5_.refs_6_), channel_id=1, source_target_pairs={{0,2},{2,0},{4,6},{6,4},{8,10},{10,8},{12,14},{14,12},{16,18},{18,... | collective-permute-start | bytes 1105928 | tf_op jit(solution)/shard_map/near_core/ppermute | solution.py:345
  74.1 7.6 %collective-permute-start.18 = (bf16[2,240,384]{2,1,0:T(8,128)(2,1)S(1)}, bf16[2,240,384]{2,1,0:T(8,128)(2,1)}, u32[]{:S(2)}, u32[]{:S(2)}) collective-permute-start(bf16[2,240,384]{2,1,0:T(8,128)(2,1)S(1)} %collective-permute-done.7.refs_6_.refs_7_), channel_id=1, source_target_pairs={{0,2},{2,0},{4,6},{6,4},{8,10},{10,8},{12,14},{14,12},{16,18},{18,... | collective-permute-start | bytes 1105928 | tf_op jit(solution)/shard_map/near_core/ppermute | solution.py:345
  80.4 6.3 %copy-start.3 = (bf16[2,240,384]{2,1,0:T(8,128)(2,1)}, bf16[2,240,384]{2,1,0:T(8,128)(2,1)S(1)}, u32[]{:S(2)}) copy-start(bf16[2,240,384]{2,1,0:T(8,128)(2,1)S(1)} %collective-permute-done.23.refs_16_.refs_17_) | copy-start | bytes 1105924
  80.4 1.7 %collective-permute-start.24 = (bf16[2,240,384]{2,1,0:T(8,128)(2,1)S(1)}, bf16[2,240,384]{2,1,0:T(8,128)(2,1)S(1)}, u32[]{:S(2)}, u32[]{:S(2)}) collective-permute-start(bf16[2,240,384]{2,1,0:T(8,128)(2,1)S(1)} %collective-permute-done.20.refs_13_.refs_14_), channel_id=1, source_target_pairs={{0,2},{2,0},{4,6},{6,4},{8,10},{10,8},{12,14},{14,12},{16,18},{18,... | collective-permute-start | bytes 1105928 | tf_op jit(solution)/shard_map/far_core/ppermute | solution.py:345
  81.1 2.1 %collective-permute-start.25 = (bf16[2,240,384]{2,1,0:T(8,128)(2,1)S(1)}, bf16[2,240,384]{2,1,0:T(8,128)(2,1)S(1)}, u32[]{:S(2)}, u32[]{:S(2)}) collective-permute-start(bf16[2,240,384]{2,1,0:T(8,128)(2,1)S(1)} %collective-permute-done.21.refs_14_.refs_15_), channel_id=1, source_target_pairs={{0,2},{2,0},{4,6},{6,4},{8,10},{10,8},{12,14},{14,12},{16,18},{18,... | collective-permute-start | bytes 1105928 | tf_op jit(solution)/shard_map/far_core/ppermute | solution.py:345
  81.1 2.5 %collective-permute-start.19 = (bf16[2,240,384]{2,1,0:T(8,128)(2,1)}, bf16[2,240,384]{2,1,0:T(8,128)(2,1)S(1)}, u32[]{:S(2)}, u32[]{:S(2)}) collective-permute-start(bf16[2,240,384]{2,1,0:T(8,128)(2,1)} %collective-permute-done.15.refs_7_.refs_8_), channel_id=1, source_target_pairs={{0,2},{2,0},{4,6},{6,4},{8,10},{10,8},{12,14},{14,12},{16,18},{18,... | collective-permute-start | bytes 1105928 | tf_op jit(solution)/shard_map/near_core/ppermute | solution.py:345
  81.6 2.2 %collective-permute-start.26 = (bf16[2,240,384]{2,1,0:T(8,128)(2,1)S(1)}, bf16[2,240,384]{2,1,0:T(8,128)(2,1)S(1)}, u32[]{:S(2)}, u32[]{:S(2)}) collective-permute-start(bf16[2,240,384]{2,1,0:T(8,128)(2,1)S(1)} %collective-permute-done.22.refs_15_.refs_16_), channel_id=1, source_target_pairs={{0,2},{2,0},{4,6},{6,4},{8,10},{10,8},{12,14},{14,12},{16,18},{18,... | collective-permute-start | bytes 1105928 | tf_op jit(solution)/shard_map/far_core/ppermute | solution.py:345
  83.8 1.0 copy-start.20
  86.8 7.0 %collective-permute-start.27 = (bf16[128,768]{1,0:T(8,128)(2,1)S(1)}, bf16[128,768]{1,0:T(8,128)(2,1)S(1)}, u32[]{:S(2)}, u32[]{:S(2)}) collective-permute-start(bf16[128,768]{1,0:T(8,128)(2,1)S(1)} %get-tuple-element.81.refs_1_), channel_id=1, source_target_pairs={{0,1},{1,0},{2,3},{3,2},{4,5},{5,4},{6,7},{7,6},{8,9},{9,8},{10,11... | collective-permute-start | bytes 589832 | tf_op jit(solution)/shard_map/normed2_x/ppermute | solution.py:349
  93.8 1.0 copy-start.4
  94.7 10.6 %copy-start.1 = (bf16[768,1536]{1,0:T(8,128)(2,1)S(1)}, bf16[768,1536]{1,0:T(8,128)(2,1)}, u32[]{:S(2)}) copy-start(bf16[768,1536]{1,0:T(8,128)(2,1)} %up_ref.1) | copy-start | bytes 7077892
  94.8 10.6 %copy-start.2 = (bf16[1536,768]{1,0:T(8,128)(2,1)S(1)}, bf16[1536,768]{1,0:T(8,128)(2,1)}, u32[]{:S(2)}) copy-start(bf16[1536,768]{1,0:T(8,128)(2,1)} %down_ref.1) | copy-start | bytes 7077892
  99.2 6.2 %collective-permute-start.28 = (bf16[128,768]{1,0:T(8,128)(2,1)S(1)}, bf16[128,768]{1,0:T(8,128)(2,1)S(1)}, u32[]{:S(2)}, u32[]{:S(2)}) collective-permute-start(bf16[128,768]{1,0:T(8,128)(2,1)S(1)} %get-tuple-element.84.own_ref), channel_id=1, source_target_pairs={{0,1},{1,0},{2,3},{3,2},{4,5},{5,4},{6,7},{7,6},{8,9},{9,8},{10,11... | collective-permute-start | bytes 589832 | tf_op jit(solution)/shard_map/normed3_x/ppermute | solution.py:349
  107.0 5.8 %collective-permute-start.29 = (bf16[128,768]{1,0:T(8,128)(2,1)S(1)}, bf16[128,768]{1,0:T(8,128)(2,1)S(1)}, u32[]{:S(2)}, u32[]{:S(2)}) collective-permute-start(bf16[128,768]{1,0:T(8,128)(2,1)S(1)} %get-tuple-element.87), channel_id=1, source_target_pairs={{0,1},{1,0},{2,3},{3,2},{4,5},{5,4},{6,7},{7,6},{8,9},{9,8},{10,11... | collective-permute-start | bytes 589832 | tf_op jit(solution)/shard_map/part_x/ppermute | solution.py:349
  108.4 4.4 %collective-permute-start.30 = (f32[1,128]{1,0:T(1,128)S(1)}, f32[1,128]{1,0:T(1,128)S(1)}, u32[]{:S(2)}, u32[]{:S(2)}) collective-permute-start(f32[1,128]{1,0:T(1,128)S(1)} %get-tuple-element.88.own_head_ref), channel_id=1, source_target_pairs={{0,1},{1,0},{2,3},{3,2},{4,5},{5,4},{6,7},{7,6},{8,9},{9,8},{10,11... | collective-permute-start | bytes 1544 | tf_op jit(solution)/shard_map/head_x/ppermute | solution.py:349

commit v4 on v3

--- a/solution.py
+++ b/solution.py
@@ -370,6 +370,10 @@
     )(*pieces)
 
 
+def add_kernel(first_ref, second_ref, out_ref):
+    out_ref[...] = first_ref[...] + second_ref[...]
+
+
 def after(value, *others):
     return lax.optimization_barrier((value, *others))[0]
 
@@ -467,6 +471,10 @@
         with jax.named_scope(name):
             return lax.ppermute(a, ("gx", "gz"), pairs)
 
+    def diagonal(a, name):
+        with jax.named_scope(name):
+            return lax.ppermute(a, ("gx", "gz"), [(device, device ^ 5) for device in range(2 * peers)])
+
     first_half = lane_half(cross_qkv.T)
     half = lane_half(jnp.concatenate([depth_qkv.T, cross_out, depth_out], axis=0))
     pieces = first_half, to(first_half, 4, "cross_z1"), to(first_half, 8, "cross_z2"), to(first_half, 12, "cross_z3")
@@ -478,30 +486,33 @@
     )(tokens.reshape(rows, width), encoding, gains, head_weight.reshape(1, width))
 
     pieces, near, half, normed = lax.optimization_barrier((pieces, near, half, normed))
-    far = to(half, 8, "rest_z2"), to(half, 12, "rest_z3")
     pieces = stack(*pieces)
     pieces_1, pieces_2 = cross_over(pieces, 0, "cross_1"), cross_over(pieces, 1, "cross_2")
     near = stack(half, near)
+    with jax.named_scope("rest_middle"):
+        pairs = [(4 * at + k, 12 - 4 * at + k) for at in (1, 2) for k in range(4)]
+        crossed = lax.ppermute(near, "gx", pairs)
+    with jax.named_scope("rest_onward"):
+        pairs = [(4 * at + k, 12 * (at - 1) + k) for at in (1, 2) for k in range(4)]
+        passed = lax.ppermute(crossed, "gx", pairs)
     near_1, near_2 = cross_over(near, 0, "near_1"), cross_over(near, 1, "near_2")
     lined = lax.all_to_all(
         normed.reshape(peers, rows // peers, width), "gx", split_axis=0, concat_axis=0, tiled=True
     ).reshape(rows, width)
 
-    pieces, pieces_1, pieces_2, near, near_1, near_2, far, lined = lax.optimization_barrier(
-        (pieces, pieces_1, pieces_2, near, near_1, near_2, far, lined)
+    pieces, pieces_1, pieces_2, near, near_1, near_2, crossed, passed, lined = lax.optimization_barrier(
+        (pieces, pieces_1, pieces_2, near, near_1, near_2, crossed, passed, lined)
     )
     pieces_3 = cross_over(pieces_1, 1, "cross_3")
     cross_pieces = [to(piece, 1, "cross_core") for piece in (pieces, pieces_1, pieces_2)]
 
-    pieces, pieces_1, pieces_2, pieces_3, cross_pieces, near, near_1, near_2, far, lined = lax.optimization_barrier(
-        (pieces, pieces_1, pieces_2, pieces_3, cross_pieces, near, near_1, near_2, far, lined)
-    )
+    far = call(add_kernel, shape(crossed.shape, BF16), [VMEM] * 2, vmem=8)(crossed, passed)
+    pieces_3, far = lax.optimization_barrier((pieces_3, far))
     cross_pieces = [pieces, pieces_1, pieces_2, pieces_3, *cross_pieces, to(pieces_3, 1, "cross_core")]
-    near_3 = cross_over(near_1, 1, "near_3")
-    far = stack(*far)
     far_1, far_2 = cross_over(far, 0, "far_1"), cross_over(far, 1, "far_2")
-    near_pieces = [near, near_1, near_2, near_3]
-    near_pieces += [to(piece, 1, "near_core") for piece in near_pieces]
+    inner = (z == 1) | (z == 2)
+    rest_planes = [z, z ^ 1, jnp.where(inner, z ^ 3, z ^ 2), jnp.where(inner, z ^ 2, z ^ 3)]
+    rest_place = jnp.stack([y, c, x] + rest_planes).astype(jnp.int32)
     place = jnp.stack([y, c, x] + planes).astype(jnp.int32)
     mixed = call(
         functools.partial(cross_kernel, plan=plan, rows=chunk),
@@ -510,12 +521,14 @@
         [pltpu.VMEM((3 * width, width), BF16)],
         us=30,
     )(place, lined, *cross_pieces)
-    attended = mixed
+    mixed, far_1, near_1 = lax.optimization_barrier((mixed, far_1, near_1))
     mixed = lax.all_to_all(
         mixed.reshape(peers, rows // peers, width), "gx", split_axis=0, concat_axis=0, tiled=True
     ).reshape(rows, width)
-    far_3 = cross_over(after(far_1, far_2, attended), 1, "far_3")
-    far_pieces = [far, far_1, far_2, after(far_3, mixed)]
+    near_3, far_3 = cross_over(near_1, 1, "near_3"), cross_over(far_1, 1, "far_3")
+    near_pieces = [near, near_1, near_2, near_3]
+    near_pieces += [to(piece, 1, "near_core") for piece in near_pieces]
+    far_pieces = [far, far_1, far_2, far_3]
     far_pieces += [to(piece, 1, "far_core") for piece in far_pieces]
     stream, normed = call(
         functools.partial(cross_out_kernel, chunk=chunk, count=count),
@@ -523,14 +536,14 @@
         [SMEM] + [VMEM] * 19,
         [pltpu.VMEM((width, width), BF16)],
         us=2,
-    )(place, mixed, stream, gains, *near_pieces, *far_pieces)
+    )(rest_place, mixed, stream, gains, *near_pieces, *far_pieces)
     peer = to_x(normed, "normed2_x")
     stream, normed = call(
         functools.partial(depth_kernel, plan=plan, chunk=chunk, count=count),
         (wide, narrow),
         [SMEM] + [VMEM] * 20,
         [pltpu.VMEM((3 * width, width), BF16), pltpu.VMEM((width, width), BF16)],
-    )(place, normed, peer, stream, gains, *near_pieces, *far_pieces)
+    )(rest_place, normed, peer, stream, gains, *near_pieces, *far_pieces)
     peer = to_x(normed, "normed3_x")
     own_part, peer_part, own_head, peer_head = call(
         mlp_kernel, (narrow, narrow, row, row), [VMEM] * 6

time: 115 us -> 111 us (0.965)
  starting transfers between devices: 40.9 us -> 38 us
    ppermute x18 -> x16, waiting for transfers between devices: 14.7 us -> 3.36 us  [shift(): return lax.ppermute(a, 'gx', [(i, i ^ step) for i in range(peers)])]
    ppermute x9, waiting for transfers between devices: 8.97 us -> 19.1 us  [cross_over(): return lax.ppermute(a, ('gx', 'gz'), pairs)]
    ppermute x18 -> x16, starting transfers between devices: 13.4 us -> 8.85 us  [shift(): return lax.ppermute(a, 'gx', [(i, i ^ step) for i in range(peers)])]
    ppermute x0 -> x2, waiting for transfers between devices: none -> 3.42 us  [the longest x1 3.41 us: fast_body(): passed = lax.ppermute(crossed, 'gx', pairs)]
    all_to_all x1, waiting for transfers between devices: 6.35 us -> 4.26 us  [fast_body(): lax.all_to_all(mixed.reshape(peers, rows // peers, width), 'gx', split_ax...]
    ppermute x0 -> x2, starting transfers between devices: none -> 1.98 us  [the longest x1 1.29 us: fast_body(): passed = lax.ppermute(crossed, 'gx', pairs)]
    all_to_all x1, starting transfers between devices: 4.25 us -> 5.94 us  [fast_body(): lax.all_to_all(normed.reshape(peers, rows // peers, width), 'gx', split_a...]
    ppermute x9, starting transfers between devices: 12.2 us -> 10.6 us  [cross_over(): return lax.ppermute(a, ('gx', 'gz'), pairs)]
  transfers between devices with their start and end apart: 33 -> 33, of which waited for: 16 -> 13; matrix products, arithmetic and copies ran while one was open for 3% -> 3% of each run, Pallas kernels for 5% -> 5%
where the time goes in v4:
time: 111 us; the launch traced here: 110 us
  waiting for transfers between devices  42.6 us (38%)
  starting transfers between devices  38 us (34%)
  Pallas kernels  15.5 us (14%)
  local copies, waits for them, and re-layouts  9.84 us (9%)
  other arithmetic  2.5 us (2%)
  between operations  1.53 us (1%)
    ppermute x9, waiting for transfers between devices, cross_over(): return lax.ppermute(a, ('gx', 'gz'), pairs)  19.1 us
    ppermute x4, waiting for transfers between devices, swap_x(): return lax.ppermute(a, 'gz', [(0, 1), (1, 0)])  12.3 us
    ppermute x9, starting transfers between devices, cross_over(): return lax.ppermute(a, ('gx', 'gz'), pairs)  10.6 us
    unnamed x32, local copies, waits for them, and re-layouts  8.97 us
    ppermute x16, starting transfers between devices, shift(): return lax.ppermute(a, 'gx', [(i, i ^ step) for i in range(peers)])  8.85 us
    all_to_all x1, starting transfers between devices, fast_body(): lax.all_to_all(normed.reshape(peers, rows // peers, width), 'gx', split_a...  5.94 us
    all_to_all x1, starting transfers between devices, fast_body(): lax.all_to_all(mixed.reshape(peers, rows // peers, width), 'gx', split_ax...  5.44 us
    ppermute x4, starting transfers between devices, swap_x(): return lax.ppermute(a, 'gz', [(0, 1), (1, 0)])  5.2 us
  transfers between devices with their start and end apart: 33, of which 13 were waited for; matrix products, arithmetic and copies ran while one was open for 3% of the time, Pallas kernels for 5%

profile of v4, /device:TPU:0, one launch (start us, length us, event | category | flops | bytes accessed | tf_op | source)
XLA Modules:
  0.0 109.9 jit_solution(14995723051089863612)
XLA Ops:
  0.6 0.0 copy-start
  0.6 0.9 copy-done
  1.6 3.1 %collective-permute-start = (bf16[144,384]{1,0:T(8,128)(2,1)S(1)}, bf16[144,384]{1,0:T(8,128)(2,1)S(1)}, u32[]{:S(2)}, u32[]{:S(2)}) collective-permute-start(bf16[144,384]{1,0:T(8,128)(2,1)S(1)} %dynamic-slice_bitcast_fusion.refs_0_), channel_id=1, source_target_pairs={{0,8},{2,10},{4,12},{6,14},{8,0},{10,2},{12,4},{14,6},{16,24},{18,... | collective-permute-start | bytes 331784 | tf_op jit(solution)/shard_map/cross_z1/ppermute | solution.py:345
  4.7 2.6 %collective-permute-start.1 = (bf16[144,384]{1,0:T(8,128)(2,1)S(1)}, bf16[144,384]{1,0:T(8,128)(2,1)S(1)}, u32[]{:S(2)}, u32[]{:S(2)}) collective-permute-start(bf16[144,384]{1,0:T(8,128)(2,1)S(1)} %dynamic-slice_bitcast_fusion.refs_0_), channel_id=1, source_target_pairs={{0,16},{2,18},{4,20},{6,22},{8,24},{10,26},{12,28},{14,30},{16,0},... | collective-permute-start | bytes 331784 | tf_op jit(solution)/shard_map/cross_z2/ppermute | solution.py:345
  7.3 0.9 fusion.1.refs_0_
  8.2 1.0 collective-permute-start.3
  9.2 1.5 %cosine_select_fusion.encoding_ref = f32[128,768]{1,0:T(8,128)S(1)} fusion(f32[768]{0:T(1024)S(1)} %fusion.10, s32[128]{0:T(128)S(1)} %fusion.17, s32[128]{0:T(128)S(1)} %get-tuple-element.73, s32[128]{0:T(128)S(1)} %get-tuple-element.72, pred[768]{0:T(1024)(128)(4,1)S(1)} %broadcast_compare_fusion.1, pred[768]{0:T(1024)(128)(4,1)S(1)} %get-tuple-element.75, ...), kind=kLoop, calls=%fused_computation | loop fusion | flops 491520 | bytes 400128 | tf_op jit(solution)/shard_map/encoding/jit(_where)/select_n | solution.py:460
  10.8 0.7 reshape.94.head_ref
  11.5 0.9 copy-done.12
  12.4 0.7 copy-done.13
  13.1 1.0 shard_map.113
  14.1 2.0 %collective-permute-done.1.refs_2_ = bf16[144,384]{1,0:T(8,128)(2,1)S(1)} collective-permute-done((bf16[144,384]{1,0:T(8,128)(2,1)S(1)}, bf16[144,384]{1,0:T(8,128)(2,1)S(1)}, u32[]{:S(2)}, u32[]{:S(2)}) %collective-permute-start.1) | collective-permute-done | bytes 110624 | tf_op jit(solution)/shard_map/cross_z2/ppermute | solution.py:345
  16.0 1.4 %collective-permute-done.3.refs_1_ = bf16[240,384]{1,0:T(8,128)(2,1)S(1)} collective-permute-done((bf16[240,384]{1,0:T(8,128)(2,1)S(1)}, bf16[240,384]{1,0:T(8,128)(2,1)S(1)}, u32[]{:S(2)}, u32[]{:S(2)}) %collective-permute-start.3) | collective-permute-done | bytes 184352 | tf_op jit(solution)/shard_map/rest_z1/ppermute | solution.py:345
  17.4 0.7 collective-permute-start.8
  18.2 1.6 %collective-permute-start.4 = (bf16[4,144,384]{2,1,0:T(8,128)(2,1)S(1)}, bf16[4,144,384]{2,1,0:T(8,128)(2,1)S(1)}, u32[]{:S(2)}, u32[]{:S(2)}) collective-permute-start(bf16[4,144,384]{2,1,0:T(8,128)(2,1)S(1)} %shard_map.114.refs_2_), channel_id=1, source_target_pairs={{0,1},{1,0},{2,6},{3,7},{4,5},{5,4},{6,2},{7,3},{8,9},{9,8},{10,14... | collective-permute-start | bytes 1327112 | tf_op jit(solution)/shard_map/cross_1/ppermute | solution.py:472
  19.8 1.5 %collective-permute-start.5 = (bf16[4,144,384]{2,1,0:T(8,128)(2,1)S(1)}, bf16[4,144,384]{2,1,0:T(8,128)(2,1)}, u32[]{:S(2)}, u32[]{:S(2)}) collective-permute-start(bf16[4,144,384]{2,1,0:T(8,128)(2,1)S(1)} %shard_map.114.refs_2_), channel_id=1, source_target_pairs={{0,4},{1,5},{2,3},{3,2},{4,0},{5,1},{6,7},{7,6},{8,12},{9,13},{10,... | collective-permute-start | bytes 1327112 | tf_op jit(solution)/shard_map/cross_2/ppermute | solution.py:472
  21.3 0.5 collective-permute-start.6
  21.8 0.5 collective-permute-start.7
  22.3 5.9 %all-to-all-start = ((bf16[16,8,768]{2,1,0:T(8,128)(2,1)}), bf16[16,8,768]{2,1,0:T(8,128)(2,1)S(1)}, u32[]{:S(2)}, u32[]{:S(2)}) async-start(bf16[16,8,768]{2,1,0:T(8,128)(2,1)} %bitcast.12), calls=%async_computation | async-start | bytes 393216 | tf_op jit(solution)/shard_map/all_to_all | solution.py:499
  28.3 1.3 %collective-permute-start.9 = (bf16[2,240,384]{2,1,0:T(8,128)(2,1)S(1)}, bf16[2,240,384]{2,1,0:T(8,128)(2,1)S(1)}, u32[]{:S(2)}, u32[]{:S(2)}) collective-permute-start(bf16[2,240,384]{2,1,0:T(8,128)(2,1)S(1)} %collective-permute-done.8.first_ref), channel_id=1, source_target_pairs={{8,0},{10,2},{12,4},{14,6},{16,24},{18,26},{20,28},{22,30},{9,1},{... | collective-permute-start | bytes 1105928 | tf_op jit(solution)/shard_map/rest_onward/ppermute | solution.py:497
  29.6 8.7 %collective-permute-done.6.refs_5_.refs_6_ = bf16[2,240,384]{2,1,0:T(8,128)(2,1)S(1)} collective-permute-done((bf16[2,240,384]{2,1,0:T(8,128)(2,1)S(1)}, bf16[2,240,384]{2,1,0:T(8,128)(2,1)S(1)}, u32[]{:S(2)}, u32[]{:S(2)}) %collective-permute-start.6) | collective-permute-done | bytes 368672 | tf_op jit(solution)/shard_map/near_1/ppermute | solution.py:472
  38.3 0.7 collective-permute-done.7.refs_6_.refs_7_
  39.0 0.1 all-to-all-done
  39.2 3.4 %collective-permute-done.9.second_ref = bf16[2,240,384]{2,1,0:T(8,128)(2,1)S(1)} collective-permute-done((bf16[2,240,384]{2,1,0:T(8,128)(2,1)S(1)}, bf16[2,240,384]{2,1,0:T(8,128)(2,1)S(1)}, u32[]{:S(2)}, u32[]{:S(2)}) %collective-permute-start.9) | collective-permute-done | bytes 368672 | tf_op jit(solution)/shard_map/rest_onward/ppermute | solution.py:497
  42.6 0.7 copy-done.10
  43.3 1.5 %collective-permute-start.10 = (bf16[4,144,384]{2,1,0:T(8,128)(2,1)S(1)}, bf16[4,144,384]{2,1,0:T(8,128)(2,1)}, u32[]{:S(2)}, u32[]{:S(2)}) collective-permute-start(bf16[4,144,384]{2,1,0:T(8,128)(2,1)S(1)} %collective-permute-done.4.refs_3_), channel_id=1, source_target_pairs={{0,4},{1,5},{2,3},{3,2},{4,0},{5,1},{6,7},{7,6},{8,12},{9,13},{10,... | collective-permute-start | bytes 1327112 | tf_op jit(solution)/shard_map/cross_3/ppermute | solution.py:472
  44.8 0.5 collective-permute-start.11
  45.3 1.0 copy-done.11
  46.3 0.1 shard_map.116.refs_12_.refs_13_
  46.3 5.4 %collective-permute-done.10.refs_5_ = bf16[4,144,384]{2,1,0:T(8,128)(2,1)} collective-permute-done((bf16[4,144,384]{2,1,0:T(8,128)(2,1)S(1)}, bf16[4,144,384]{2,1,0:T(8,128)(2,1)}, u32[]{:S(2)}, u32[]{:S(2)}) %collective-permute-start.10) | collective-permute-done | bytes 442400 | tf_op jit(solution)/shard_map/cross_3/ppermute | solution.py:472
  51.7 0.1 stack.48.refs_0_
  51.8 0.5 collective-permute-start.17
  52.3 0.1 collective-permute-start.19
  52.4 1.5 %collective-permute-start.15 = (bf16[2,240,384]{2,1,0:T(8,128)(2,1)S(1)}, bf16[2,240,384]{2,1,0:T(8,128)(2,1)S(1)}, u32[]{:S(2)}, u32[]{:S(2)}) collective-permute-start(bf16[2,240,384]{2,1,0:T(8,128)(2,1)S(1)} %shard_map.116.refs_12_.refs_13_), channel_id=1, source_target_pairs={{0,1},{1,0},{2,6},{3,7},{4,5},{5,4},{6,2},{7,3},{8,9},{9,8},{10,14... | collective-permute-start | bytes 1105928 | tf_op jit(solution)/shard_map/far_1/ppermute | solution.py:472
  53.9 1.5 %collective-permute-start.21 = (bf16[2,240,384]{2,1,0:T(8,128)(2,1)S(1)}, bf16[2,240,384]{2,1,0:T(8,128)(2,1)S(1)}, u32[]{:S(2)}, u32[]{:S(2)}) collective-permute-start(bf16[2,240,384]{2,1,0:T(8,128)(2,1)S(1)} %shard_map.116.refs_12_.refs_13_), channel_id=1, source_target_pairs={{0,4},{1,5},{2,3},{3,2},{4,0},{5,1},{6,7},{7,6},{8,12},{9,13},{10,... | collective-permute-start | bytes 1105928 | tf_op jit(solution)/shard_map/far_2/ppermute | solution.py:472
  55.4 1.0 copy-done.7
  56.4 1.0 copy-done.9
  57.4 4.4 %shard_map.117 = bf16[128,768]{1,0:T(8,128)(2,1)S(1)} custom-call(s32[7]{0:T(128)S(1)} %stack.48.refs_0_, bf16[128,768]{1,0:T(8,128)(2,1)S(1)} %bitcast.19, bf16[4,144,384]{2,1,0:T(8,128)(2,1)S(1)} %copy-done.7, bf16[4,144,384]{2,1,0:T(8,128)(2,1)S(1)} %copy-done.9, bf16[4,144,384]{2,1,0:T(8,128)(2,1)} %collective-permute-done.5.refs_4_, ...), custom_call_target="tpu_custom_call" | custom-call | flops 30000001024 | bytes 90000000 | tf_op jit(solution)/shard_map/pallas_call | solution.py:517
  61.8 0.0 copy-start.5
  61.8 0.7 copy-done.5
  62.5 0.8 collective-permute-done.15.refs_13_.refs_14_
  63.3 1.8 %collective-permute-start.16 = (bf16[2,240,384]{2,1,0:T(8,128)(2,1)S(1)}, bf16[2,240,384]{2,1,0:T(8,128)(2,1)}, u32[]{:S(2)}, u32[]{:S(2)}) collective-permute-start(bf16[2,240,384]{2,1,0:T(8,128)(2,1)S(1)} %collective-permute-done.6.refs_5_.refs_6_), channel_id=1, source_target_pairs={{0,4},{1,5},{2,3},{3,2},{4,0},{5,1},{6,7},{7,6},{8,12},{9,13},{10,... | collective-permute-start | bytes 1105928 | tf_op jit(solution)/shard_map/near_3/ppermute | solution.py:472
  65.1 0.2 collective-permute-start.22
  65.3 5.4 %all-to-all-start.1 = ((bf16[16,8,768]{2,1,0:T(8,128)(2,1)}), bf16[16,8,768]{2,1,0:T(8,128)(2,1)S(1)}, u32[]{:S(2)}, u32[]{:S(2)}) async-start(bf16[16,8,768]{2,1,0:T(8,128)(2,1)} %bitcast.20), calls=%async_computation.1 | async-start | bytes 393216 | tf_op jit(solution)/shard_map/all_to_all | solution.py:525
  70.8 0.5 collective-permute-start.25
  71.3 0.1 collective-permute-start.18
  71.4 0.4 collective-permute-start.24
  71.8 0.1 collective-permute-start.20
  71.9 3.5 %collective-permute-done.22.refs_15_.refs_16_ = bf16[2,240,384]{2,1,0:T(8,128)(2,1)} collective-permute-done((bf16[2,240,384]{2,1,0:T(8,128)(2,1)S(1)}, bf16[2,240,384]{2,1,0:T(8,128)(2,1)}, u32[]{:S(2)}, u32[]{:S(2)}) %collective-permute-start.22) | collective-permute-done | bytes 368672 | tf_op jit(solution)/shard_map/far_3/ppermute | solution.py:472
  75.4 0.1 stack.45.refs_0_
  75.5 4.3 %all-to-all-done.1 = bf16[16,8,768]{2,1,0:T(8,128)(2,1)S(1)} async-done(((bf16[16,8,768]{2,1,0:T(8,128)(2,1)}), bf16[16,8,768]{2,1,0:T(8,128)(2,1)S(1)}, u32[]{:S(2)}, u32[]{:S(2)}) %all-to-all-start.1) | async-done | bytes 196640 | tf_op jit(solution)/shard_map/all_to_all | solution.py:525
  79.8 1.0 copy-done.15
  80.8 2.3 %shard_map.118 = (f32[128,768]{1,0:T(8,128)S(1)}, bf16[128,768]{1,0:T(8,128)(2,1)S(1)}) custom-call(s32[7]{0:T(128)S(1)} %stack.45.refs_0_, bf16[128,768]{1,0:T(8,128)(2,1)S(1)} %bitcast.21, f32[128,768]{1,0:T(8,128)S(1)} %copy-done.15, f32[3,768]{1,0:T(4,128)S(1)} %get-tuple-element.56.refs_3_.refs_4_, bf16[2,240,384]{2,1,0:T(8,128)(2,1)S(1)} %shard_map.115.refs_4_.refs_5_, ...), custom_call_target="tpu_custom_call" | custom-call | flops 2000000000 | bytes 6000000 | tf_op jit(solution)/shard_map/pallas_call | solution.py:533
  83.1 1.6 %collective-permute-start.27 = (bf16[128,768]{1,0:T(8,128)(2,1)S(1)}, bf16[128,768]{1,0:T(8,128)(2,1)S(1)}, u32[]{:S(2)}, u32[]{:S(2)}) collective-permute-start(bf16[128,768]{1,0:T(8,128)(2,1)S(1)} %get-tuple-element.61.refs_1_), channel_id=1, source_target_pairs={{0,1},{1,0},{2,3},{3,2},{4,5},{5,4},{6,7},{7,6},{8,9},{9,8},{10,11... | collective-permute-start | bytes 589832 | tf_op jit(solution)/shard_map/normed2_x/ppermute | solution.py:349
  84.7 5.1 %collective-permute-done.27.refs_2_ = bf16[128,768]{1,0:T(8,128)(2,1)S(1)} collective-permute-done((bf16[128,768]{1,0:T(8,128)(2,1)S(1)}, bf16[128,768]{1,0:T(8,128)(2,1)S(1)}, u32[]{:S(2)}, u32[]{:S(2)}) %collective-permute-start.27) | collective-permute-done | bytes 196640 | tf_op jit(solution)/shard_map/normed2_x/ppermute | solution.py:349
  89.7 1.0 copy-done.4
  90.7 4.9 %shard_map.119 = (f32[128,768]{1,0:T(8,128)S(1)}, bf16[128,768]{1,0:T(8,128)(2,1)S(1)}) custom-call(s32[7]{0:T(128)S(1)} %stack.45.refs_0_, bf16[128,768]{1,0:T(8,128)(2,1)S(1)} %get-tuple-element.61.refs_1_, bf16[128,768]{1,0:T(8,128)(2,1)S(1)} %collective-permute-done.27.refs_2_, f32[128,768]{1,0:T(8,128)S(1)} %get-tuple-element.62.refs_3_, ...), custom_call_target="tpu_custom_call" | custom-call | flops 1000000000 | bytes 3000000 | tf_op jit(solution)/shard_map/pallas_call | solution.py:541
  95.6 1.6 %collective-permute-start.28 = (bf16[128,768]{1,0:T(8,128)(2,1)S(1)}, bf16[128,768]{1,0:T(8,128)(2,1)S(1)}, u32[]{:S(2)}, u32[]{:S(2)}) collective-permute-start(bf16[128,768]{1,0:T(8,128)(2,1)S(1)} %get-tuple-element.64.own_ref), channel_id=1, source_target_pairs={{0,1},{1,0},{2,3},{3,2},{4,5},{5,4},{6,7},{7,6},{8,9},{9,8},{10,11... | collective-permute-start | bytes 589832 | tf_op jit(solution)/shard_map/normed3_x/ppermute | solution.py:349
  97.2 4.2 %collective-permute-done.28.peer_ref = bf16[128,768]{1,0:T(8,128)(2,1)S(1)} collective-permute-done((bf16[128,768]{1,0:T(8,128)(2,1)S(1)}, bf16[128,768]{1,0:T(8,128)(2,1)S(1)}, u32[]{:S(2)}, u32[]{:S(2)}) %collective-permute-start.28) | collective-permute-done | bytes 196640 | tf_op jit(solution)/shard_map/normed3_x/ppermute | solution.py:349
  101.3 1.7 %shard_map.120 = (bf16[128,768]{1,0:T(8,128)(2,1)S(1)}, bf16[128,768]{1,0:T(8,128)(2,1)S(1)}, f32[1,128]{1,0:T(1,128)S(1)}, f32[1,128]{1,0:T(1,128)S(1)}) custom-call(bf16[128,768]{1,0:T(8,128)(2,1)S(1)} %get-tuple-element.64.own_ref, bf16[128,768]{1,0:T(8,128)(2,1)S(1)} %collective-permute-done.28.peer_ref, f32[128,768]{1,0:T(8,128)S(1)} %get-tuple-element.63.stream_ref, ...), custom_call_target="tpu_custom_call" | custom-call | flops 1000000000 | bytes 3000000 | tf_op jit(solution)/shard_map/pallas_call | solution.py:548
  103.0 1.6 %collective-permute-start.29 = (bf16[128,768]{1,0:T(8,128)(2,1)S(1)}, bf16[128,768]{1,0:T(8,128)(2,1)S(1)}, u32[]{:S(2)}, u32[]{:S(2)}) collective-permute-start(bf16[128,768]{1,0:T(8,128)(2,1)S(1)} %get-tuple-element.67), channel_id=1, source_target_pairs={{0,1},{1,0},{2,3},{3,2},{4,5},{5,4},{6,7},{7,6},{8,9},{9,8},{10,11... | collective-permute-start | bytes 589832 | tf_op jit(solution)/shard_map/part_x/ppermute | solution.py:349
  104.6 0.5 collective-permute-start.30
  105.8 3.1 %collective-permute-done.30.got_head_ref = f32[1,128]{1,0:T(1,128)S(1)} collective-permute-done((f32[1,128]{1,0:T(1,128)S(1)}, f32[1,128]{1,0:T(1,128)S(1)}, u32[]{:S(2)}, u32[]{:S(2)}) %collective-permute-start.30) | collective-permute-done | bytes 544 | tf_op jit(solution)/shard_map/head_x/ppermute | solution.py:349
  108.9 1.1 shard_map.121
  (54 shorter events, 0.2 us)
Async XLA Ops:
  0.6 0.9 copy-start
  1.6 12.5 %collective-permute-start = (bf16[144,384]{1,0:T(8,128)(2,1)S(1)}, bf16[144,384]{1,0:T(8,128)(2,1)S(1)}, u32[]{:S(2)}, u32[]{:S(2)}) collective-permute-start(bf16[144,384]{1,0:T(8,128)(2,1)S(1)} %dynamic-slice_bitcast_fusion.refs_0_), channel_id=1, source_target_pairs={{0,8},{2,10},{4,12},{6,14},{8,0},{10,2},{12,4},{14,6},{16,24},{18,... | collective-permute-start | bytes 331784 | tf_op jit(solution)/shard_map/cross_z1/ppermute | solution.py:345
  4.7 11.4 %collective-permute-start.1 = (bf16[144,384]{1,0:T(8,128)(2,1)S(1)}, bf16[144,384]{1,0:T(8,128)(2,1)S(1)}, u32[]{:S(2)}, u32[]{:S(2)}) collective-permute-start(bf16[144,384]{1,0:T(8,128)(2,1)S(1)} %dynamic-slice_bitcast_fusion.refs_0_), channel_id=1, source_target_pairs={{0,16},{2,18},{4,20},{6,22},{8,24},{10,26},{12,28},{14,30},{16,0},... | collective-permute-start | bytes 331784 | tf_op jit(solution)/shard_map/cross_z2/ppermute | solution.py:345
  7.3 8.8 %collective-permute-start.2 = (bf16[144,384]{1,0:T(8,128)(2,1)S(1)}, bf16[144,384]{1,0:T(8,128)(2,1)S(1)}, u32[]{:S(2)}, u32[]{:S(2)}) collective-permute-start(bf16[144,384]{1,0:T(8,128)(2,1)S(1)} %dynamic-slice_bitcast_fusion.refs_0_), channel_id=1, source_target_pairs={{0,24},{2,26},{4,28},{6,30},{8,16},{10,18},{12,20},{14,22},{16,8},... | collective-permute-start | bytes 331784 | tf_op jit(solution)/shard_map/cross_z3/ppermute | solution.py:345
  8.2 9.2 %collective-permute-start.3 = (bf16[240,384]{1,0:T(8,128)(2,1)S(1)}, bf16[240,384]{1,0:T(8,128)(2,1)S(1)}, u32[]{:S(2)}, u32[]{:S(2)}) collective-permute-start(bf16[240,384]{1,0:T(8,128)(2,1)S(1)} %fusion.1.refs_0_), channel_id=1, source_target_pairs={{0,8},{2,10},{4,12},{6,14},{8,0},{10,2},{12,4},{14,6},{16,24},{18,... | collective-permute-start | bytes 552968 | tf_op jit(solution)/shard_map/rest_z1/ppermute | solution.py:345
  11.5 0.9 copy-start.12
  12.4 0.7 copy-start.13
  14.1 4.1 %copy-start.14 = (f32[128,768]{1,0:T(8,128)}, f32[128,768]{1,0:T(8,128)S(1)}, u32[]{:S(2)}) copy-start(f32[128,768]{1,0:T(8,128)S(1)} %get-tuple-element.55.refs_2_) | copy-start | bytes 1179652
  17.4 10.8 %collective-permute-start.8 = (bf16[2,240,384]{2,1,0:T(8,128)(2,1)S(1)}, bf16[2,240,384]{2,1,0:T(8,128)(2,1)S(1)}, u32[]{:S(2)}, u32[]{:S(2)}) collective-permute-start(bf16[2,240,384]{2,1,0:T(8,128)(2,1)S(1)} %shard_map.115.refs_4_.refs_5_), channel_id=1, source_target_pairs={{8,16},{10,18},{12,20},{14,22},{16,8},{18,10},{20,12},{22,14},{9,1... | collective-permute-start | bytes 1105928 | tf_op jit(solution)/shard_map/rest_middle/ppermute | solution.py:494
  18.2 34.1 %copy-start.6 = (bf16[4,144,384]{2,1,0:T(8,128)(2,1)}, bf16[4,144,384]{2,1,0:T(8,128)(2,1)S(1)}, u32[]{:S(2)}) copy-start(bf16[4,144,384]{2,1,0:T(8,128)(2,1)S(1)} %shard_map.114.refs_2_) | copy-start | bytes 1327108
  18.2 20.9 %collective-permute-start.4 = (bf16[4,144,384]{2,1,0:T(8,128)(2,1)S(1)}, bf16[4,144,384]{2,1,0:T(8,128)(2,1)S(1)}, u32[]{:S(2)}, u32[]{:S(2)}) collective-permute-start(bf16[4,144,384]{2,1,0:T(8,128)(2,1)S(1)} %shard_map.114.refs_2_), channel_id=1, source_target_pairs={{0,1},{1,0},{2,6},{3,7},{4,5},{5,4},{6,2},{7,3},{8,9},{9,8},{10,14... | collective-permute-start | bytes 1327112 | tf_op jit(solution)/shard_map/cross_1/ppermute | solution.py:472
  19.8 19.4 %collective-permute-start.5 = (bf16[4,144,384]{2,1,0:T(8,128)(2,1)S(1)}, bf16[4,144,384]{2,1,0:T(8,128)(2,1)}, u32[]{:S(2)}, u32[]{:S(2)}) collective-permute-start(bf16[4,144,384]{2,1,0:T(8,128)(2,1)S(1)} %shard_map.114.refs_2_), channel_id=1, source_target_pairs={{0,4},{1,5},{2,3},{3,2},{4,0},{5,1},{6,7},{7,6},{8,12},{9,13},{10,... | collective-permute-start | bytes 1327112 | tf_op jit(solution)/shard_map/cross_2/ppermute | solution.py:472
  21.3 17.0 %collective-permute-start.6 = (bf16[2,240,384]{2,1,0:T(8,128)(2,1)S(1)}, bf16[2,240,384]{2,1,0:T(8,128)(2,1)S(1)}, u32[]{:S(2)}, u32[]{:S(2)}) collective-permute-start(bf16[2,240,384]{2,1,0:T(8,128)(2,1)S(1)} %shard_map.115.refs_4_.refs_5_), channel_id=1, source_target_pairs={{0,1},{1,0},{2,6},{3,7},{4,5},{5,4},{6,2},{7,3},{8,9},{9,8},{10,14... | collective-permute-start | bytes 1105928 | tf_op jit(solution)/shard_map/near_1/ppermute | solution.py:472
  21.8 17.2 %collective-permute-start.7 = (bf16[2,240,384]{2,1,0:T(8,128)(2,1)S(1)}, bf16[2,240,384]{2,1,0:T(8,128)(2,1)S(1)}, u32[]{:S(2)}, u32[]{:S(2)}) collective-permute-start(bf16[2,240,384]{2,1,0:T(8,128)(2,1)S(1)} %shard_map.115.refs_4_.refs_5_), channel_id=1, source_target_pairs={{0,4},{1,5},{2,3},{3,2},{4,0},{5,1},{6,7},{7,6},{8,12},{9,13},{10,... | collective-permute-start | bytes 1105928 | tf_op jit(solution)/shard_map/near_2/ppermute | solution.py:472
  22.3 16.8 %all-to-all-start = ((bf16[16,8,768]{2,1,0:T(8,128)(2,1)}), bf16[16,8,768]{2,1,0:T(8,128)(2,1)S(1)}, u32[]{:S(2)}, u32[]{:S(2)}) async-start(bf16[16,8,768]{2,1,0:T(8,128)(2,1)} %bitcast.12), calls=%async_computation | async-start | bytes 393216 | tf_op jit(solution)/shard_map/all_to_all | solution.py:499
  28.3 14.3 %collective-permute-start.9 = (bf16[2,240,384]{2,1,0:T(8,128)(2,1)S(1)}, bf16[2,240,384]{2,1,0:T(8,128)(2,1)S(1)}, u32[]{:S(2)}, u32[]{:S(2)}) collective-permute-start(bf16[2,240,384]{2,1,0:T(8,128)(2,1)S(1)} %collective-permute-done.8.first_ref), channel_id=1, source_target_pairs={{8,0},{10,2},{12,4},{14,6},{16,24},{18,26},{20,28},{22,30},{9,1},{... | collective-permute-start | bytes 1105928 | tf_op jit(solution)/shard_map/rest_onward/ppermute | solution.py:497
  39.1 13.3 %copy-start.8 = (bf16[4,144,384]{2,1,0:T(8,128)(2,1)}, bf16[4,144,384]{2,1,0:T(8,128)(2,1)S(1)}, u32[]{:S(2)}) copy-start(bf16[4,144,384]{2,1,0:T(8,128)(2,1)S(1)} %collective-permute-done.4.refs_3_) | copy-start | bytes 1327108
  42.6 0.7 copy-start.10
  43.3 8.4 %collective-permute-start.10 = (bf16[4,144,384]{2,1,0:T(8,128)(2,1)S(1)}, bf16[4,144,384]{2,1,0:T(8,128)(2,1)}, u32[]{:S(2)}, u32[]{:S(2)}) collective-permute-start(bf16[4,144,384]{2,1,0:T(8,128)(2,1)S(1)} %collective-permute-done.4.refs_3_), channel_id=1, source_target_pairs={{0,4},{1,5},{2,3},{3,2},{4,0},{5,1},{6,7},{7,6},{8,12},{9,13},{10,... | collective-permute-start | bytes 1327112 | tf_op jit(solution)/shard_map/cross_3/ppermute | solution.py:472
  44.8 7.6 %collective-permute-start.12 = (bf16[4,144,384]{2,1,0:T(8,128)(2,1)S(1)}, bf16[4,144,384]{2,1,0:T(8,128)(2,1)}, u32[]{:S(2)}, u32[]{:S(2)}) collective-permute-start(bf16[4,144,384]{2,1,0:T(8,128)(2,1)S(1)} %collective-permute-done.4.refs_3_), channel_id=1, source_target_pairs={{0,2},{2,0},{4,6},{6,4},{8,10},{10,8},{12,14},{14,12},{16,18},{18,... | collective-permute-start | bytes 1327112 | tf_op jit(solution)/shard_map/cross_core/ppermute | solution.py:345
  44.8 7.5 %collective-permute-start.11 = (bf16[4,144,384]{2,1,0:T(8,128)(2,1)S(1)}, bf16[4,144,384]{2,1,0:T(8,128)(2,1)}, u32[]{:S(2)}, u32[]{:S(2)}) collective-permute-start(bf16[4,144,384]{2,1,0:T(8,128)(2,1)S(1)} %shard_map.114.refs_2_), channel_id=1, source_target_pairs={{0,2},{2,0},{4,6},{6,4},{8,10},{10,8},{12,14},{14,12},{16,18},{18,... | collective-permute-start | bytes 1327112 | tf_op jit(solution)/shard_map/cross_core/ppermute | solution.py:345
  45.3 8.6 %collective-permute-start.13 = (bf16[4,144,384]{2,1,0:T(8,128)(2,1)}, bf16[4,144,384]{2,1,0:T(8,128)(2,1)}, u32[]{:S(2)}, u32[]{:S(2)}) collective-permute-start(bf16[4,144,384]{2,1,0:T(8,128)(2,1)} %collective-permute-done.5.refs_4_), channel_id=1, source_target_pairs={{0,2},{2,0},{4,6},{6,4},{8,10},{10,8},{12,14},{14,12},{16,18},{18,... | collective-permute-start | bytes 1327112 | tf_op jit(solution)/shard_map/cross_core/ppermute | solution.py:345
  45.3 1.0 copy-start.11
  51.7 3.7 %collective-permute-start.14 = (bf16[4,144,384]{2,1,0:T(8,128)(2,1)}, bf16[4,144,384]{2,1,0:T(8,128)(2,1)}, u32[]{:S(2)}, u32[]{:S(2)}) collective-permute-start(bf16[4,144,384]{2,1,0:T(8,128)(2,1)} %collective-permute-done.10.refs_5_), channel_id=1, source_target_pairs={{0,2},{2,0},{4,6},{6,4},{8,10},{10,8},{12,14},{14,12},{16,18},{18,... | collective-permute-start | bytes 1327112 | tf_op jit(solution)/shard_map/cross_core/ppermute | solution.py:345
  51.8 13.3 %collective-permute-start.17 = (bf16[2,240,384]{2,1,0:T(8,128)(2,1)S(1)}, bf16[2,240,384]{2,1,0:T(8,128)(2,1)S(1)}, u32[]{:S(2)}, u32[]{:S(2)}) collective-permute-start(bf16[2,240,384]{2,1,0:T(8,128)(2,1)S(1)} %shard_map.115.refs_4_.refs_5_), channel_id=1, source_target_pairs={{0,2},{2,0},{4,6},{6,4},{8,10},{10,8},{12,14},{14,12},{16,18},{18,... | collective-permute-start | bytes 1105928 | tf_op jit(solution)/shard_map/near_core/ppermute | solution.py:345
  52.3 18.9 %collective-permute-start.19 = (bf16[2,240,384]{2,1,0:T(8,128)(2,1)S(1)}, bf16[2,240,384]{2,1,0:T(8,128)(2,1)S(1)}, u32[]{:S(2)}, u32[]{:S(2)}) collective-permute-start(bf16[2,240,384]{2,1,0:T(8,128)(2,1)S(1)} %collective-permute-done.7.refs_6_.refs_7_), channel_id=1, source_target_pairs={{0,2},{2,0},{4,6},{6,4},{8,10},{10,8},{12,14},{14,12},{16,18},{18,... | collective-permute-start | bytes 1105928 | tf_op jit(solution)/shard_map/near_core/ppermute | solution.py:345
  52.4 10.9 %collective-permute-start.15 = (bf16[2,240,384]{2,1,0:T(8,128)(2,1)S(1)}, bf16[2,240,384]{2,1,0:T(8,128)(2,1)S(1)}, u32[]{:S(2)}, u32[]{:S(2)}) collective-permute-start(bf16[2,240,384]{2,1,0:T(8,128)(2,1)S(1)} %shard_map.116.refs_12_.refs_13_), channel_id=1, source_target_pairs={{0,1},{1,0},{2,6},{3,7},{4,5},{5,4},{6,2},{7,3},{8,9},{9,8},{10,14... | collective-permute-start | bytes 1105928 | tf_op jit(solution)/shard_map/far_1/ppermute | solution.py:472
  53.9 16.9 %collective-permute-start.21 = (bf16[2,240,384]{2,1,0:T(8,128)(2,1)S(1)}, bf16[2,240,384]{2,1,0:T(8,128)(2,1)S(1)}, u32[]{:S(2)}, u32[]{:S(2)}) collective-permute-start(bf16[2,240,384]{2,1,0:T(8,128)(2,1)S(1)} %shard_map.116.refs_12_.refs_13_), channel_id=1, source_target_pairs={{0,4},{1,5},{2,3},{3,2},{4,0},{5,1},{6,7},{7,6},{8,12},{9,13},{10,... | collective-permute-start | bytes 1105928 | tf_op jit(solution)/shard_map/far_2/ppermute | solution.py:472
  55.4 16.0 %collective-permute-start.23 = (bf16[2,240,384]{2,1,0:T(8,128)(2,1)S(1)}, bf16[2,240,384]{2,1,0:T(8,128)(2,1)}, u32[]{:S(2)}, u32[]{:S(2)}) collective-permute-start(bf16[2,240,384]{2,1,0:T(8,128)(2,1)S(1)} %shard_map.116.refs_12_.refs_13_), channel_id=1, source_target_pairs={{0,2},{2,0},{4,6},{6,4},{8,10},{10,8},{12,14},{14,12},{16,18},{18,... | collective-permute-start | bytes 1105928 | tf_op jit(solution)/shard_map/far_core/ppermute | solution.py:345
  55.4 1.0 copy-start.7
  56.4 1.0 copy-start.9
  61.8 0.7 copy-start.5
  63.3 8.5 %collective-permute-start.16 = (bf16[2,240,384]{2,1,0:T(8,128)(2,1)S(1)}, bf16[2,240,384]{2,1,0:T(8,128)(2,1)}, u32[]{:S(2)}, u32[]{:S(2)}) collective-permute-start(bf16[2,240,384]{2,1,0:T(8,128)(2,1)S(1)} %collective-permute-done.6.refs_5_.refs_6_), channel_id=1, source_target_pairs={{0,4},{1,5},{2,3},{3,2},{4,0},{5,1},{6,7},{7,6},{8,12},{9,13},{10,... | collective-permute-start | bytes 1105928 | tf_op jit(solution)/shard_map/near_3/ppermute | solution.py:472
  65.1 10.3 %collective-permute-start.22 = (bf16[2,240,384]{2,1,0:T(8,128)(2,1)S(1)}, bf16[2,240,384]{2,1,0:T(8,128)(2,1)}, u32[]{:S(2)}, u32[]{:S(2)}) collective-permute-start(bf16[2,240,384]{2,1,0:T(8,128)(2,1)S(1)} %collective-permute-done.15.refs_13_.refs_14_), channel_id=1, source_target_pairs={{0,4},{1,5},{2,3},{3,2},{4,0},{5,1},{6,7},{7,6},{8,12},{9,13},{10,... | collective-permute-start | bytes 1105928 | tf_op jit(solution)/shard_map/far_3/ppermute | solution.py:472
  65.3 14.4 %all-to-all-start.1 = ((bf16[16,8,768]{2,1,0:T(8,128)(2,1)}), bf16[16,8,768]{2,1,0:T(8,128)(2,1)S(1)}, u32[]{:S(2)}, u32[]{:S(2)}) async-start(bf16[16,8,768]{2,1,0:T(8,128)(2,1)} %bitcast.20), calls=%async_computation.1 | async-start | bytes 393216 | tf_op jit(solution)/shard_map/all_to_all | solution.py:525
  70.8 12.3 %copy-start.3 = (bf16[2,240,384]{2,1,0:T(8,128)(2,1)}, bf16[2,240,384]{2,1,0:T(8,128)(2,1)S(1)}, u32[]{:S(2)}) copy-start(bf16[2,240,384]{2,1,0:T(8,128)(2,1)S(1)} %collective-permute-done.21.refs_14_.refs_15_) | copy-start | bytes 1105924
  70.8 4.7 %collective-permute-start.25 = (bf16[2,240,384]{2,1,0:T(8,128)(2,1)S(1)}, bf16[2,240,384]{2,1,0:T(8,128)(2,1)}, u32[]{:S(2)}, u32[]{:S(2)}) collective-permute-start(bf16[2,240,384]{2,1,0:T(8,128)(2,1)S(1)} %collective-permute-done.21.refs_14_.refs_15_), channel_id=1, source_target_pairs={{0,2},{2,0},{4,6},{6,4},{8,10},{10,8},{12,14},{14,12},{16,18},{18,... | collective-permute-start | bytes 1105928 | tf_op jit(solution)/shard_map/far_core/ppermute | solution.py:345
  71.3 4.2 %collective-permute-start.18 = (bf16[2,240,384]{2,1,0:T(8,128)(2,1)S(1)}, bf16[2,240,384]{2,1,0:T(8,128)(2,1)}, u32[]{:S(2)}, u32[]{:S(2)}) collective-permute-start(bf16[2,240,384]{2,1,0:T(8,128)(2,1)S(1)} %collective-permute-done.6.refs_5_.refs_6_), channel_id=1, source_target_pairs={{0,2},{2,0},{4,6},{6,4},{8,10},{10,8},{12,14},{14,12},{16,18},{18,... | collective-permute-start | bytes 1105928 | tf_op jit(solution)/shard_map/near_core/ppermute | solution.py:345
  71.4 4.1 %collective-permute-start.24 = (bf16[2,240,384]{2,1,0:T(8,128)(2,1)S(1)}, bf16[2,240,384]{2,1,0:T(8,128)(2,1)}, u32[]{:S(2)}, u32[]{:S(2)}) collective-permute-start(bf16[2,240,384]{2,1,0:T(8,128)(2,1)S(1)} %collective-permute-done.15.refs_13_.refs_14_), channel_id=1, source_target_pairs={{0,2},{2,0},{4,6},{6,4},{8,10},{10,8},{12,14},{14,12},{16,18},{18,... | collective-permute-start | bytes 1105928 | tf_op jit(solution)/shard_map/far_core/ppermute | solution.py:345
  71.8 8.0 %collective-permute-start.20 = (bf16[2,240,384]{2,1,0:T(8,128)(2,1)}, bf16[2,240,384]{2,1,0:T(8,128)(2,1)}, u32[]{:S(2)}, u32[]{:S(2)}) collective-permute-start(bf16[2,240,384]{2,1,0:T(8,128)(2,1)} %collective-permute-done.16.refs_7_.refs_8_), channel_id=1, source_target_pairs={{0,2},{2,0},{4,6},{6,4},{8,10},{10,8},{12,14},{14,12},{16,18},{18,... | collective-permute-start | bytes 1105928 | tf_op jit(solution)/shard_map/near_core/ppermute | solution.py:345
  75.4 4.4 %collective-permute-start.26 = (bf16[2,240,384]{2,1,0:T(8,128)(2,1)}, bf16[2,240,384]{2,1,0:T(8,128)(2,1)}, u32[]{:S(2)}, u32[]{:S(2)}) collective-permute-start(bf16[2,240,384]{2,1,0:T(8,128)(2,1)} %collective-permute-done.22.refs_15_.refs_16_), channel_id=1, source_target_pairs={{0,2},{2,0},{4,6},{6,4},{8,10},{10,8},{12,14},{14,12},{16,18},{18,... | collective-permute-start | bytes 1105928 | tf_op jit(solution)/shard_map/far_core/ppermute | solution.py:345
  79.8 1.0 copy-start.15
  83.1 6.6 %collective-permute-start.27 = (bf16[128,768]{1,0:T(8,128)(2,1)S(1)}, bf16[128,768]{1,0:T(8,128)(2,1)S(1)}, u32[]{:S(2)}, u32[]{:S(2)}) collective-permute-start(bf16[128,768]{1,0:T(8,128)(2,1)S(1)} %get-tuple-element.61.refs_1_), channel_id=1, source_target_pairs={{0,1},{1,0},{2,3},{3,2},{4,5},{5,4},{6,7},{7,6},{8,9},{9,8},{10,11... | collective-permute-start | bytes 589832 | tf_op jit(solution)/shard_map/normed2_x/ppermute | solution.py:349
  89.7 1.0 copy-start.4
  90.7 10.6 %copy-start.1 = (bf16[768,1536]{1,0:T(8,128)(2,1)S(1)}, bf16[768,1536]{1,0:T(8,128)(2,1)}, u32[]{:S(2)}) copy-start(bf16[768,1536]{1,0:T(8,128)(2,1)} %up_ref.1) | copy-start | bytes 7077892
  90.7 10.6 %copy-start.2 = (bf16[1536,768]{1,0:T(8,128)(2,1)S(1)}, bf16[1536,768]{1,0:T(8,128)(2,1)}, u32[]{:S(2)}) copy-start(bf16[1536,768]{1,0:T(8,128)(2,1)} %down_ref.1) | copy-start | bytes 7077892
  95.6 5.7 %collective-permute-start.28 = (bf16[128,768]{1,0:T(8,128)(2,1)S(1)}, bf16[128,768]{1,0:T(8,128)(2,1)S(1)}, u32[]{:S(2)}, u32[]{:S(2)}) collective-permute-start(bf16[128,768]{1,0:T(8,128)(2,1)S(1)} %get-tuple-element.64.own_ref), channel_id=1, source_target_pairs={{0,1},{1,0},{2,3},{3,2},{4,5},{5,4},{6,7},{7,6},{8,9},{9,8},{10,11... | collective-permute-start | bytes 589832 | tf_op jit(solution)/shard_map/normed3_x/ppermute | solution.py:349
  103.0 5.8 %collective-permute-start.29 = (bf16[128,768]{1,0:T(8,128)(2,1)S(1)}, bf16[128,768]{1,0:T(8,128)(2,1)S(1)}, u32[]{:S(2)}, u32[]{:S(2)}) collective-permute-start(bf16[128,768]{1,0:T(8,128)(2,1)S(1)} %get-tuple-element.67), channel_id=1, source_target_pairs={{0,1},{1,0},{2,3},{3,2},{4,5},{5,4},{6,7},{7,6},{8,9},{9,8},{10,11... | collective-permute-start | bytes 589832 | tf_op jit(solution)/shard_map/part_x/ppermute | solution.py:349
  104.6 4.2 %collective-permute-start.30 = (f32[1,128]{1,0:T(1,128)S(1)}, f32[1,128]{1,0:T(1,128)S(1)}, u32[]{:S(2)}, u32[]{:S(2)}) collective-permute-start(f32[1,128]{1,0:T(1,128)S(1)} %get-tuple-element.68.own_head_ref), channel_id=1, source_target_pairs={{0,1},{1,0},{2,3},{3,2},{4,5},{5,4},{6,7},{7,6},{8,9},{9,8},{10,11... | collective-permute-start | bytes 1544 | tf_op jit(solution)/shard_map/head_x/ppermute | solution.py:349

commit v5 on v4

--- a/solution.py
+++ b/solution.py
@@ -320,22 +320,26 @@
     normed_ref[...] = rms(stream, gains_ref[1:2])
 
 
-def depth_kernel(*refs, plan, chunk, count):
-    place_ref, own_ref, peer_ref, stream_ref, gains_ref = refs[:5]
-    near_refs, far_refs = refs[5:13], refs[13:21]
-    out_ref, normed_ref, held_ref, out_held_ref = refs[21:]
+def depth_own_kernel(*refs, chunk, count):
+    place_ref, own_ref = refs[:2]
+    near_refs, far_refs, (q_ref, kv_ref, held_ref, out_held_ref) = refs[2:10], refs[10:18], refs[18:]
     width = own_ref.shape[1]
     assemble_both(place_ref, near_refs, far_refs, held_ref, 0, chunk)
     assemble_both(place_ref, near_refs, far_refs, out_held_ref, chunk + count, count)
     own = own_ref[...]
-    both = jnp.concatenate([own, peer_ref[...]], axis=0)
-    q = project(own, held_ref[:width]) * BF16(HDIM**-0.5)
-    k = project(both, held_ref[width : 2 * width])
-    v = project(both, held_ref[2 * width :])
+    q_ref[...] = project(own, held_ref[:width]) * BF16(HDIM**-0.5)
+    kv_ref[...] = project(own, held_ref[width:])
+
+
+def depth_kernel(
+    peer_ref, stream_ref, gains_ref, q_ref, kv_ref, held_ref, out_held_ref, out_ref, normed_ref, *, plan
+):
+    width = peer_ref.shape[1]
+    kv = jnp.concatenate([kv_ref[...], project(peer_ref[...], held_ref[width:])], axis=0)
     n = plan.rows
     columns = along(2 * n, lambda row: plan.column(row % n))
     bias = bias_where(down(n, plan.column) == columns)
-    mixed = attend_heads(q, k, v, bias, width // HDIM).astype(BF16)
+    mixed = attend_heads(q_ref[...], kv[:, :width], kv[:, width:], bias, width // HDIM).astype(BF16)
     stream = stream_ref[...] + jnp.dot(mixed, out_held_ref[...], preferred_element_type=F32)
     out_ref[...] = stream
     normed_ref[...] = rms(stream, gains_ref[2:3])
@@ -538,12 +542,15 @@
         us=2,
     )(rest_place, mixed, stream, gains, *near_pieces, *far_pieces)
     peer = to_x(normed, "normed2_x")
+    own_side = call(
+        functools.partial(depth_own_kernel, chunk=chunk, count=count),
+        (narrow, shape((rows, 2 * width), BF16), shape((3 * width, width), BF16), shape((width, width), BF16)),
+        [SMEM] + [VMEM] * 17,
+        us=5,
+    )(rest_place, normed, *near_pieces, *far_pieces)
     stream, normed = call(
-        functools.partial(depth_kernel, plan=plan, chunk=chunk, count=count),
-        (wide, narrow),
-        [SMEM] + [VMEM] * 20,
-        [pltpu.VMEM((3 * width, width), BF16), pltpu.VMEM((width, width), BF16)],
-    )(rest_place, normed, peer, stream, gains, *near_pieces, *far_pieces)
+        functools.partial(depth_kernel, plan=plan), (wide, narrow), [VMEM] * 7, us=3
+    )(peer, stream, gains, *own_side)
     peer = to_x(normed, "normed3_x")
     own_part, peer_part, own_head, peer_head = call(
         mlp_kernel, (narrow, narrow, row, row), [VMEM] * 6

time: 111 us -> 110 us (level)
  waiting for transfers between devices: 42.6 us -> 39.6 us
  local copies, waits for them, and re-layouts: 9.84 us -> 12.4 us
    ppermute x4, waiting for transfers between devices: 12.3 us -> 9.06 us  [swap_x(): return lax.ppermute(a, 'gz', [(0, 1), (1, 0)])]
    unnamed x32 -> x40, local copies, waits for them, and re-layouts: 8.97 us -> 11.5 us
    pallas_call x1 -> x2, Pallas kernels: 4.87 us -> 5.03 us  [the longest x1 3.22 us: fast_body(): call(functools.partial(depth_own_kernel, chunk=chunk, count=count), (narr...]
  transfers between devices with their start and end apart: 33 -> 33, of which waited for: 13 -> 13; matrix products, arithmetic and copies ran while one was open for 3% -> 3% of each run, Pallas kernels for 5% -> 8%
where the time goes in v5:
time: 110 us
  waiting for transfers between devices  39.6 us (36%)
  starting transfers between devices  38 us (35%)
  Pallas kernels  15.6 us (14%)
  local copies, waits for them, and re-layouts  12.4 us (11%)
  other arithmetic  2.5 us (2%)
  between operations  1.5 us (1%)
    ppermute x9, waiting for transfers between devices, cross_over(): return lax.ppermute(a, ('gx', 'gz'), pairs)  18.6 us
    unnamed x40, local copies, waits for them, and re-layouts  11.5 us
    ppermute x9, starting transfers between devices, cross_over(): return lax.ppermute(a, ('gx', 'gz'), pairs)  10.6 us
    ppermute x4, waiting for transfers between devices, swap_x(): return lax.ppermute(a, 'gz', [(0, 1), (1, 0)])  9.06 us
    ppermute x16, starting transfers between devices, shift(): return lax.ppermute(a, 'gx', [(i, i ^ step) for i in range(peers)])  8.84 us
    all_to_all x1, starting transfers between devices, fast_body(): lax.all_to_all(normed.reshape(peers, rows // peers, width), 'gx', split_a...  5.94 us
    all_to_all x1, starting transfers between devices, fast_body(): lax.all_to_all(mixed.reshape(peers, rows // peers, width), 'gx', split_ax...  5.46 us
    ppermute x4, starting transfers between devices, swap_x(): return lax.ppermute(a, 'gz', [(0, 1), (1, 0)])  5.2 us
  transfers between devices with their start and end apart: 33, of which 13 were waited for; matrix products, arithmetic and copies ran while one was open for 3% of the time, Pallas kernels for 8%

profile of v5, /device:TPU:0, one launch (start us, length us, event | category | flops | bytes accessed | tf_op | source)
XLA Modules:
  0.0 109.6 jit_solution(2112412873784134431)
XLA Ops:
  0.6 0.9 copy-done
  1.6 3.1 %collective-permute-start = (bf16[144,384]{1,0:T(8,128)(2,1)S(1)}, bf16[144,384]{1,0:T(8,128)(2,1)S(1)}, u32[]{:S(2)}, u32[]{:S(2)}) collective-permute-start(bf16[144,384]{1,0:T(8,128)(2,1)S(1)} %dynamic-slice_bitcast_fusion.refs_0_), channel_id=1, source_target_pairs={{0,8},{2,10},{4,12},{6,14},{8,0},{10,2},{12,4},{14,6},{16,24},{18,... | collective-permute-start | bytes 331784 | tf_op jit(solution)/shard_map/cross_z1/ppermute | solution.py:349
  4.7 2.6 %collective-permute-start.1 = (bf16[144,384]{1,0:T(8,128)(2,1)S(1)}, bf16[144,384]{1,0:T(8,128)(2,1)S(1)}, u32[]{:S(2)}, u32[]{:S(2)}) collective-permute-start(bf16[144,384]{1,0:T(8,128)(2,1)S(1)} %dynamic-slice_bitcast_fusion.refs_0_), channel_id=1, source_target_pairs={{0,16},{2,18},{4,20},{6,22},{8,24},{10,26},{12,28},{14,30},{16,0},... | collective-permute-start | bytes 331784 | tf_op jit(solution)/shard_map/cross_z2/ppermute | solution.py:349
  7.3 0.9 fusion.1.refs_0_
  8.2 1.0 collective-permute-start.3
  9.2 1.5 %cosine_select_fusion.encoding_ref = f32[128,768]{1,0:T(8,128)S(1)} fusion(f32[768]{0:T(1024)S(1)} %fusion.10, s32[128]{0:T(128)S(1)} %fusion.17, s32[128]{0:T(128)S(1)} %get-tuple-element.81, s32[128]{0:T(128)S(1)} %get-tuple-element.80, pred[768]{0:T(1024)(128)(4,1)S(1)} %broadcast_compare_fusion.1, pred[768]{0:T(1024)(128)(4,1)S(1)} %get-tuple-element.83, ...), kind=kLoop, calls=%fused_computation | loop fusion | flops 491520 | bytes 400128 | tf_op jit(solution)/shard_map/encoding/jit(_where)/select_n | solution.py:464
  10.8 0.7 reshape.94.head_ref
  11.5 0.9 copy-done.16
  12.4 0.7 copy-done.17
  13.1 1.0 shard_map.113
  14.1 2.0 %collective-permute-done.1.refs_2_ = bf16[144,384]{1,0:T(8,128)(2,1)S(1)} collective-permute-done((bf16[144,384]{1,0:T(8,128)(2,1)S(1)}, bf16[144,384]{1,0:T(8,128)(2,1)S(1)}, u32[]{:S(2)}, u32[]{:S(2)}) %collective-permute-start.1) | collective-permute-done | bytes 110624 | tf_op jit(solution)/shard_map/cross_z2/ppermute | solution.py:349
  16.0 1.4 %collective-permute-done.3.refs_1_ = bf16[240,384]{1,0:T(8,128)(2,1)S(1)} collective-permute-done((bf16[240,384]{1,0:T(8,128)(2,1)S(1)}, bf16[240,384]{1,0:T(8,128)(2,1)S(1)}, u32[]{:S(2)}, u32[]{:S(2)}) %collective-permute-start.3) | collective-permute-done | bytes 184352 | tf_op jit(solution)/shard_map/rest_z1/ppermute | solution.py:349
  17.4 0.7 collective-permute-start.8
  18.2 1.6 %collective-permute-start.4 = (bf16[4,144,384]{2,1,0:T(8,128)(2,1)S(1)}, bf16[4,144,384]{2,1,0:T(8,128)(2,1)S(1)}, u32[]{:S(2)}, u32[]{:S(2)}) collective-permute-start(bf16[4,144,384]{2,1,0:T(8,128)(2,1)S(1)} %shard_map.114.refs_2_), channel_id=1, source_target_pairs={{0,1},{1,0},{2,6},{3,7},{4,5},{5,4},{6,2},{7,3},{8,9},{9,8},{10,14... | collective-permute-start | bytes 1327112 | tf_op jit(solution)/shard_map/cross_1/ppermute | solution.py:476
  19.8 1.5 %collective-permute-start.5 = (bf16[4,144,384]{2,1,0:T(8,128)(2,1)S(1)}, bf16[4,144,384]{2,1,0:T(8,128)(2,1)S(1)}, u32[]{:S(2)}, u32[]{:S(2)}) collective-permute-start(bf16[4,144,384]{2,1,0:T(8,128)(2,1)S(1)} %shard_map.114.refs_2_), channel_id=1, source_target_pairs={{0,4},{1,5},{2,3},{3,2},{4,0},{5,1},{6,7},{7,6},{8,12},{9,13},{10,... | collective-permute-start | bytes 1327112 | tf_op jit(solution)/shard_map/cross_2/ppermute | solution.py:476
  21.3 0.5 collective-permute-start.6
  21.8 0.5 collective-permute-start.7
  22.3 5.9 %all-to-all-start = ((bf16[16,8,768]{2,1,0:T(8,128)(2,1)}), bf16[16,8,768]{2,1,0:T(8,128)(2,1)S(1)}, u32[]{:S(2)}, u32[]{:S(2)}) async-start(bf16[16,8,768]{2,1,0:T(8,128)(2,1)} %bitcast.12), calls=%async_computation | async-start | bytes 393216 | tf_op jit(solution)/shard_map/all_to_all | solution.py:503
  28.3 1.3 %collective-permute-start.9 = (bf16[2,240,384]{2,1,0:T(8,128)(2,1)S(1)}, bf16[2,240,384]{2,1,0:T(8,128)(2,1)S(1)}, u32[]{:S(2)}, u32[]{:S(2)}) collective-permute-start(bf16[2,240,384]{2,1,0:T(8,128)(2,1)S(1)} %collective-permute-done.8.first_ref), channel_id=1, source_target_pairs={{8,0},{10,2},{12,4},{14,6},{16,24},{18,26},{20,28},{22,30},{9,1},{... | collective-permute-start | bytes 1105928 | tf_op jit(solution)/shard_map/rest_onward/ppermute | solution.py:501
  29.6 0.7 copy-done.12
  30.3 8.1 %collective-permute-done.6.refs_5_.refs_3_ = bf16[2,240,384]{2,1,0:T(8,128)(2,1)} collective-permute-done((bf16[2,240,384]{2,1,0:T(8,128)(2,1)S(1)}, bf16[2,240,384]{2,1,0:T(8,128)(2,1)}, u32[]{:S(2)}, u32[]{:S(2)}) %collective-permute-start.6) | collective-permute-done | bytes 368672 | tf_op jit(solution)/shard_map/near_1/ppermute | solution.py:476
  38.4 0.6 collective-permute-done.7.refs_6_.refs_4_
  39.0 0.1 all-to-all-done
  39.1 3.4 %collective-permute-done.9.second_ref = bf16[2,240,384]{2,1,0:T(8,128)(2,1)S(1)} collective-permute-done((bf16[2,240,384]{2,1,0:T(8,128)(2,1)S(1)}, bf16[2,240,384]{2,1,0:T(8,128)(2,1)S(1)}, u32[]{:S(2)}, u32[]{:S(2)}) %collective-permute-start.9) | collective-permute-done | bytes 368672 | tf_op jit(solution)/shard_map/rest_onward/ppermute | solution.py:501
  42.6 0.8 copy-done.14
  43.3 1.5 %collective-permute-start.10 = (bf16[4,144,384]{2,1,0:T(8,128)(2,1)S(1)}, bf16[4,144,384]{2,1,0:T(8,128)(2,1)S(1)}, u32[]{:S(2)}, u32[]{:S(2)}) collective-permute-start(bf16[4,144,384]{2,1,0:T(8,128)(2,1)S(1)} %collective-permute-done.4.refs_3_), channel_id=1, source_target_pairs={{0,4},{1,5},{2,3},{3,2},{4,0},{5,1},{6,7},{7,6},{8,12},{9,13},{10,... | collective-permute-start | bytes 1327112 | tf_op jit(solution)/shard_map/cross_3/ppermute | solution.py:476
  44.8 0.5 collective-permute-start.11
  45.3 1.0 copy-done.13
  46.3 1.0 copy-done.15
  47.4 0.8 copy-done.6
  48.1 3.5 %collective-permute-done.10.refs_5_ = bf16[4,144,384]{2,1,0:T(8,128)(2,1)S(1)} collective-permute-done((bf16[4,144,384]{2,1,0:T(8,128)(2,1)S(1)}, bf16[4,144,384]{2,1,0:T(8,128)(2,1)S(1)}, u32[]{:S(2)}, u32[]{:S(2)}) %collective-permute-start.10) | collective-permute-done | bytes 442400 | tf_op jit(solution)/shard_map/cross_3/ppermute | solution.py:476
  51.7 0.5 collective-permute-start.17
  52.2 0.1 collective-permute-start.19
  52.3 1.5 %collective-permute-start.15 = (bf16[2,240,384]{2,1,0:T(8,128)(2,1)}, bf16[2,240,384]{2,1,0:T(8,128)(2,1)}, u32[]{:S(2)}, u32[]{:S(2)}) collective-permute-start(bf16[2,240,384]{2,1,0:T(8,128)(2,1)} %copy-done.6), channel_id=1, source_target_pairs={{0,1},{1,0},{2,6},{3,7},{4,5},{5,4},{6,2},{7,3},{8,9},{9,8},{10,14... | collective-permute-start | bytes 1105928 | tf_op jit(solution)/shard_map/far_1/ppermute | solution.py:476
  53.8 1.5 %collective-permute-start.21 = (bf16[2,240,384]{2,1,0:T(8,128)(2,1)}, bf16[2,240,384]{2,1,0:T(8,128)(2,1)}, u32[]{:S(2)}, u32[]{:S(2)}) collective-permute-start(bf16[2,240,384]{2,1,0:T(8,128)(2,1)} %copy-done.6), channel_id=1, source_target_pairs={{0,4},{1,5},{2,3},{3,2},{4,0},{5,1},{6,7},{7,6},{8,12},{9,13},{10,... | collective-permute-start | bytes 1105928 | tf_op jit(solution)/shard_map/far_2/ppermute | solution.py:476
  55.3 4.6 %shard_map.117 = bf16[128,768]{1,0:T(8,128)(2,1)} custom-call(s32[7]{0:T(128)S(1)} %stack.48.refs_0_, bf16[128,768]{1,0:T(8,128)(2,1)S(1)} %bitcast.19, bf16[4,144,384]{2,1,0:T(8,128)(2,1)S(1)} %shard_map.114.refs_2_, bf16[4,144,384]{2,1,0:T(8,128)(2,1)S(1)} %collective-permute-done.4.refs_3_, bf16[4,144,384]{2,1,0:T(8,128)(2,1)S(1)} %collective-permute-done.5.refs_4_, ...), custom_call_target="tpu_custom_call" | custom-call | flops 30000001024 | bytes 90000000 | tf_op jit(solution)/shard_map/pallas_call | solution.py:521
  59.9 3.7 %collective-permute-done.15.refs_13_.refs_11_ = bf16[2,240,384]{2,1,0:T(8,128)(2,1)} collective-permute-done((bf16[2,240,384]{2,1,0:T(8,128)(2,1)}, bf16[2,240,384]{2,1,0:T(8,128)(2,1)}, u32[]{:S(2)}, u32[]{:S(2)}) %collective-permute-start.15) | collective-permute-done | bytes 368672 | tf_op jit(solution)/shard_map/far_1/ppermute | solution.py:476
  63.5 1.8 %collective-permute-start.16 = (bf16[2,240,384]{2,1,0:T(8,128)(2,1)}, bf16[2,240,384]{2,1,0:T(8,128)(2,1)S(1)}, u32[]{:S(2)}, u32[]{:S(2)}) collective-permute-start(bf16[2,240,384]{2,1,0:T(8,128)(2,1)} %collective-permute-done.6.refs_5_.refs_3_), channel_id=1, source_target_pairs={{0,4},{1,5},{2,3},{3,2},{4,0},{5,1},{6,7},{7,6},{8,12},{9,13},{10,... | collective-permute-start | bytes 1105928 | tf_op jit(solution)/shard_map/near_3/ppermute | solution.py:476
  65.3 0.7 copy-done.9
  66.0 0.2 collective-permute-start.22
  66.3 5.5 %all-to-all-start.1 = ((bf16[16,8,768]{2,1,0:T(8,128)(2,1)}), bf16[16,8,768]{2,1,0:T(8,128)(2,1)S(1)}, u32[]{:S(2)}, u32[]{:S(2)}) async-start(bf16[16,8,768]{2,1,0:T(8,128)(2,1)} %bitcast.14), calls=%async_computation.1 | async-start | bytes 393216 | tf_op jit(solution)/shard_map/all_to_all | solution.py:529
  71.8 0.5 collective-permute-start.25
  72.2 0.1 collective-permute-start.18
  72.3 0.4 collective-permute-start.24
  72.7 0.1 collective-permute-start.20
  72.9 2.7 %collective-permute-done.22.refs_15_.refs_13_ = bf16[2,240,384]{2,1,0:T(8,128)(2,1)S(1)} collective-permute-done((bf16[2,240,384]{2,1,0:T(8,128)(2,1)}, bf16[2,240,384]{2,1,0:T(8,128)(2,1)S(1)}, u32[]{:S(2)}, u32[]{:S(2)}) %collective-permute-start.22) | collective-permute-done | bytes 368672 | tf_op jit(solution)/shard_map/far_3/ppermute | solution.py:476
  75.6 0.1 stack.45.refs_0_
  75.7 5.1 %all-to-all-done.1 = bf16[16,8,768]{2,1,0:T(8,128)(2,1)S(1)} async-done(((bf16[16,8,768]{2,1,0:T(8,128)(2,1)}), bf16[16,8,768]{2,1,0:T(8,128)(2,1)S(1)}, u32[]{:S(2)}, u32[]{:S(2)}) %all-to-all-start.1) | async-done | bytes 196640 | tf_op jit(solution)/shard_map/all_to_all | solution.py:529
  80.7 1.0 copy-done.4
  81.7 1.0 copy-done.7
  82.7 1.0 copy-done.10
  83.7 1.0 copy-done.19
  84.7 2.1 %shard_map.118 = (f32[128,768]{1,0:T(8,128)S(1)}, bf16[128,768]{1,0:T(8,128)(2,1)S(1)}) custom-call(s32[7]{0:T(128)S(1)} %stack.45.refs_0_, bf16[128,768]{1,0:T(8,128)(2,1)S(1)} %bitcast.20, f32[128,768]{1,0:T(8,128)S(1)} %copy-done.19, f32[3,768]{1,0:T(4,128)S(1)} %get-tuple-element.60.refs_3_.gains_ref, ...), custom_call_target="tpu_custom_call" | custom-call | flops 2000000000 | bytes 6000000 | tf_op jit(solution)/shard_map/pallas_call | solution.py:537
  86.8 1.6 %collective-permute-start.27 = (bf16[128,768]{1,0:T(8,128)(2,1)S(1)}, bf16[128,768]{1,0:T(8,128)(2,1)S(1)}, u32[]{:S(2)}, u32[]{:S(2)}) collective-permute-start(bf16[128,768]{1,0:T(8,128)(2,1)S(1)} %get-tuple-element.65.refs_1_), channel_id=1, source_target_pairs={{0,1},{1,0},{2,3},{3,2},{4,5},{5,4},{6,7},{7,6},{8,9},{9,8},{10,11... | collective-permute-start | bytes 589832 | tf_op jit(solution)/shard_map/normed2_x/ppermute | solution.py:353
  88.4 3.2 %shard_map.119 = (bf16[128,768]{1,0:T(8,128)(2,1)S(1)}, bf16[128,1536]{1,0:T(8,128)(2,1)S(1)}, bf16[2304,768]{1,0:T(8,128)(2,1)S(1)}, bf16[768,768]{1,0:T(8,128)(2,1)S(1)}) custom-call(s32[7]{0:T(128)S(1)} %stack.45.refs_0_, bf16[128,768]{1,0:T(8,128)(2,1)S(1)} %get-tuple-element.65.refs_1_, bf16[2,240,384]{2,1,0:T(8,128)(2,1)S(1)} %shard_map.115.refs_4_.refs_2_, ...), custom_call_target="tpu_custom_call" | custom-call | flops 5000000000 | bytes 15000000 | tf_op jit(solution)/shard_map/pallas_call | solution.py:545
  91.6 1.8 %collective-permute-done.27.peer_ref = bf16[128,768]{1,0:T(8,128)(2,1)S(1)} collective-permute-done((bf16[128,768]{1,0:T(8,128)(2,1)S(1)}, bf16[128,768]{1,0:T(8,128)(2,1)S(1)}, u32[]{:S(2)}, u32[]{:S(2)}) %collective-permute-start.27) | collective-permute-done | bytes 196640 | tf_op jit(solution)/shard_map/normed2_x/ppermute | solution.py:353
  93.4 1.8 %shard_map.120 = (f32[128,768]{1,0:T(8,128)S(1)}, bf16[128,768]{1,0:T(8,128)(2,1)S(1)}) custom-call(bf16[128,768]{1,0:T(8,128)(2,1)S(1)} %collective-permute-done.27.peer_ref, f32[128,768]{1,0:T(8,128)S(1)} %get-tuple-element.66.stream_ref, f32[3,768]{1,0:T(4,128)S(1)} %get-tuple-element.60.refs_3_.gains_ref, bf16[128,768]{1,0:T(8,128)(2,1)S(1)} %get-tuple-element.67.q_ref, ...), custom_call_target="tpu_custom_call" | custom-call | flops 3000000000 | bytes 9000000 | tf_op jit(solution)/shard_map/pallas_call | solution.py:551
  95.2 1.6 %collective-permute-start.28 = (bf16[128,768]{1,0:T(8,128)(2,1)S(1)}, bf16[128,768]{1,0:T(8,128)(2,1)S(1)}, u32[]{:S(2)}, u32[]{:S(2)}) collective-permute-start(bf16[128,768]{1,0:T(8,128)(2,1)S(1)} %get-tuple-element.72.own_ref), channel_id=1, source_target_pairs={{0,1},{1,0},{2,3},{3,2},{4,5},{5,4},{6,7},{7,6},{8,9},{9,8},{10,11... | collective-permute-start | bytes 589832 | tf_op jit(solution)/shard_map/normed3_x/ppermute | solution.py:353
  96.8 4.2 %collective-permute-done.28.peer_ref = bf16[128,768]{1,0:T(8,128)(2,1)S(1)} collective-permute-done((bf16[128,768]{1,0:T(8,128)(2,1)S(1)}, bf16[128,768]{1,0:T(8,128)(2,1)S(1)}, u32[]{:S(2)}, u32[]{:S(2)}) %collective-permute-start.28) | collective-permute-done | bytes 196640 | tf_op jit(solution)/shard_map/normed3_x/ppermute | solution.py:353
  101.0 1.7 %shard_map.121 = (bf16[128,768]{1,0:T(8,128)(2,1)S(1)}, bf16[128,768]{1,0:T(8,128)(2,1)S(1)}, f32[1,128]{1,0:T(1,128)S(1)}, f32[1,128]{1,0:T(1,128)S(1)}) custom-call(bf16[128,768]{1,0:T(8,128)(2,1)S(1)} %get-tuple-element.72.own_ref, bf16[128,768]{1,0:T(8,128)(2,1)S(1)} %collective-permute-done.28.peer_ref, f32[128,768]{1,0:T(8,128)S(1)} %get-tuple-element.71.stream_ref, ...), custom_call_target="tpu_custom_call" | custom-call | flops 1000000000 | bytes 3000000 | tf_op jit(solution)/shard_map/pallas_call | solution.py:555
  102.7 1.6 %collective-permute-start.29 = (bf16[128,768]{1,0:T(8,128)(2,1)S(1)}, bf16[128,768]{1,0:T(8,128)(2,1)S(1)}, u32[]{:S(2)}, u32[]{:S(2)}) collective-permute-start(bf16[128,768]{1,0:T(8,128)(2,1)S(1)} %get-tuple-element.75), channel_id=1, source_target_pairs={{0,1},{1,0},{2,3},{3,2},{4,5},{5,4},{6,7},{7,6},{8,9},{9,8},{10,11... | collective-permute-start | bytes 589832 | tf_op jit(solution)/shard_map/part_x/ppermute | solution.py:353
  104.2 0.5 collective-permute-start.30
  105.4 3.1 %collective-permute-done.30.got_head_ref = f32[1,128]{1,0:T(1,128)S(1)} collective-permute-done((f32[1,128]{1,0:T(1,128)S(1)}, f32[1,128]{1,0:T(1,128)S(1)}, u32[]{:S(2)}, u32[]{:S(2)}) %collective-permute-start.30) | collective-permute-done | bytes 544 | tf_op jit(solution)/shard_map/head_x/ppermute | solution.py:353
  108.5 1.1 shard_map.122
  (63 shorter events, 0.4 us)
Async XLA Ops:
  0.6 0.9 copy-start
  1.6 12.5 %collective-permute-start = (bf16[144,384]{1,0:T(8,128)(2,1)S(1)}, bf16[144,384]{1,0:T(8,128)(2,1)S(1)}, u32[]{:S(2)}, u32[]{:S(2)}) collective-permute-start(bf16[144,384]{1,0:T(8,128)(2,1)S(1)} %dynamic-slice_bitcast_fusion.refs_0_), channel_id=1, source_target_pairs={{0,8},{2,10},{4,12},{6,14},{8,0},{10,2},{12,4},{14,6},{16,24},{18,... | collective-permute-start | bytes 331784 | tf_op jit(solution)/shard_map/cross_z1/ppermute | solution.py:349
  4.7 11.4 %collective-permute-start.1 = (bf16[144,384]{1,0:T(8,128)(2,1)S(1)}, bf16[144,384]{1,0:T(8,128)(2,1)S(1)}, u32[]{:S(2)}, u32[]{:S(2)}) collective-permute-start(bf16[144,384]{1,0:T(8,128)(2,1)S(1)} %dynamic-slice_bitcast_fusion.refs_0_), channel_id=1, source_target_pairs={{0,16},{2,18},{4,20},{6,22},{8,24},{10,26},{12,28},{14,30},{16,0},... | collective-permute-start | bytes 331784 | tf_op jit(solution)/shard_map/cross_z2/ppermute | solution.py:349
  7.3 8.8 %collective-permute-start.2 = (bf16[144,384]{1,0:T(8,128)(2,1)S(1)}, bf16[144,384]{1,0:T(8,128)(2,1)S(1)}, u32[]{:S(2)}, u32[]{:S(2)}) collective-permute-start(bf16[144,384]{1,0:T(8,128)(2,1)S(1)} %dynamic-slice_bitcast_fusion.refs_0_), channel_id=1, source_target_pairs={{0,24},{2,26},{4,28},{6,30},{8,16},{10,18},{12,20},{14,22},{16,8},... | collective-permute-start | bytes 331784 | tf_op jit(solution)/shard_map/cross_z3/ppermute | solution.py:349
  8.2 9.2 %collective-permute-start.3 = (bf16[240,384]{1,0:T(8,128)(2,1)S(1)}, bf16[240,384]{1,0:T(8,128)(2,1)S(1)}, u32[]{:S(2)}, u32[]{:S(2)}) collective-permute-start(bf16[240,384]{1,0:T(8,128)(2,1)S(1)} %fusion.1.refs_0_), channel_id=1, source_target_pairs={{0,8},{2,10},{4,12},{6,14},{8,0},{10,2},{12,4},{14,6},{16,24},{18,... | collective-permute-start | bytes 552968 | tf_op jit(solution)/shard_map/rest_z1/ppermute | solution.py:349
  11.5 0.9 copy-start.16
  12.4 0.7 copy-start.17
  14.1 4.1 %copy-start.18 = (f32[128,768]{1,0:T(8,128)}, f32[128,768]{1,0:T(8,128)S(1)}, u32[]{:S(2)}) copy-start(f32[128,768]{1,0:T(8,128)S(1)} %get-tuple-element.59.refs_2_) | copy-start | bytes 1179652
  17.4 10.8 %collective-permute-start.8 = (bf16[2,240,384]{2,1,0:T(8,128)(2,1)S(1)}, bf16[2,240,384]{2,1,0:T(8,128)(2,1)S(1)}, u32[]{:S(2)}, u32[]{:S(2)}) collective-permute-start(bf16[2,240,384]{2,1,0:T(8,128)(2,1)S(1)} %shard_map.115.refs_4_.refs_2_), channel_id=1, source_target_pairs={{8,16},{10,18},{12,20},{14,22},{16,8},{18,10},{20,12},{22,14},{9,1... | collective-permute-start | bytes 1105928 | tf_op jit(solution)/shard_map/rest_middle/ppermute | solution.py:498
  18.2 20.9 %collective-permute-start.4 = (bf16[4,144,384]{2,1,0:T(8,128)(2,1)S(1)}, bf16[4,144,384]{2,1,0:T(8,128)(2,1)S(1)}, u32[]{:S(2)}, u32[]{:S(2)}) collective-permute-start(bf16[4,144,384]{2,1,0:T(8,128)(2,1)S(1)} %shard_map.114.refs_2_), channel_id=1, source_target_pairs={{0,1},{1,0},{2,6},{3,7},{4,5},{5,4},{6,2},{7,3},{8,9},{9,8},{10,14... | collective-permute-start | bytes 1327112 | tf_op jit(solution)/shard_map/cross_1/ppermute | solution.py:476
  19.8 19.4 %collective-permute-start.5 = (bf16[4,144,384]{2,1,0:T(8,128)(2,1)S(1)}, bf16[4,144,384]{2,1,0:T(8,128)(2,1)S(1)}, u32[]{:S(2)}, u32[]{:S(2)}) collective-permute-start(bf16[4,144,384]{2,1,0:T(8,128)(2,1)S(1)} %shard_map.114.refs_2_), channel_id=1, source_target_pairs={{0,4},{1,5},{2,3},{3,2},{4,0},{5,1},{6,7},{7,6},{8,12},{9,13},{10,... | collective-permute-start | bytes 1327112 | tf_op jit(solution)/shard_map/cross_2/ppermute | solution.py:476
  21.3 17.1 %collective-permute-start.6 = (bf16[2,240,384]{2,1,0:T(8,128)(2,1)S(1)}, bf16[2,240,384]{2,1,0:T(8,128)(2,1)}, u32[]{:S(2)}, u32[]{:S(2)}) collective-permute-start(bf16[2,240,384]{2,1,0:T(8,128)(2,1)S(1)} %shard_map.115.refs_4_.refs_2_), channel_id=1, source_target_pairs={{0,1},{1,0},{2,6},{3,7},{4,5},{5,4},{6,2},{7,3},{8,9},{9,8},{10,14... | collective-permute-start | bytes 1105928 | tf_op jit(solution)/shard_map/near_1/ppermute | solution.py:476
  21.8 17.2 %collective-permute-start.7 = (bf16[2,240,384]{2,1,0:T(8,128)(2,1)S(1)}, bf16[2,240,384]{2,1,0:T(8,128)(2,1)S(1)}, u32[]{:S(2)}, u32[]{:S(2)}) collective-permute-start(bf16[2,240,384]{2,1,0:T(8,128)(2,1)S(1)} %shard_map.115.refs_4_.refs_2_), channel_id=1, source_target_pairs={{0,4},{1,5},{2,3},{3,2},{4,0},{5,1},{6,7},{7,6},{8,12},{9,13},{10,... | collective-permute-start | bytes 1105928 | tf_op jit(solution)/shard_map/near_2/ppermute | solution.py:476
  22.3 16.8 %all-to-all-start = ((bf16[16,8,768]{2,1,0:T(8,128)(2,1)}), bf16[16,8,768]{2,1,0:T(8,128)(2,1)S(1)}, u32[]{:S(2)}, u32[]{:S(2)}) async-start(bf16[16,8,768]{2,1,0:T(8,128)(2,1)} %bitcast.12), calls=%async_computation | async-start | bytes 393216 | tf_op jit(solution)/shard_map/all_to_all | solution.py:503
  28.3 14.3 %collective-permute-start.9 = (bf16[2,240,384]{2,1,0:T(8,128)(2,1)S(1)}, bf16[2,240,384]{2,1,0:T(8,128)(2,1)S(1)}, u32[]{:S(2)}, u32[]{:S(2)}) collective-permute-start(bf16[2,240,384]{2,1,0:T(8,128)(2,1)S(1)} %collective-permute-done.8.first_ref), channel_id=1, source_target_pairs={{8,0},{10,2},{12,4},{14,6},{16,24},{18,26},{20,28},{22,30},{9,1},{... | collective-permute-start | bytes 1105928 | tf_op jit(solution)/shard_map/rest_onward/ppermute | solution.py:501
  29.6 0.7 copy-start.12
  39.0 3.6 %copy-start.3 = (bf16[2,240,384]{2,1,0:T(8,128)(2,1)}, bf16[2,240,384]{2,1,0:T(8,128)(2,1)S(1)}, u32[]{:S(2)}) copy-start(bf16[2,240,384]{2,1,0:T(8,128)(2,1)S(1)} %collective-permute-done.7.refs_6_.refs_4_) | copy-start | bytes 1105924
  42.6 0.8 copy-start.14
  43.3 8.3 %collective-permute-start.10 = (bf16[4,144,384]{2,1,0:T(8,128)(2,1)S(1)}, bf16[4,144,384]{2,1,0:T(8,128)(2,1)S(1)}, u32[]{:S(2)}, u32[]{:S(2)}) collective-permute-start(bf16[4,144,384]{2,1,0:T(8,128)(2,1)S(1)} %collective-permute-done.4.refs_3_), channel_id=1, source_target_pairs={{0,4},{1,5},{2,3},{3,2},{4,0},{5,1},{6,7},{7,6},{8,12},{9,13},{10,... | collective-permute-start | bytes 1327112 | tf_op jit(solution)/shard_map/cross_3/ppermute | solution.py:476
  44.8 7.5 %collective-permute-start.12 = (bf16[4,144,384]{2,1,0:T(8,128)(2,1)S(1)}, bf16[4,144,384]{2,1,0:T(8,128)(2,1)S(1)}, u32[]{:S(2)}, u32[]{:S(2)}) collective-permute-start(bf16[4,144,384]{2,1,0:T(8,128)(2,1)S(1)} %collective-permute-done.4.refs_3_), channel_id=1, source_target_pairs={{0,2},{2,0},{4,6},{6,4},{8,10},{10,8},{12,14},{14,12},{16,18},{18,... | collective-permute-start | bytes 1327112 | tf_op jit(solution)/shard_map/cross_core/ppermute | solution.py:349
  44.8 7.4 %collective-permute-start.11 = (bf16[4,144,384]{2,1,0:T(8,128)(2,1)S(1)}, bf16[4,144,384]{2,1,0:T(8,128)(2,1)S(1)}, u32[]{:S(2)}, u32[]{:S(2)}) collective-permute-start(bf16[4,144,384]{2,1,0:T(8,128)(2,1)S(1)} %shard_map.114.refs_2_), channel_id=1, source_target_pairs={{0,2},{2,0},{4,6},{6,4},{8,10},{10,8},{12,14},{14,12},{16,18},{18,... | collective-permute-start | bytes 1327112 | tf_op jit(solution)/shard_map/cross_core/ppermute | solution.py:349
  45.3 8.5 %collective-permute-start.13 = (bf16[4,144,384]{2,1,0:T(8,128)(2,1)S(1)}, bf16[4,144,384]{2,1,0:T(8,128)(2,1)}, u32[]{:S(2)}, u32[]{:S(2)}) collective-permute-start(bf16[4,144,384]{2,1,0:T(8,128)(2,1)S(1)} %collective-permute-done.5.refs_4_), channel_id=1, source_target_pairs={{0,2},{2,0},{4,6},{6,4},{8,10},{10,8},{12,14},{14,12},{16,18},{18,... | collective-permute-start | bytes 1327112 | tf_op jit(solution)/shard_map/cross_core/ppermute | solution.py:349
  45.3 1.0 copy-start.13
  46.3 1.0 copy-start.15
  47.3 0.8 copy-start.6
  51.6 3.7 %collective-permute-start.14 = (bf16[4,144,384]{2,1,0:T(8,128)(2,1)S(1)}, bf16[4,144,384]{2,1,0:T(8,128)(2,1)}, u32[]{:S(2)}, u32[]{:S(2)}) collective-permute-start(bf16[4,144,384]{2,1,0:T(8,128)(2,1)S(1)} %collective-permute-done.10.refs_5_), channel_id=1, source_target_pairs={{0,2},{2,0},{4,6},{6,4},{8,10},{10,8},{12,14},{14,12},{16,18},{18,... | collective-permute-start | bytes 1327112 | tf_op jit(solution)/shard_map/cross_core/ppermute | solution.py:349
  51.7 13.6 %collective-permute-start.17 = (bf16[2,240,384]{2,1,0:T(8,128)(2,1)S(1)}, bf16[2,240,384]{2,1,0:T(8,128)(2,1)S(1)}, u32[]{:S(2)}, u32[]{:S(2)}) collective-permute-start(bf16[2,240,384]{2,1,0:T(8,128)(2,1)S(1)} %shard_map.115.refs_4_.refs_2_), channel_id=1, source_target_pairs={{0,2},{2,0},{4,6},{6,4},{8,10},{10,8},{12,14},{14,12},{16,18},{18,... | collective-permute-start | bytes 1105928 | tf_op jit(solution)/shard_map/near_core/ppermute | solution.py:349
  52.2 20.0 %collective-permute-start.19 = (bf16[2,240,384]{2,1,0:T(8,128)(2,1)}, bf16[2,240,384]{2,1,0:T(8,128)(2,1)}, u32[]{:S(2)}, u32[]{:S(2)}) collective-permute-start(bf16[2,240,384]{2,1,0:T(8,128)(2,1)} %copy-done.3), channel_id=1, source_target_pairs={{0,2},{2,0},{4,6},{6,4},{8,10},{10,8},{12,14},{14,12},{16,18},{18,... | collective-permute-start | bytes 1105928 | tf_op jit(solution)/shard_map/near_core/ppermute | solution.py:349
  52.3 11.2 %collective-permute-start.15 = (bf16[2,240,384]{2,1,0:T(8,128)(2,1)}, bf16[2,240,384]{2,1,0:T(8,128)(2,1)}, u32[]{:S(2)}, u32[]{:S(2)}) collective-permute-start(bf16[2,240,384]{2,1,0:T(8,128)(2,1)} %copy-done.6), channel_id=1, source_target_pairs={{0,1},{1,0},{2,6},{3,7},{4,5},{5,4},{6,2},{7,3},{8,9},{9,8},{10,14... | collective-permute-start | bytes 1105928 | tf_op jit(solution)/shard_map/far_1/ppermute | solution.py:476
  53.8 17.9 %collective-permute-start.21 = (bf16[2,240,384]{2,1,0:T(8,128)(2,1)}, bf16[2,240,384]{2,1,0:T(8,128)(2,1)}, u32[]{:S(2)}, u32[]{:S(2)}) collective-permute-start(bf16[2,240,384]{2,1,0:T(8,128)(2,1)} %copy-done.6), channel_id=1, source_target_pairs={{0,4},{1,5},{2,3},{3,2},{4,0},{5,1},{6,7},{7,6},{8,12},{9,13},{10,... | collective-permute-start | bytes 1105928 | tf_op jit(solution)/shard_map/far_2/ppermute | solution.py:476
  55.3 17.1 %collective-permute-start.23 = (bf16[2,240,384]{2,1,0:T(8,128)(2,1)}, bf16[2,240,384]{2,1,0:T(8,128)(2,1)}, u32[]{:S(2)}, u32[]{:S(2)}) collective-permute-start(bf16[2,240,384]{2,1,0:T(8,128)(2,1)} %copy-done.6), channel_id=1, source_target_pairs={{0,2},{2,0},{4,6},{6,4},{8,10},{10,8},{12,14},{14,12},{16,18},{18,... | collective-permute-start | bytes 1105928 | tf_op jit(solution)/shard_map/far_core/ppermute | solution.py:349
  63.5 9.2 %collective-permute-start.16 = (bf16[2,240,384]{2,1,0:T(8,128)(2,1)}, bf16[2,240,384]{2,1,0:T(8,128)(2,1)S(1)}, u32[]{:S(2)}, u32[]{:S(2)}) collective-permute-start(bf16[2,240,384]{2,1,0:T(8,128)(2,1)} %collective-permute-done.6.refs_5_.refs_3_), channel_id=1, source_target_pairs={{0,4},{1,5},{2,3},{3,2},{4,0},{5,1},{6,7},{7,6},{8,12},{9,13},{10,... | collective-permute-start | bytes 1105928 | tf_op jit(solution)/shard_map/near_3/ppermute | solution.py:476
  65.3 0.7 copy-start.9
  66.0 9.5 %collective-permute-start.22 = (bf16[2,240,384]{2,1,0:T(8,128)(2,1)}, bf16[2,240,384]{2,1,0:T(8,128)(2,1)S(1)}, u32[]{:S(2)}, u32[]{:S(2)}) collective-permute-start(bf16[2,240,384]{2,1,0:T(8,128)(2,1)} %collective-permute-done.15.refs_13_.refs_11_), channel_id=1, source_target_pairs={{0,4},{1,5},{2,3},{3,2},{4,0},{5,1},{6,7},{7,6},{8,12},{9,13},{10,... | collective-permute-start | bytes 1105928 | tf_op jit(solution)/shard_map/far_3/ppermute | solution.py:476
  66.3 14.5 %all-to-all-start.1 = ((bf16[16,8,768]{2,1,0:T(8,128)(2,1)}), bf16[16,8,768]{2,1,0:T(8,128)(2,1)S(1)}, u32[]{:S(2)}, u32[]{:S(2)}) async-start(bf16[16,8,768]{2,1,0:T(8,128)(2,1)} %bitcast.14), calls=%async_computation.1 | async-start | bytes 393216 | tf_op jit(solution)/shard_map/all_to_all | solution.py:529
  71.8 3.9 %collective-permute-start.25 = (bf16[2,240,384]{2,1,0:T(8,128)(2,1)}, bf16[2,240,384]{2,1,0:T(8,128)(2,1)S(1)}, u32[]{:S(2)}, u32[]{:S(2)}) collective-permute-start(bf16[2,240,384]{2,1,0:T(8,128)(2,1)} %collective-permute-done.21.refs_14_.refs_12_), channel_id=1, source_target_pairs={{0,2},{2,0},{4,6},{6,4},{8,10},{10,8},{12,14},{14,12},{16,18},{18,... | collective-permute-start | bytes 1105928 | tf_op jit(solution)/shard_map/far_core/ppermute | solution.py:349
  72.2 3.4 %collective-permute-start.18 = (bf16[2,240,384]{2,1,0:T(8,128)(2,1)}, bf16[2,240,384]{2,1,0:T(8,128)(2,1)S(1)}, u32[]{:S(2)}, u32[]{:S(2)}) collective-permute-start(bf16[2,240,384]{2,1,0:T(8,128)(2,1)} %collective-permute-done.6.refs_5_.refs_3_), channel_id=1, source_target_pairs={{0,2},{2,0},{4,6},{6,4},{8,10},{10,8},{12,14},{14,12},{16,18},{18,... | collective-permute-start | bytes 1105928 | tf_op jit(solution)/shard_map/near_core/ppermute | solution.py:349
  72.3 3.3 %collective-permute-start.24 = (bf16[2,240,384]{2,1,0:T(8,128)(2,1)}, bf16[2,240,384]{2,1,0:T(8,128)(2,1)S(1)}, u32[]{:S(2)}, u32[]{:S(2)}) collective-permute-start(bf16[2,240,384]{2,1,0:T(8,128)(2,1)} %collective-permute-done.15.refs_13_.refs_11_), channel_id=1, source_target_pairs={{0,2},{2,0},{4,6},{6,4},{8,10},{10,8},{12,14},{14,12},{16,18},{18,... | collective-permute-start | bytes 1105928 | tf_op jit(solution)/shard_map/far_core/ppermute | solution.py:349
  72.7 8.0 %collective-permute-start.20 = (bf16[2,240,384]{2,1,0:T(8,128)(2,1)S(1)}, bf16[2,240,384]{2,1,0:T(8,128)(2,1)S(1)}, u32[]{:S(2)}, u32[]{:S(2)}) collective-permute-start(bf16[2,240,384]{2,1,0:T(8,128)(2,1)S(1)} %collective-permute-done.16.refs_7_.refs_5_), channel_id=1, source_target_pairs={{0,2},{2,0},{4,6},{6,4},{8,10},{10,8},{12,14},{14,12},{16,18},{18,... | collective-permute-start | bytes 1105928 | tf_op jit(solution)/shard_map/near_core/ppermute | solution.py:349
  75.6 5.2 %collective-permute-start.26 = (bf16[2,240,384]{2,1,0:T(8,128)(2,1)S(1)}, bf16[2,240,384]{2,1,0:T(8,128)(2,1)S(1)}, u32[]{:S(2)}, u32[]{:S(2)}) collective-permute-start(bf16[2,240,384]{2,1,0:T(8,128)(2,1)S(1)} %collective-permute-done.22.refs_15_.refs_13_), channel_id=1, source_target_pairs={{0,2},{2,0},{4,6},{6,4},{8,10},{10,8},{12,14},{14,12},{16,18},{18,... | collective-permute-start | bytes 1105928 | tf_op jit(solution)/shard_map/far_core/ppermute | solution.py:349
  80.7 1.0 copy-start.4
  81.7 1.0 copy-start.7
  82.7 1.0 copy-start.10
  83.7 1.0 copy-start.19
  84.7 3.7 %copy-start.5 = (bf16[2,240,384]{2,1,0:T(8,128)(2,1)S(1)}, bf16[2,240,384]{2,1,0:T(8,128)(2,1)}, u32[]{:S(2)}) copy-start(bf16[2,240,384]{2,1,0:T(8,128)(2,1)} %copy-done.3) | copy-start | bytes 1105924
  84.7 3.7 %copy-start.8 = (bf16[2,240,384]{2,1,0:T(8,128)(2,1)S(1)}, bf16[2,240,384]{2,1,0:T(8,128)(2,1)}, u32[]{:S(2)}) copy-start(bf16[2,240,384]{2,1,0:T(8,128)(2,1)} %copy-done.6) | copy-start | bytes 1105924
  84.7 3.7 %copy-start.11 = (bf16[2,240,384]{2,1,0:T(8,128)(2,1)S(1)}, bf16[2,240,384]{2,1,0:T(8,128)(2,1)}, u32[]{:S(2)}) copy-start(bf16[2,240,384]{2,1,0:T(8,128)(2,1)} %copy-done.9) | copy-start | bytes 1105924
  86.8 6.6 %collective-permute-start.27 = (bf16[128,768]{1,0:T(8,128)(2,1)S(1)}, bf16[128,768]{1,0:T(8,128)(2,1)S(1)}, u32[]{:S(2)}, u32[]{:S(2)}) collective-permute-start(bf16[128,768]{1,0:T(8,128)(2,1)S(1)} %get-tuple-element.65.refs_1_), channel_id=1, source_target_pairs={{0,1},{1,0},{2,3},{3,2},{4,5},{5,4},{6,7},{7,6},{8,9},{9,8},{10,11... | collective-permute-start | bytes 589832 | tf_op jit(solution)/shard_map/normed2_x/ppermute | solution.py:353
  93.4 7.6 %copy-start.1 = (bf16[768,1536]{1,0:T(8,128)(2,1)S(1)}, bf16[768,1536]{1,0:T(8,128)(2,1)}, u32[]{:S(2)}) copy-start(bf16[768,1536]{1,0:T(8,128)(2,1)} %up_ref.1) | copy-start | bytes 7077892
  93.4 7.6 %copy-start.2 = (bf16[1536,768]{1,0:T(8,128)(2,1)S(1)}, bf16[1536,768]{1,0:T(8,128)(2,1)}, u32[]{:S(2)}) copy-start(bf16[1536,768]{1,0:T(8,128)(2,1)} %down_ref.1) | copy-start | bytes 7077892
  95.2 5.7 %collective-permute-start.28 = (bf16[128,768]{1,0:T(8,128)(2,1)S(1)}, bf16[128,768]{1,0:T(8,128)(2,1)S(1)}, u32[]{:S(2)}, u32[]{:S(2)}) collective-permute-start(bf16[128,768]{1,0:T(8,128)(2,1)S(1)} %get-tuple-element.72.own_ref), channel_id=1, source_target_pairs={{0,1},{1,0},{2,3},{3,2},{4,5},{5,4},{6,7},{7,6},{8,9},{9,8},{10,11... | collective-permute-start | bytes 589832 | tf_op jit(solution)/shard_map/normed3_x/ppermute | solution.py:353
  102.7 5.8 %collective-permute-start.29 = (bf16[128,768]{1,0:T(8,128)(2,1)S(1)}, bf16[128,768]{1,0:T(8,128)(2,1)S(1)}, u32[]{:S(2)}, u32[]{:S(2)}) collective-permute-start(bf16[128,768]{1,0:T(8,128)(2,1)S(1)} %get-tuple-element.75), channel_id=1, source_target_pairs={{0,1},{1,0},{2,3},{3,2},{4,5},{5,4},{6,7},{7,6},{8,9},{9,8},{10,11... | collective-permute-start | bytes 589832 | tf_op jit(solution)/shard_map/part_x/ppermute | solution.py:353
  104.2 4.2 %collective-permute-start.30 = (f32[1,128]{1,0:T(1,128)S(1)}, f32[1,128]{1,0:T(1,128)S(1)}, u32[]{:S(2)}, u32[]{:S(2)}) collective-permute-start(f32[1,128]{1,0:T(1,128)S(1)} %get-tuple-element.76.own_head_ref), channel_id=1, source_target_pairs={{0,1},{1,0},{2,3},{3,2},{4,5},{5,4},{6,7},{7,6},{8,9},{9,8},{10,11... | collective-permute-start | bytes 1544 | tf_op jit(solution)/shard_map/head_x/ppermute | solution.py:353
